TPU v7x, 128 devices: a whole 4x4x4 slice. The times are simulated.
128 devices in a mesh: chan: 8 (over x_hi, y), tmpl: 16 (over z, x_lo, core).
Axes of the slice: x: 4 (x_hi: 2, x_lo: 2; x = x_hi * 2 + x_lo), y: 4, z: 4, core: 2. Of those that a mesh axis runs over, the one named last changes fastest.
Arguments:
- samples: bfloat16 [16, 2048, 1024], P(None, 'chan', 'tmpl'), may hold values from -20 to 20
- template_spectra: bfloat16 [2, 256, 2048, 512], P(None, 'tmpl', 'chan'), may hold values from -6 to 6
- lag_lengths: int32 [256], P('tmpl'), may hold values from 64 to 512
- offsets: int32 [16], replicated, may hold values from 0 to 1023
Outputs:
- stacked: float32 [256, 1024], P('tmpl', 'chan')
All inputs are finite; a program needn't handle non-finite values.
Results may differ from a plain program's by a relative error of at most 0.009.
Values may be sent and summed in bfloat16 or wider, within the bound.
No kernel may reach another device: no remote copies, remote signals or barrier semaphores. Data moves between devices by JAX's collectives and lax.ppermute only.
A program may use at most 128 MiB of HBM per device.

v0:
```python
import math

import jax
import jax.numpy as jnp
from jax import lax
from jax.sharding import PartitionSpec as P

epsilon = 1e-06
highest = lax.Precision.HIGHEST


def twiddles(length, bin_count):
    sample_index = lax.iota(jnp.int32, length)
    bin_index = lax.iota(jnp.int32, bin_count)
    phase = sample_index[:, None] * bin_index[None, :] % length
    angle = phase.astype(jnp.float32) * (2.0 * math.pi / length)
    return (jnp.cos(angle), jnp.sin(angle))


def inverse_table(bin_count):
    length = 2 * bin_count
    cosine, sine = twiddles(length, bin_count)
    return jnp.concatenate([cosine.T, -sine.T], axis=0) * (2.0 / length)


def transform(record):
    leading = record.shape[:2]
    length = record.shape[2]
    cosine, sine = twiddles(length, length // 2)
    forward_table = jnp.concatenate([cosine, -sine], axis=1)
    high_part = forward_table.astype(jnp.bfloat16)
    low_part = (forward_table - high_part.astype(jnp.float32)).astype(jnp.bfloat16)
    flattened = record.reshape(-1, length)
    result = jnp.dot(flattened, high_part, preferred_element_type=jnp.float32)
    result = result + jnp.dot(flattened, low_part, preferred_element_type=jnp.float32)
    return result.astype(jnp.bfloat16).reshape(leading + (length,))


def cross_terms(form, spectra, real_tmpl, imag_tmpl):
    bin_count = real_tmpl.shape[2]
    data_real = spectra[:, :, :bin_count]
    data_imag = spectra[:, :, bin_count:]

    def product(left, right):
        return jnp.einsum(form, left, right, preferred_element_type=jnp.float32)

    real_part = product(real_tmpl, data_real) + product(imag_tmpl, data_imag)
    imag_part = product(real_tmpl, data_imag) - product(imag_tmpl, data_real)
    return jnp.concatenate([real_part, imag_part], axis=2)


def offset_phases(offsets, bin_count):
    length = 2 * bin_count
    bin_index = lax.iota(jnp.int32, bin_count)
    phase = offsets[:, None] * bin_index[None, :] % length
    angle = phase.astype(jnp.float32) * (2.0 * math.pi / length)
    return (jnp.cos(angle), jnp.sin(angle))


def delay_cross(cross, cosine, sine):
    bin_count = cosine.shape[-1]
    real_part = cross[..., :bin_count]
    imag_part = cross[..., bin_count:]
    return jnp.concatenate(
        [real_part * cosine + imag_part * sine, imag_part * cosine - real_part * sine], axis=-1
    )


def delay_energy(energy, offsets):

    def delay_single(row, shift_by):
        return jnp.roll(row, shift_by)

    return jax.vmap(delay_single)(energy, offsets)


def window_powers(energy, lag_lengths, channel_total):
    length = energy.shape[1]
    doubled = jnp.concatenate([energy, energy], axis=1)
    prefix = jnp.concatenate(
        [jnp.zeros((energy.shape[0], 1), jnp.float32), jnp.cumsum(doubled, axis=1)], axis=1
    )

    def window_single(window):
        ahead = lax.dynamic_slice_in_dim(prefix, window, length, 1)
        return (ahead - prefix[:, :length]) / (channel_total * window.astype(jnp.float32))

    return jax.vmap(window_single)(lag_lengths)


def body(samples, template_spectra, lag_lengths, offsets):
    segment_total = samples.shape[0]
    chan_groups = lax.axis_size("chan")
    channel_total = samples.shape[1] * chan_groups
    real_tmpl = template_spectra[0]
    imag_tmpl = template_spectra[1]
    bin_count = real_tmpl.shape[2]
    length = 2 * bin_count
    wide = samples.astype(jnp.float32)
    energy_part = jnp.sum(wide * wide, axis=1)
    real_wide = real_tmpl.astype(jnp.float32)
    imag_wide = imag_tmpl.astype(jnp.float32)
    tmpl_part = jnp.sum(real_wide * real_wide + imag_wide * imag_wide, axis=(1, 2)) * (2.0 / length)
    energy_chan, tmpl_energy = lax.psum((energy_part, tmpl_part), "chan")
    energy = lax.all_gather(energy_chan, "tmpl", axis=1, tiled=True)
    record = lax.all_gather(samples, "tmpl", axis=2, tiled=True)
    spectra = transform(record)
    powers = window_powers(delay_energy(energy, offsets), lag_lengths, channel_total)
    backward = inverse_table(bin_count)
    cosine, sine = offset_phases(offsets, bin_count)
    scale = 1.0 / math.sqrt(segment_total)
    row_count = segment_total // chan_groups
    summed = lax.psum_scatter(
        cross_terms("tcf,scf->stf", spectra, real_tmpl, imag_tmpl),
        "chan",
        scatter_dimension=0,
        tiled=True,
    )
    first_row = lax.axis_index("chan") * row_count
    local_cos = lax.dynamic_slice_in_dim(cosine, first_row, row_count, 0)
    local_sin = lax.dynamic_slice_in_dim(sine, first_row, row_count, 0)
    delayed = delay_cross(summed, local_cos[:, None, :], local_sin[:, None, :])
    correlation = jnp.einsum("stf,fk->tsk", delayed, backward, precision=highest)
    local_power = lax.dynamic_slice_in_dim(powers, first_row, row_count, 1)
    scores = correlation / jnp.sqrt(tmpl_energy[:, None, None] * local_power + epsilon)
    partial_stack = jnp.sum(scores, axis=1) * scale
    stacked = lax.psum_scatter(partial_stack, "chan", scatter_dimension=1, tiled=True)
    return stacked


def solution(mesh):
    return jax.shard_map(
        body,
        mesh=mesh,
        in_specs=(P(None, "chan", "tmpl"), P(None, "tmpl", "chan", None), P("tmpl"), P()),
        out_specs=P("tmpl", "chan"),
        check_vma=False,
    )
```

profile of v0, /device:TPU:0, one launch (start us, length us, event | category | flops | bytes accessed | tf_op | source)
XLA Modules:
  0.0 370.1 jit_solution(5564108378099970865)
XLA Ops:
  6.5 2.1 copy.21
  8.8 5.8 %fusion.65 = (bf16[1,16,256,512]{3,2,1,0:T(8,128)(2,1)}, bf16[1,16,256,512]{3,2,1,0:T(8,128)(2,1)}) fusion(bf16[2,16,256,512]{3,2,1,0:T(8,128)(2,1)} %param.5), kind=kLoop, calls=%fused_computation.97 | loop fusion | bytes 16777216 | tf_op jit(solution)/shard_map/slice | solution.py:95
  14.6 8.1 %copy.32 = bf16[1,16,256,512]{2,1,3,0:T(8,128)(2,1)} copy(bf16[1,16,256,512]{3,2,1,0:T(8,128)(2,1)} %get-tuple-element.42) | data formatting | bytes 8388608
  22.7 8.0 %copy.31 = bf16[1,16,256,512]{2,1,3,0:T(8,128)(2,1)} copy(bf16[1,16,256,512]{3,2,1,0:T(8,128)(2,1)} %get-tuple-element.41) | data formatting | bytes 8388608
  31.0 5.5 %add_reduce_fusion = f32[16]{0:T(128)S(1)} fusion(bf16[1,16,256,512]{2,1,3,0:T(8,128)(2,1)} %copy.32, bf16[1,16,256,512]{2,1,3,0:T(8,128)(2,1)} %copy.31), kind=kLoop, calls=%fused_computation.4 | loop fusion | flops 12582896 | bytes 8388672 | tf_op jit(solution)/shard_map/reduce_sum | solution.py:103
  36.5 26.5 %all-reduce.2 = (f32[16,64]{1,0:T(8,128)S(1)}, f32[16]{0:T(128)}) all-reduce(f32[16,64]{1,0:T(8,128)S(1)} %multiply_reduce_fusion, f32[16]{0:T(128)S(1)} %broadcast_multiply_fusion.1), channel_id=1, replica_groups=mesh['chan'=8,'tmpl'=16] {'chan'}, use_global_device_ids=true, to_apply=%region_4.5 | all-reduce | flops 1040 | bytes 8320 | tf_op jit(solution)/shard_map/psum | solution.py:104
  63.0 20.8 %all-gather = f32[16,64,16]{1,2,0:T(8,128)S(1)} all-gather(f32[1,64,16]{1,2,0:T(8,128)S(1)} %bitcast.91), channel_id=1, replica_groups=mesh['chan'=8,'tmpl'=16] {'tmpl'}, dimensions={0}, use_global_device_ids=true | all-gather | bytes 69632 | tf_op jit(solution)/shard_map/all_gather | solution.py:105
  84.0 33.1 %while.2 = (s32[]{:T(128)}, f32[16,2048]{1,0:T(8,128)S(1)}, s32[16,2]{0,1:T(2,128)S(1)}, f32[16,1024]{1,0:T(8,128)S(1)}, s32[]{:T(128)}, /*index=5*/s32[]{:T(128)}) while((s32[]{:T(128)}, f32[16,2048]{1,0:T(8,128)S(1)}, s32[16,2]{0,1:T(2,128)S(1)}, f32[16,1024]{1,0:T(8,128)S(1)}, s32[]{:T(128)}, /*index=5*/s32[]{:T(128)}) %tuple.36), condition=%wide.while_cond, body=%wide.while_body.sunk | while | flops 2 | bytes 16497 | solution.py:72
  117.1 4.5 %reduce-window.6 = f32[16,16,128]{2,1,0:T(8,128)S(1)} reduce-window(f32[16,16,128]{2,1,0:T(8,128)S(1)} %bitcast.88, f32[]{:T(128)} %constant.76.clone.1), window={size=1x1x128 pad=0_0x0_0x127_0}, to_apply=%region_5.6 | reduce-window | flops 4161536 | bytes 262148 | tf_op jit(solution)/shard_map/reduce-window
  125.5 9.1 %sine_negate_fusion = (f32[1024,512]{1,0:T(8,128)S(1)}, f32[1024,512]{1,0:T(8,128)}) fusion(), kind=kLoop, calls=%fused_computation.36 | loop fusion | flops 7864320 | bytes 4194304 | tf_op jit(solution)/shard_map/neg | solution.py:30
  134.6 9.2 %sine_negate_fusion.1 = (f32[512,1024]{1,0:T(8,128)}, f32[512,1024]{1,0:T(8,128)}) fusion(), kind=kLoop, calls=%fused_computation.40 | loop fusion | flops 7864320 | bytes 4194304 | tf_op jit(solution)/shard_map/neg | solution.py:23
  143.8 12.3 %copy.22 = bf16[16,256,1024]{2,1,0:T(8,128)(2,1)} copy(bf16[16,256,1024]{1,0,2:T(8,128)(2,1)} %all-gather.3.cloned.1.call-done) | data formatting | bytes 16777216 | tf_op jit(solution)/shard_map/all_gather | solution.py:106
  156.1 15.3 %fusion.14 = f32[1024,4096]{1,0:T(8,128)} fusion(bf16[4096,1024]{1,0:T(8,128)(2,1)} %bitcast.82, f32[1024,512]{1,0:T(8,128)S(1)} %get-tuple-element.49, f32[1024,512]{1,0:T(8,128)} %get-tuple-element.50), kind=kOutput, calls=%fused_computation.29 | convolution fusion | flops 8594128896 | bytes 29360128 | tf_op jit(solution)/shard_map/dot_general | solution.py:34
  171.3 16.5 %add_convert_fusion = bf16[1024,4096]{1,0:T(8,128)(2,1)} fusion(f32[1024,4096]{1,0:T(8,128)} %fusion.14, bf16[4096,1024]{1,0:T(8,128)(2,1)} %bitcast.83, f32[1024,512]{1,0:T(8,128)S(1)} %get-tuple-element.49, f32[1024,512]{1,0:T(8,128)} %get-tuple-element.50), kind=kOutput, calls=%fused_computation.3 | convolution fusion | flops 8603566080 | bytes 37748736 | tf_op jit(solution)/shard_map/dot_general | solution.py:35
  187.8 9.9 %copy.41 = bf16[128,8,16,256]{3,2,1,0:T(8,128)(2,1)} copy(bf16[128,8,16,256]{3,1,2,0:T(8,128)(2,1)} %bitcast.84) | data formatting | bytes 16777216
  197.7 5.4 %fusion.7 = f32[512,16,16]{2,1,0:T(8,128)} fusion(bf16[16,256,1024]{1,0,2:T(8,128)(2,1)} %bitcast.78, bf16[1,16,256,512]{2,1,3,0:T(8,128)(2,1)S(1)} %copy-done.1), kind=kOutput, calls=%fused_computation.13 | convolution fusion | flops 67108864 | bytes 13107200 | tf_op jit(solution)/shard_map/tcf,scf->stf/dot_general | solution.py:45
  203.0 5.5 %fusion.5 = f32[512,16,16]{2,1,0:T(8,128)} fusion(bf16[16,256,1024]{1,0,2:T(8,128)(2,1)} %bitcast.79, bf16[1,16,256,512]{2,1,3,0:T(8,128)(2,1)S(1)} %copy-done.1), kind=kOutput, calls=%fused_computation.11 | convolution fusion | flops 67108864 | bytes 13107200 | tf_op jit(solution)/shard_map/tcf,scf->stf/dot_general | solution.py:45
  208.6 5.6 %add_bitcast_fusion = f32[16,16,512]{1,0,2:T(8,128)} fusion(f32[512,16,16]{2,1,0:T(8,128)S(1)} %copy-done.2, bf16[16,256,1024]{1,0,2:T(8,128)(2,1)} %bitcast.80, bf16[1,16,256,512]{2,1,3,0:T(8,128)(2,1)S(1)} %copy-done), kind=kOutput, calls=%fused_computation.20 | convolution fusion | flops 67239936 | bytes 13631488 | tf_op jit(solution)/shard_map/tcf,scf->stf/dot_general | solution.py:45
  214.1 3.5 copy.25
  217.7 7.8 %subtract_bitcast_fusion = f32[16,16,512]{1,0,2:T(8,128)} fusion(f32[512,16,16]{2,1,0:T(8,128)} %fusion.5, bf16[16,256,1024]{1,0,2:T(8,128)(2,1)} %bitcast.81, bf16[1,16,256,512]{2,1,3,0:T(8,128)(2,1)} %copy.31), kind=kOutput, calls=%fused_computation.19 | convolution fusion | flops 67239936 | bytes 13631488 | tf_op jit(solution)/shard_map/tcf,scf->stf/dot_general | solution.py:45
  225.6 2.9 copy.26
  229.6 68.9 %while.3 = (s32[]{:T(128)}, f32[16,2049]{1,0:T(8,128)}, s32[16,2]{0,1:T(2,128)S(1)}, f32[16,16,1024]{2,0,1:T(8,128)}, s32[]{:T(128)}, /*index=5*/s32[]{:T(128)}) while((s32[]{:T(128)}, f32[16,2049]{1,0:T(8,128)}, s32[16,2]{0,1:T(2,128)S(1)}, f32[16,16,1024]{2,0,1:T(8,128)}, s32[]{:T(128)}, /*index=5*/s32[]{:T(128)}) %tuple.48), condition=%wide.while_cond.1, body=%wide.while_body.1.sunk | while | flops 2 | bytes 393321 | solution.py:85
  299.5 4.2 %fusion.39 = f32[16,1024]{1,0:T(8,128)S(1)} fusion(f32[512,1024]{1,0:T(8,128)S(1)} %copy-done.3, f32[512,1024]{1,0:T(8,128)} %get-tuple-element.52, f32[16,16,1024]{2,0,1:T(8,128)} %get-tuple-element.20, s32[]{:T(128)S(6)} %select_n.47, f32[2,16,512]{2,1,0:T(8,128)S(1)} %get-tuple-element.44, f32[2,16,512]{2,1,0:T(8,128)S(1)} %get-tuple-element.43, ...), kind=kOutput, calls=%fused_computation.47 | convolution fusion | flops 404963328 | bytes 4530308 | tf_op jit(solution)/shard_map/stf,fk->tsk/dot_general | solution.py:123
  304.4 59.1 %reduce-scatter.5.cloned.1.call-done = f32[16,128]{1,0:T(8,128)} async-done(((f32[16,1024]{1,0:T(8,128)}), f32[16,128]{1,0:T(8,128)}) %reduce-scatter.5.cloned.1.call-update) | async-done | bytes 8208 | tf_op jit(solution)/shard_map/reduce_scatter | solution.py:127
  (206 shorter events, 108.5 us)
Async XLA Ops:
  6.5 137.3 %all-gather.3.cloned.1.call-start = ((), (), s32[]{:S(2)}) async-start(), calls=%async_computation.2 | async-start | bytes 8912896 | tf_op jit(solution)/shard_map/all_gather | solution.py:106
  8.7 289.9 %reduce-scatter.3.cloned.1.call-start = ((), (), s32[]{:S(2)}) async-start(), calls=%async_computation.3 | async-start | bytes 1179648 | tf_op jit(solution)/shard_map/reduce_scatter | solution.py:113
  22.7 8.1 %copy-start.4 = (bf16[16,256,64]{1,2,0:T(8,128)(2,1)S(1)}, bf16[16,256,64]{1,2,0:T(8,128)(2,1)}, u32[]{:S(2)}) copy-start(bf16[16,256,64]{1,2,0:T(8,128)(2,1)} %param.4) | copy-start | bytes 1572868
  31.0 52.9 %copy-start.10 = (s32[16]{0:T(128)S(1)}, s32[16]{0:T(128)}, u32[]{:S(2)}) copy-start(s32[16]{0:T(128)} %param.7) | copy-start | bytes 196
  31.0 52.9 %copy-start.11 = (s32[16]{0:T(128)S(1)}, s32[16]{0:T(128)}, u32[]{:S(2)}) copy-start(s32[16]{0:T(128)} %param.6) | copy-start | bytes 196
  187.8 9.9 %copy-start.1 = (bf16[1,16,256,512]{2,1,3,0:T(8,128)(2,1)S(1)}, bf16[1,16,256,512]{2,1,3,0:T(8,128)(2,1)}, u32[]{:S(2)}) copy-start(bf16[1,16,256,512]{2,1,3,0:T(8,128)(2,1)} %copy.32) | copy-start | bytes 12582916
  203.0 5.5 %copy-start = (bf16[1,16,256,512]{2,1,3,0:T(8,128)(2,1)S(1)}, bf16[1,16,256,512]{2,1,3,0:T(8,128)(2,1)}, u32[]{:S(2)}) copy-start(bf16[1,16,256,512]{2,1,3,0:T(8,128)(2,1)} %copy.31) | copy-start | bytes 12582916
  203.0 5.5 %copy-start.2 = (f32[512,16,16]{2,1,0:T(8,128)S(1)}, f32[512,16,16]{2,1,0:T(8,128)}, u32[]{:S(2)}) copy-start(f32[512,16,16]{2,1,0:T(8,128)} %fusion.7) | copy-start | bytes 1572868
  225.5 3.0 copy-start.5
  225.5 4.1 %copy-start.6 = (s32[16,2]{0,1:T(2,128)S(1)}, s32[16,2]{0,1:T(2,128)}, u32[]{:S(2)}) copy-start(s32[16,2]{0,1:T(2,128)} %concatenate.32) | copy-start | bytes 388
  225.5 73.1 %copy-start.7 = (f32[2,512]{1,0:T(2,128)S(1)}, f32[2,512]{1,0:T(2,128)}, u32[]{:S(2)}) copy-start(f32[2,512]{1,0:T(2,128)} %get-tuple-element.45) | copy-start | bytes 12292
  225.5 73.1 %copy-start.8 = (f32[2,512]{1,0:T(2,128)S(1)}, f32[2,512]{1,0:T(2,128)}, u32[]{:S(2)}) copy-start(f32[2,512]{1,0:T(2,128)} %get-tuple-element.46) | copy-start | bytes 12292
  225.5 74.0 %copy-start.3 = (f32[512,1024]{1,0:T(8,128)S(1)}, f32[512,1024]{1,0:T(8,128)}, u32[]{:S(2)}) copy-start(f32[512,1024]{1,0:T(8,128)} %get-tuple-element.51) | copy-start | bytes 6291460
  225.5 74.0 %copy-start.9 = (f32[2,1024]{1,0:T(2,128)S(1)}, f32[2,1024]{1,0:T(2,128)}, u32[]{:S(2)}) copy-start(f32[2,1024]{1,0:T(2,128)} %constant_dynamic-slice_fusion.2) | copy-start | bytes 24580
  225.5 74.0 %copy-start.12 = (f32[16]{0:T(128)S(1)}, f32[16]{0:T(128)}, u32[]{:S(2)}) copy-start(f32[16]{0:T(128)} %get-tuple-element.38) | copy-start | bytes 196
  225.5 74.0 %copy-start.13 = (f32[16]{0:T(128)S(1)}, f32[16]{0:T(128)}, u32[]{:S(2)}) copy-start(f32[16]{0:T(128)} %convert_multiply_fusion) | copy-start | bytes 196
  229.6 134.0 %reduce-scatter.5.cloned.1.call-start = ((), (), s32[]{:S(2)}) async-start(), calls=%async_computation.4 | async-start | bytes 73728 | tf_op jit(solution)/shard_map/reduce_scatter | solution.py:127
Sparse Core Ops, SparseCore 0:
  9.1 55.2 all-gather.2
  229.7 66.7 reduce-scatter.2
  304.5 58.9 reduce-scatter.4
where the time goes:
time: 372 us; the launch traced here: 370 us
  local copies, waits for them, and re-layouts  157 us (42%)
  matrix products  60.3 us (16%)
  waiting for transfers between devices  59.2 us (16%)
  blocking collectives  47.2 us (13%)
  other arithmetic  32 us (9%)
  between operations  13.4 us (4%)
    gather x144, local copies, waits for them, and re-layouts  101 us
    reduce_scatter x1, waiting for transfers between devices, body(): lax.psum_scatter(partial_stack, 'chan', scatter_dimension=1, tiled=True)  59.1 us
    unnamed x36, local copies, waits for them, and re-layouts  28.4 us
    psum x1, blocking collectives, body(): energy_chan, tmpl_energy = lax.psum((energy_part, tmpl_part), 'chan')  26.5 us
    dot_general x4, matrix products, product(): return jnp.einsum(form, left, right, preferred_element_type=jnp.float32)  24.3 us
    all_gather x1, blocking collectives, body(): energy = lax.all_gather(energy_chan, 'tmpl', axis=1, tiled=True)  20.8 us
    dot_general x1, matrix products, transform(): jnp.dot(flattened, low_part, preferred_element_type=jnp.float32)  16.5 us
    dot_general x1, matrix products, transform(): result = jnp.dot(flattened, high_part, preferred_element_type=jnp.float32)  15.3 us
  transfers between devices with their start and end apart: 3, of which 1 were waited for; matrix products, arithmetic and copies ran while one was open for 42% of the time, Pallas kernels for 0%

commit v1 on v0

v1 whole, which is shorter than its diff:
```python
import math

import jax
import jax.numpy as jnp
import numpy as np
from jax import lax
from jax.experimental import pallas as pl
from jax.experimental.pallas import tpu as pltpu
from jax.sharding import PartitionSpec as P

epsilon = 1e-06
LANES = 128
BLOCK = 16
F32 = jnp.float32
BF16 = jnp.bfloat16


def tables(length):
    bins = length // 2
    angle = 2.0 * np.pi * (np.outer(np.arange(bins), np.arange(length)) % length) / length
    forward = np.concatenate([np.cos(angle), -np.sin(angle)], axis=0)
    backward = forward * (2.0 / length)
    backward_high = backward.astype(BF16)
    backward_low = (backward - backward_high.astype(np.float64)).astype(BF16)
    return forward.astype(BF16), backward_high, backward_low


def selection(segments, templates):
    rows = np.arange(segments * templates * BLOCK) // BLOCK
    return (rows[:, None] == np.arange(segments * templates)[None, :]).astype(BF16)


def template_kernel(g_ref, out_ref, energy_ref):
    t = pl.program_id(0)
    channels, bins = g_ref.shape[2:]
    total = jnp.zeros((1, bins), F32)
    for part in range(2):
        wide = g_ref[part, 0].astype(F32)
        total = total + jnp.sum(wide * wide, axis=0, keepdims=True)
        flipped = wide.T.astype(BF16)
        out_ref[:, 0, :, part * channels : (part + 1) * channels] = flipped.reshape(
            bins // BLOCK, BLOCK, channels
        )
    folded = total[:, :LANES]
    for j in range(1, bins // LANES):
        folded = folded + total[:, j * LANES : (j + 1) * LANES]
    energy_ref[pl.ds(t, 1), :] = folded


def prepare_templates(template_spectra):
    _, templates, channels, bins = template_spectra.shape
    return pl.pallas_call(
        template_kernel,
        grid=(templates,),
        in_specs=[pl.BlockSpec((2, 1, channels, bins), lambda t: (0, t, 0, 0))],
        out_specs=[
            pl.BlockSpec((bins // BLOCK, 1, BLOCK, 2 * channels), lambda t: (0, t, 0, 0)),
            pl.BlockSpec((templates, LANES), lambda t: (0, 0)),
        ],
        out_shape=[
            jax.ShapeDtypeStruct((bins // BLOCK, templates, BLOCK, 2 * channels), BF16),
            jax.ShapeDtypeStruct((templates, LANES), F32),
        ],
        compiler_params=pltpu.CompilerParams(vmem_limit_bytes=24 << 20),
        cost_estimate=pl.CostEstimate(flops=20_000_000, bytes_accessed=16 << 20, transcendentals=0),
        name="template_flip",
    )(template_spectra)


def weight_kernel(channel_total, scale, lag_ref, offset_ref, level_ref, energy_ref, out_ref, prefix):
    segments, length = energy_ref.shape
    templates = out_ref.shape[1]
    row = lax.broadcasted_iota(jnp.int32, (segments, length), 0)
    energy = energy_ref[...]
    delayed = jnp.zeros((segments, length), F32)
    for s in range(segments):
        delayed = jnp.where(row == s, pltpu.roll(energy, offset_ref[s], axis=1), delayed)
    before = lax.broadcasted_iota(jnp.int32, (LANES, LANES), 0) < lax.broadcasted_iota(
        jnp.int32, (LANES, LANES), 1
    )
    before = before.astype(F32)
    carry = jnp.zeros((segments, 1), F32)
    blocks = length // LANES
    for j in range(blocks):
        piece = delayed[:, j * LANES : (j + 1) * LANES]
        prefix[:, j * LANES : (j + 1) * LANES] = carry + jnp.dot(
            piece, before, precision=lax.Precision.HIGHEST, preferred_element_type=F32
        )
        carry = carry + jnp.sum(piece, axis=1, keepdims=True)
    first = prefix[:, :length]
    prefix[:, length : 2 * length] = first + carry
    prefix[:, 2 * length :] = first[:, :LANES] + 2.0 * carry
    span = length + LANES
    for t in range(templates):
        lag = lag_ref[t]
        start = pl.multiple_of((lag // LANES) * LANES, LANES)
        ahead = pltpu.roll(prefix[:, pl.ds(start, span)], span - lag % LANES, axis=1)[:, :length]
        power = (ahead - first) / (channel_total * lag.astype(F32))
        out_ref[:, t, :] = scale * lax.rsqrt(level_ref[t] * power + epsilon)


def score_weights(lag_lengths, offsets, level, energy, channel_total):
    segments, length = energy.shape
    templates = lag_lengths.shape[0]
    smem = pl.BlockSpec(memory_space=pltpu.SMEM)
    vmem = pl.BlockSpec(memory_space=pltpu.VMEM)

    def kernel(*refs):
        weight_kernel(channel_total, 1.0 / math.sqrt(segments), *refs)

    return pl.pallas_call(
        kernel,
        in_specs=[smem, smem, smem, vmem],
        out_specs=vmem,
        out_shape=jax.ShapeDtypeStruct((segments, templates, length), F32),
        scratch_shapes=[pltpu.VMEM((segments, 2 * length + LANES), F32)],
        compiler_params=pltpu.CompilerParams(vmem_limit_bytes=16 << 20),
        cost_estimate=pl.CostEstimate(flops=20_000_000, bytes_accessed=2 << 20, transcendentals=262144),
        name="score_weights",
    )(lag_lengths, offsets, level, energy)


def detect_kernel(
    x_ref, weight_ref, cos_ref, sin_ref, forward_ref, select_ref, tmpl_hbm, high_hbm, low_hbm,
    out_ref, tmpl, high, low, spectra, masked, sems,
):
    half = pl.program_id(0)
    blocks, segments, piece, channels = x_ref.shape
    length = blocks * piece
    bins = length // 2
    templates = weight_ref.shape[1]
    lanes = templates * BLOCK
    copies = [
        pltpu.make_async_copy(tmpl_hbm, tmpl, sems.at[0]),
        pltpu.make_async_copy(high_hbm, high, sems.at[1]),
        pltpu.make_async_copy(low_hbm, low, sems.at[2]),
    ]

    @pl.when(half == 0)
    def _():
        for copy in copies:
            copy.start()

    @pl.loop(0, segments)
    def _(s):
        record = x_ref[:, pl.ds(s, 1)].reshape(length, channels)
        result = jnp.dot(forward_ref[...], record, preferred_element_type=F32)
        real = result[:bins].astype(BF16)
        imag = result[bins:].astype(BF16)
        spectra[0, s, :, :channels] = real
        spectra[0, s, :, channels:] = imag
        spectra[1, s, :, :channels] = imag
        spectra[1, s, :, channels:] = -real

    @pl.when(half == 0)
    def _():
        for copy in copies:
            copy.wait()

    rows = 2 * segments * BLOCK
    keep = (
        lax.broadcasted_iota(jnp.int32, (rows, lanes), 0) % BLOCK
        == lax.broadcasted_iota(jnp.int32, (rows, lanes), 1) % BLOCK
    )

    @pl.loop(0, bins // BLOCK)
    def _(b):
        start = pl.multiple_of(b * BLOCK, BLOCK)
        left = spectra[:, :, pl.ds(start, BLOCK), :].reshape(rows, 2 * channels)
        right = tmpl[b].reshape(lanes, 2 * channels)
        product = lax.dot_general(left, right, (((1,), (1,)), ((), ())), preferred_element_type=F32)
        product = jnp.where(keep, product, 0.0).astype(BF16)
        for part in range(2):
            for s in range(segments):
                first = (part * segments + s) * BLOCK
                masked[pl.ds(part * bins + start, BLOCK), s * lanes : (s + 1) * lanes] = product[
                    first : first + BLOCK
                ]

    cross = jnp.dot(masked[...], select_ref[...], preferred_element_type=F32)
    real, imag = cross[:bins], cross[bins:]
    cosine, sine = cos_ref[...], sin_ref[...]
    delayed = jnp.concatenate([real * cosine + imag * sine, imag * cosine - real * sine], axis=0)
    delayed_high = delayed.astype(BF16)
    delayed_low = (delayed - delayed_high.astype(F32)).astype(BF16)

    def back(left, right):
        return lax.dot_general(left, right, (((0,), (0,)), ((), ())), preferred_element_type=F32)

    correlation = back(delayed_high, high[...]) + back(delayed_low, high[...])
    correlation = correlation + back(delayed_high, low[...])
    scores = correlation.reshape(segments, templates, length) * weight_ref[...]
    stack = jnp.sum(scores, axis=0)

    @pl.when(half == 0)
    def _():
        for j in range(length // LANES):
            out_ref[j] = stack[:, j * LANES : (j + 1) * LANES]

    @pl.when(half != 0)
    def _():
        for j in range(length // LANES):
            out_ref[j] += stack[:, j * LANES : (j + 1) * LANES]


def detect(record, weights, cosine, sine, forward, high, low, tmpl, halves):
    pieces, segments, piece, channels = record.shape
    length = pieces * piece
    templates = weights.shape[1]
    step = segments // halves
    select = selection(step, templates)
    once = pl.Buffered(1)
    anywhere = pl.BlockSpec(memory_space=pl.ANY)

    def fixed(array):
        return pl.BlockSpec(array.shape, lambda h: (0,) * array.ndim, pipeline_mode=once)

    return pl.pallas_call(
        detect_kernel,
        grid=(halves,),
        in_specs=[
            pl.BlockSpec((pieces, step, piece, channels), lambda h: (0, h, 0, 0)),
            pl.BlockSpec((step, templates, length), lambda h: (h, 0, 0)),
            pl.BlockSpec((length // 2, step * templates), lambda h: (0, h)),
            pl.BlockSpec((length // 2, step * templates), lambda h: (0, h)),
            fixed(forward),
            fixed(select),
            anywhere,
            anywhere,
            anywhere,
        ],
        out_specs=pl.BlockSpec((length // LANES, templates, LANES), lambda h: (0, 0, 0)),
        out_shape=jax.ShapeDtypeStruct((length // LANES, templates, LANES), F32),
        scratch_shapes=[
            pltpu.VMEM(tmpl.shape, BF16),
            pltpu.VMEM(high.shape, BF16),
            pltpu.VMEM(low.shape, BF16),
            pltpu.VMEM((2, step, length // 2, 2 * channels), BF16),
            pltpu.VMEM((length, step * templates * BLOCK), BF16),
            pltpu.SemaphoreType.DMA((3,)),
        ],
        compiler_params=pltpu.CompilerParams(vmem_limit_bytes=56 << 20),
        cost_estimate=pl.CostEstimate(flops=30_000_000_000, bytes_accessed=32 << 20, transcendentals=0),
        name="detect",
    )(record, weights, cosine, sine, forward, select, tmpl, high, low)


def swap(value, axis, partner):
    return lax.ppermute(value, axis, [(i, partner(i)) for i in range(lax.axis_size(axis))])


def body(samples, template_spectra, lag_lengths, offsets):
    segments, channels, piece = samples.shape
    chan_groups = lax.axis_size("chan")
    tmpl_groups = lax.axis_size("tmpl")
    channel_total = channels * chan_groups
    length = piece * tmpl_groups
    bins = length // 2
    templates = template_spectra.shape[1]

    record = lax.all_gather(jnp.transpose(samples, (0, 2, 1)), "tmpl", axis=0, tiled=False)

    wide = samples.astype(F32)
    energy = jnp.sum(wide * wide, axis=1)
    tmpl, level = prepare_templates(template_spectra)
    level = jnp.sum(level, axis=1) * (2.0 / length)

    sums = jnp.concatenate([energy, level.reshape(segments, -1)], axis=1)
    for bit in (1, 2, 4):
        sums = sums + swap(sums, "chan", lambda i: i ^ bit)
    energy = sums[:, :piece]
    level = sums[:, piece:].reshape(templates)
    me = lax.axis_index("tmpl")
    for bit in (1, 2, 4, 8):
        other = swap(energy, "tmpl", lambda i: i ^ bit)
        upper = (me & bit) != 0
        energy = jnp.concatenate(
            [jnp.where(upper, other, energy), jnp.where(upper, energy, other)], axis=1
        )
    weights = score_weights(lag_lengths, offsets, level, energy, channel_total)

    phase = offsets[None, :] * lax.iota(jnp.int32, bins)[:, None] % length
    angle = phase.astype(F32) * (2.0 * math.pi / length)
    cosine = jnp.repeat(jnp.cos(angle), templates, axis=1)
    sine = jnp.repeat(jnp.sin(angle), templates, axis=1)
    forward, high, low = tables(length)
    partial = detect(record, weights, cosine, sine, forward, high, low, tmpl, 2)
    return jnp.sum(
        lax.all_to_all(partial, "chan", 0, 0, tiled=False), axis=0
    )


def solution(mesh):
    return jax.shard_map(
        body,
        mesh=mesh,
        in_specs=(P(None, "chan", "tmpl"), P(None, "tmpl", "chan", None), P("tmpl"), P()),
        out_specs=P("tmpl", "chan"),
        check_vma=False,
    )
```

time: 372 us -> 127 us (0.34)
  local copies, waits for them, and re-layouts: 157 us -> 10 us
  matrix products: 60.3 us -> 0 us
  Pallas kernels: 0 us -> 46.5 us
  waiting for transfers between devices: 59.2 us -> 25.2 us
  blocking collectives: 47.2 us -> 14.6 us
  other arithmetic: 32 us -> 1.5 us
  starting transfers between devices: 0.08 us -> 15.3 us
    gather x144 -> x0, local copies, waits for them, and re-layouts: 101 us -> none
    dot_general x7 -> x0, matrix products: 60.3 us -> none  [the longest x4 24.3 us: product(): return jnp.einsum(form, left, right, preferred_element_type=jnp.float32)]
    reduce_scatter x2 -> x0, waiting for transfers between devices: 59.1 us -> none  [the longest x1 59.1 us: body(): lax.psum_scatter(partial_stack, 'chan', scatter_dimension=1, tiled=True)]
    pallas_call x0 -> x3, Pallas kernels: none -> 46.5 us  [the longest x1 39.8 us: detect(): pl.pallas_call(detect_kernel, grid=(halves,), in_specs=[pl.BlockSpec((pie...]
    psum x1 -> x0, blocking collectives: 26.5 us -> none  [body(): energy_chan, tmpl_energy = lax.psum((energy_part, tmpl_part), 'chan')]
    unnamed x36 -> x12, local copies, waits for them, and re-layouts: 28.4 us -> 7.6 us
    all_gather x1 -> x0, blocking collectives: 20.8 us -> none  [body(): energy = lax.all_gather(energy_chan, 'tmpl', axis=1, tiled=True)]
    neg x2 -> x0, other arithmetic: 18.3 us -> none  [the longest x1 9.16 us: inverse_table(): return jnp.concatenate([cosine.T, -sine.T], axis=0) * (2.0 / length)]
  transfers between devices with their start and end apart: 3 -> 8, of which waited for: 1 -> 7; matrix products, arithmetic and copies ran while one was open for 42% -> 3% of each run, Pallas kernels for 0% -> 5%
where the time goes in v1:
time: 127 us
  Pallas kernels  46.5 us (37%)
  waiting for transfers between devices  25.2 us (20%)
  starting transfers between devices  15.3 us (12%)
  blocking collectives  14.6 us (11%)
  between operations  13.5 us (11%)
  local copies, waits for them, and re-layouts  10 us (8%)
  other arithmetic  1.5 us (1%)
    pallas_call x1, Pallas kernels, detect(): pl.pallas_call(detect_kernel, grid=(halves,), in_specs=[pl.BlockSpec((pie...  39.8 us
    ppermute x7, starting transfers between devices, swap(): lax.ppermute(value, axis, [(i, partner(i)) for i in range(lax.axis_size(a...  15.3 us
    all_to_all x1, blocking collectives, body(): return jnp.sum(lax.all_to_all(partial, 'chan', 0, 0, tiled=False), axis=0)  14.6 us
    all_gather x1, waiting for transfers between devices, body(): lax.all_gather(jnp.transpose(samples, (0, 2, 1)), 'tmpl', axis=0, tiled=F...  12.6 us
    ppermute x7, waiting for transfers between devices, swap(): lax.ppermute(value, axis, [(i, partner(i)) for i in range(lax.axis_size(a...  11.8 us
    unnamed x12, local copies, waits for them, and re-layouts  7.6 us
    pallas_call x1, Pallas kernels, prepare_templates(): pl.pallas_call(template_kernel, grid=(templates,), in_specs=[pl.BlockSpec...  4.65 us
  transfers between devices with their start and end apart: 8, of which 7 were waited for; matrix products, arithmetic and copies ran while one was open for 3% of the time, Pallas kernels for 5%

profile of v1, /device:TPU:0, one launch (start us, length us, event | category | flops | bytes accessed | tf_op | source)
XLA Modules:
  0.0 126.6 jit_solution(11721557789599080484)
XLA Ops:
  6.5 0.7 all-gather.3.cloned.1.call-update
  7.3 3.4 %copy-done = bf16[2,16,256,512]{3,2,1,0:T(8,128)(2,1)S(1)} copy-done((bf16[2,16,256,512]{3,2,1,0:T(8,128)(2,1)S(1)}, bf16[2,16,256,512]{3,2,1,0:T(8,128)(2,1)}, u32[]{:S(2)}) %copy-start) | copy-done | bytes 8388632
  10.6 4.6 %template_flip.1 = (bf16[32,16,16,512]{3,2,1,0:T(8,128)(2,1)S(1)}, f32[16,128]{1,0:T(8,128)S(1)}) custom-call(bf16[2,16,256,512]{3,2,1,0:T(8,128)(2,1)S(1)} %copy-done), custom_call_target="tpu_custom_call" | custom-call | flops 20000000 | bytes 16777216 | tf_op jit(solution)/shard_map/template_flip/pallas_call | solution.py:52
  15.3 3.2 %copy-done.4 = bf16[32,16,16,512]{3,2,1,0:T(8,128)(2,1)} copy-done((bf16[32,16,16,512]{3,2,1,0:T(8,128)(2,1)}, bf16[32,16,16,512]{3,2,1,0:T(8,128)(2,1)S(1)}, u32[]{:S(2)}) %copy-start.4) | copy-done | bytes 8388632
  19.0 1.7 %collective-permute-start = (f32[16,65]{1,0:T(8,128)S(1)}, f32[16,65]{1,0:T(8,128)S(1)}, u32[]{:S(2)}, u32[]{:S(2)}) collective-permute-start(f32[16,65]{1,0:T(8,128)S(1)} %pad_maximum_fusion.3), channel_id=1, source_target_pairs={{0,16},{16,0},{32,48},{48,32},{64,80},{80,64},{96,112},{112,96},{1... | collective-permute-start | bytes 12488 | tf_op jit(solution)/shard_map/ppermute | solution.py:249
  20.7 2.0 %collective-permute-done = f32[16,65]{1,0:T(8,128)S(1)} collective-permute-done((f32[16,65]{1,0:T(8,128)S(1)}, f32[16,65]{1,0:T(8,128)S(1)}, u32[]{:S(2)}, u32[]{:S(2)}) %collective-permute-start) | collective-permute-done | bytes 4192 | tf_op jit(solution)/shard_map/ppermute | solution.py:249
  22.8 3.3 %collective-permute-start.1 = (f32[16,65]{1,0:T(8,128)S(1)}, f32[16,65]{1,0:T(8,128)S(1)}, u32[]{:S(2)}, u32[]{:S(2)}) collective-permute-start(f32[16,65]{1,0:T(8,128)S(1)} %fusion.8), channel_id=1, source_target_pairs={{0,32},{16,48},{32,0},{48,16},{64,96},{80,112},{96,64},{112,80},{1... | collective-permute-start | bytes 12488 | tf_op jit(solution)/shard_map/ppermute | solution.py:249
  26.1 1.9 %collective-permute-done.1 = f32[16,65]{1,0:T(8,128)S(1)} collective-permute-done((f32[16,65]{1,0:T(8,128)S(1)}, f32[16,65]{1,0:T(8,128)S(1)}, u32[]{:S(2)}, u32[]{:S(2)}) %collective-permute-start.1) | collective-permute-done | bytes 4192 | tf_op jit(solution)/shard_map/ppermute | solution.py:249
  28.0 3.1 %collective-permute-start.2 = (f32[16,65]{1,0:T(8,128)S(1)}, f32[16,65]{1,0:T(8,128)S(1)}, u32[]{:S(2)}, u32[]{:S(2)}) collective-permute-start(f32[16,65]{1,0:T(8,128)S(1)} %add.16), channel_id=1, source_target_pairs={{0,64},{16,80},{32,96},{48,112},{64,0},{80,16},{96,32},{112,48},{1... | collective-permute-start | bytes 12488 | tf_op jit(solution)/shard_map/ppermute | solution.py:249
  31.1 2.2 %collective-permute-done.2 = f32[16,65]{1,0:T(8,128)S(1)} collective-permute-done((f32[16,65]{1,0:T(8,128)S(1)}, f32[16,65]{1,0:T(8,128)S(1)}, u32[]{:S(2)}, u32[]{:S(2)}) %collective-permute-start.2) | collective-permute-done | bytes 4192 | tf_op jit(solution)/shard_map/ppermute | solution.py:249
  33.3 1.2 collective-permute-done.3
  34.5 1.6 %collective-permute-start.4 = (f32[16,128]{1,0:T(8,128)S(1)}, f32[16,128]{1,0:T(8,128)S(1)}, u32[]{:S(2)}, u32[]{:S(2)}) collective-permute-start(f32[16,128]{1,0:T(8,128)S(1)} %pad_maximum_fusion.4), channel_id=1, source_target_pairs={{0,2},{1,3},{2,0},{3,1},{4,6},{5,7},{6,4},{7,5},{8,10},{9,11},{10,... | collective-permute-start | bytes 24584 | tf_op jit(solution)/shard_map/ppermute | solution.py:249
  36.1 2.2 %collective-permute-done.4 = f32[16,128]{1,0:T(8,128)S(1)} collective-permute-done((f32[16,128]{1,0:T(8,128)S(1)}, f32[16,128]{1,0:T(8,128)S(1)}, u32[]{:S(2)}, u32[]{:S(2)}) %collective-permute-start.4) | collective-permute-done | bytes 8224 | tf_op jit(solution)/shard_map/ppermute | solution.py:249
  38.4 1.7 %collective-permute-start.5 = (f32[16,256]{1,0:T(8,128)S(1)}, f32[16,256]{1,0:T(8,128)S(1)}, u32[]{:S(2)}, u32[]{:S(2)}) collective-permute-start(f32[16,256]{1,0:T(8,128)S(1)} %pad_maximum_fusion.2), channel_id=1, source_target_pairs={{0,4},{1,5},{2,6},{3,7},{4,0},{5,1},{6,2},{7,3},{8,12},{9,13},{10,... | collective-permute-start | bytes 49160 | tf_op jit(solution)/shard_map/ppermute | solution.py:249
  40.4 1.0 copy.14.cos_ref
  41.5 1.0 copy.15.sin_ref
  42.6 4.0 %collective-permute-start.6 = (f32[16,512]{1,0:T(8,128)S(1)}, f32[16,512]{1,0:T(8,128)S(1)}, u32[]{:S(2)}, u32[]{:S(2)}) collective-permute-start(f32[16,512]{1,0:T(8,128)S(1)} %pad_maximum_fusion.1), channel_id=1, source_target_pairs={{0,8},{1,9},{2,10},{3,11},{4,12},{5,13},{6,14},{7,15},{8,0},{9,1},... | collective-permute-start | bytes 98312 | tf_op jit(solution)/shard_map/ppermute | solution.py:249
  46.7 2.4 %collective-permute-done.6 = f32[16,512]{1,0:T(8,128)S(1)} collective-permute-done((f32[16,512]{1,0:T(8,128)S(1)}, f32[16,512]{1,0:T(8,128)S(1)}, u32[]{:S(2)}, u32[]{:S(2)}) %collective-permute-start.6) | collective-permute-done | bytes 32800 | tf_op jit(solution)/shard_map/ppermute | solution.py:249
  49.1 2.1 %score_weights.1.weight_ref = f32[16,16,1024]{2,1,0:T(8,128)S(1)} custom-call(s32[16]{0:T(128)S(1)} %copy-done.3, s32[16]{0:T(128)S(1)} %copy-done.2, f32[16]{0:T(128)S(1)} %slice_reduce_fusion.refs_2_, f32[16,1024]{1,0:T(8,128)S(1)} %pad_maximum_fusion.refs_3_), custom_call_target="tpu_custom_call" | custom-call | flops 20000000 | bytes 2097152 | tf_op jit(solution)/shard_map/score_weights/pallas_call | solution.py:111
  51.2 1.0 copy-done.1
  52.2 12.6 %all-gather.3.cloned.1.call-done = bf16[256,64,256]{2,1,0:T(8,128)(2,1)} async-done(((bf16[16,64,256]{2,1,0:T(8,128)(2,1)}), bf16[256,64,256]{2,1,0:T(8,128)(2,1)}) %all-gather.3.cloned.1.call-update) | async-done | bytes 8388624 | tf_op jit(solution)/shard_map/all_gather | solution.py:261
  64.8 39.8 %detect.1 = f32[8,16,128]{2,1,0:T(8,128)} custom-call(bf16[16,16,64,256]{3,2,1,0:T(8,128)(2,1)} %bitcast.11, f32[16,16,1024]{2,1,0:T(8,128)} %copy-done.1, f32[512,256]{1,0:T(8,128)} %copy.14.cos_ref, f32[512,256]{1,0:T(8,128)} %copy.15.sin_ref, bf16[1024,1024]{1,0:T(8,128)(2,1)} %constant.42.clone.forward_ref, bf16[2048,128]{1,0:T(8,128)(2,1)} %constant.43.clone.select_ref, ...), custom_call_target="tpu_custom_call" | custom-call | flops 30000001024 | bytes 33554432 | tf_op jit(solution)/shard_map/detect/pallas_call | solution.py:218
  104.6 14.6 %all_to_all.5 = f32[8,16,128]{2,1,0:T(8,128)S(1)} all-to-all(f32[8,16,128]{2,1,0:T(8,128)} %detect.1), channel_id=1, replica_groups=mesh['chan'=8,'tmpl'=16] {'chan'}, dimensions={0} | all-to-all | bytes 131072 | tf_op jit(solution)/shard_map/all_to_all | solution.py:289
  119.2 0.6 reduce_sum.29
  (32 shorter events, 1.3 us)
Async XLA Ops:
  6.5 12.2 %copy-start.5 = (bf16[16,256,64]{1,2,0:T(8,128)(2,1)S(1)}, bf16[16,256,64]{1,2,0:T(8,128)(2,1)}, u32[]{:S(2)}) copy-start(bf16[16,256,64]{1,2,0:T(8,128)(2,1)} %param.8) | copy-start | bytes 1572868
  6.5 33.6 %copy-start.2 = (s32[16]{0:T(128)S(1)}, s32[16]{0:T(128)}, u32[]{:S(2)}) copy-start(s32[16]{0:T(128)} %refs_1_.1) | copy-start | bytes 196
  6.5 42.6 %copy-start.3 = (s32[16]{0:T(128)S(1)}, s32[16]{0:T(128)}, u32[]{:S(2)}) copy-start(s32[16]{0:T(128)} %refs_0_.1) | copy-start | bytes 196
  6.5 58.2 %all-gather.3.cloned.1.call-start = ((), (), s32[]{:S(2)}) async-start(), calls=%async_computation.1 | async-start | bytes 8912896 | tf_op jit(solution)/shard_map/all_gather | solution.py:261
  7.3 3.4 %copy-start = (bf16[2,16,256,512]{3,2,1,0:T(8,128)(2,1)S(1)}, bf16[2,16,256,512]{3,2,1,0:T(8,128)(2,1)}, u32[]{:S(2)}) copy-start(bf16[2,16,256,512]{3,2,1,0:T(8,128)(2,1)} %g_ref.1) | copy-start | bytes 25165828
  15.3 3.2 %copy-start.4 = (bf16[32,16,16,512]{3,2,1,0:T(8,128)(2,1)}, bf16[32,16,16,512]{3,2,1,0:T(8,128)(2,1)S(1)}, u32[]{:S(2)}) copy-start(bf16[32,16,16,512]{3,2,1,0:T(8,128)(2,1)S(1)} %get-tuple-element.8.tmpl_hbm) | copy-start | bytes 25165828
  19.0 3.7 %collective-permute-start = (f32[16,65]{1,0:T(8,128)S(1)}, f32[16,65]{1,0:T(8,128)S(1)}, u32[]{:S(2)}, u32[]{:S(2)}) collective-permute-start(f32[16,65]{1,0:T(8,128)S(1)} %pad_maximum_fusion.3), channel_id=1, source_target_pairs={{0,16},{16,0},{32,48},{48,32},{64,80},{80,64},{96,112},{112,96},{1... | collective-permute-start | bytes 12488 | tf_op jit(solution)/shard_map/ppermute | solution.py:249
  22.8 5.2 %collective-permute-start.1 = (f32[16,65]{1,0:T(8,128)S(1)}, f32[16,65]{1,0:T(8,128)S(1)}, u32[]{:S(2)}, u32[]{:S(2)}) collective-permute-start(f32[16,65]{1,0:T(8,128)S(1)} %fusion.8), channel_id=1, source_target_pairs={{0,32},{16,48},{32,0},{48,16},{64,96},{80,112},{96,64},{112,80},{1... | collective-permute-start | bytes 12488 | tf_op jit(solution)/shard_map/ppermute | solution.py:249
  28.0 5.3 %collective-permute-start.2 = (f32[16,65]{1,0:T(8,128)S(1)}, f32[16,65]{1,0:T(8,128)S(1)}, u32[]{:S(2)}, u32[]{:S(2)}) collective-permute-start(f32[16,65]{1,0:T(8,128)S(1)} %add.16), channel_id=1, source_target_pairs={{0,64},{16,80},{32,96},{48,112},{64,0},{80,16},{96,32},{112,48},{1... | collective-permute-start | bytes 12488 | tf_op jit(solution)/shard_map/ppermute | solution.py:249
  33.3 1.2 collective-permute-start.3
  34.5 3.8 %collective-permute-start.4 = (f32[16,128]{1,0:T(8,128)S(1)}, f32[16,128]{1,0:T(8,128)S(1)}, u32[]{:S(2)}, u32[]{:S(2)}) collective-permute-start(f32[16,128]{1,0:T(8,128)S(1)} %pad_maximum_fusion.4), channel_id=1, source_target_pairs={{0,2},{1,3},{2,0},{3,1},{4,6},{5,7},{6,4},{7,5},{8,10},{9,11},{10,... | collective-permute-start | bytes 24584 | tf_op jit(solution)/shard_map/ppermute | solution.py:249
  38.4 4.1 %collective-permute-start.5 = (f32[16,256]{1,0:T(8,128)S(1)}, f32[16,256]{1,0:T(8,128)S(1)}, u32[]{:S(2)}, u32[]{:S(2)}) collective-permute-start(f32[16,256]{1,0:T(8,128)S(1)} %pad_maximum_fusion.2), channel_id=1, source_target_pairs={{0,4},{1,5},{2,6},{3,7},{4,0},{5,1},{6,2},{7,3},{8,12},{9,13},{10,... | collective-permute-start | bytes 49160 | tf_op jit(solution)/shard_map/ppermute | solution.py:249
  42.6 6.5 %collective-permute-start.6 = (f32[16,512]{1,0:T(8,128)S(1)}, f32[16,512]{1,0:T(8,128)S(1)}, u32[]{:S(2)}, u32[]{:S(2)}) collective-permute-start(f32[16,512]{1,0:T(8,128)S(1)} %pad_maximum_fusion.1), channel_id=1, source_target_pairs={{0,8},{1,9},{2,10},{3,11},{4,12},{5,13},{6,14},{7,15},{8,0},{9,1},... | collective-permute-start | bytes 98312 | tf_op jit(solution)/shard_map/ppermute | solution.py:249
  51.2 1.0 copy-start.1
Sparse Core Ops, SparseCore 0:
  9.1 55.6 all-gather.2

commit v2 on v1

v2 whole, which is shorter than its diff:
```python
import math

import jax
import jax.numpy as jnp
import numpy as np
from jax import lax
from jax.experimental import pallas as pl
from jax.experimental.pallas import tpu as pltpu
from jax.sharding import PartitionSpec as P

epsilon = 1e-06
LANES = 128
BLOCK = 16
F32 = jnp.float32
BF16 = jnp.bfloat16


def bin_order(bins):
    return np.concatenate([np.arange(0, bins, 2), np.arange(1, bins, 2)])


def tables(length):
    bins = length // 2
    angle = 2.0 * np.pi * (np.outer(bin_order(bins), np.arange(length)) % length) / length
    cosine, sine = np.cos(angle), -np.sin(angle)
    near = bins // 2
    even = np.concatenate([cosine[:near, :bins], sine[:near, :bins]], axis=0)
    odd = np.concatenate([cosine[near:, :bins], sine[near:, :bins]], axis=0)
    backward = np.concatenate([cosine, sine], axis=0) * (2.0 / length)
    high = backward.astype(BF16)
    low = (backward - high.astype(np.float64)).astype(BF16)
    return even.astype(BF16), odd.astype(BF16), high, low


def template_kernel(g_ref, out_ref, energy_ref, flipped):
    t = pl.program_id(0)
    channels, bins = g_ref.shape[2:]
    total = jnp.zeros((1, bins), F32)
    for part in range(2):
        wide = g_ref[part, 0].astype(F32)
        total = total + jnp.sum(wide * wide, axis=0, keepdims=True)
        turned = wide.T
        half = bins // 2 // BLOCK
        for j in range(channels // LANES):
            flipped[j] = turned[:, j * LANES : (j + 1) * LANES]
            first = part * channels + j * LANES
            for parity in range(2):
                rows = flipped[j, pl.ds(parity, bins // 2, stride=2), :].astype(BF16)
                out_ref[parity * half : (parity + 1) * half, 0, :, first : first + LANES] = (
                    rows.reshape(half, BLOCK, LANES)
                )
    folded = total[:, :LANES]
    for j in range(1, bins // LANES):
        folded = folded + total[:, j * LANES : (j + 1) * LANES]
    energy_ref[pl.ds(t, 1), :] = folded


def prepare_templates(template_spectra):
    _, templates, channels, bins = template_spectra.shape
    return pl.pallas_call(
        template_kernel,
        grid=(templates,),
        in_specs=[pl.BlockSpec((2, 1, channels, bins), lambda t: (0, t, 0, 0))],
        out_specs=[
            pl.BlockSpec((bins // BLOCK, 1, BLOCK, 2 * channels), lambda t: (0, t, 0, 0)),
            pl.BlockSpec((templates, LANES), lambda t: (0, 0)),
        ],
        out_shape=[
            jax.ShapeDtypeStruct((bins // BLOCK, templates, BLOCK, 2 * channels), BF16),
            jax.ShapeDtypeStruct((templates, LANES), F32),
        ],
        scratch_shapes=[pltpu.VMEM((channels // LANES, bins, LANES), F32)],
        compiler_params=pltpu.CompilerParams(vmem_limit_bytes=12 << 20),
        cost_estimate=pl.CostEstimate(flops=20_000_000, bytes_accessed=16 << 20, transcendentals=0),
        name="template_flip",
    )(template_spectra)


def weight_kernel(channel_total, scale, lag_ref, offset_ref, level_ref, energy_ref, out_ref, prefix):
    segments, length = energy_ref.shape
    templates = out_ref.shape[0]
    row = lax.broadcasted_iota(jnp.int32, (segments, length), 0)
    energy = energy_ref[...]
    delayed = jnp.zeros((segments, length), F32)
    for s in range(segments):
        delayed = jnp.where(row == s, pltpu.roll(energy, offset_ref[s], axis=1), delayed)
    before = lax.broadcasted_iota(jnp.int32, (LANES, LANES), 0) < lax.broadcasted_iota(
        jnp.int32, (LANES, LANES), 1
    )
    before = before.astype(F32)
    carry = jnp.zeros((segments, 1), F32)
    blocks = length // LANES
    for j in range(blocks):
        piece = delayed[:, j * LANES : (j + 1) * LANES]
        prefix[:, j * LANES : (j + 1) * LANES] = carry + jnp.dot(
            piece, before, precision=lax.Precision.HIGHEST, preferred_element_type=F32
        )
        carry = carry + jnp.sum(piece, axis=1, keepdims=True)
    first = prefix[:, :length]
    prefix[:, length : 2 * length] = first + carry
    prefix[:, 2 * length :] = first[:, :LANES] + 2.0 * carry
    span = length + LANES
    for t in range(templates):
        lag = lag_ref[t]
        start = pl.multiple_of((lag // LANES) * LANES, LANES)
        ahead = pltpu.roll(prefix[:, pl.ds(start, span)], span - lag % LANES, axis=1)[:, :length]
        power = (ahead - first) / (channel_total * lag.astype(F32))
        out_ref[t] = scale * lax.rsqrt(level_ref[t] * power + epsilon)


def score_weights(lag_lengths, offsets, level, energy, channel_total):
    segments, length = energy.shape
    templates = lag_lengths.shape[0]
    smem = pl.BlockSpec(memory_space=pltpu.SMEM)
    vmem = pl.BlockSpec(memory_space=pltpu.VMEM)

    def kernel(*refs):
        weight_kernel(channel_total, 1.0 / math.sqrt(segments), *refs)

    return pl.pallas_call(
        kernel,
        in_specs=[smem, smem, smem, vmem],
        out_specs=vmem,
        out_shape=jax.ShapeDtypeStruct((templates, segments, length), F32),
        scratch_shapes=[pltpu.VMEM((segments, 2 * length + LANES), F32)],
        compiler_params=pltpu.CompilerParams(vmem_limit_bytes=16 << 20),
        cost_estimate=pl.CostEstimate(flops=20_000_000, bytes_accessed=2 << 20, transcendentals=262144),
        name="score_weights",
    )(lag_lengths, offsets, level, energy)


def store_spectra(spectra, s, even_ref, odd_ref, summed, differed):
    near, channels = even_ref.shape[0] // 2, summed.shape[-1]
    for first, table, record in ((0, even_ref, summed), (near, odd_ref, differed)):
        result = jnp.dot(table[...], record[...], preferred_element_type=F32).astype(BF16)
        real, imag = result[:near], result[near:]
        spectra[0, s, first : first + near, :channels] = real
        spectra[0, s, first : first + near, channels:] = imag
        spectra[1, s, first : first + near, :channels] = imag
        spectra[1, s, first : first + near, channels:] = -real


def exchange_lanes(blocks):
    blocks = list(blocks)
    index = lax.broadcasted_iota(jnp.int32, blocks[0].shape, 1) // BLOCK
    for bit in (1, 2, 4):
        upper = (index & bit) != 0
        for i in range(8):
            if i & bit:
                continue
            first, second = blocks[i], blocks[i + bit]
            shift = BLOCK * bit
            blocks[i] = jnp.where(upper, pltpu.roll(second, shift, axis=1), first)
            blocks[i + bit] = jnp.where(upper, second, pltpu.roll(first, LANES - shift, axis=1))
    return blocks


def detect_kernel(
    record_hbm, tmpl_hbm, even_hbm, odd_hbm, high_hbm, low_hbm, cos_ref, sin_ref, weight_ref, out_ref,
    record, tmpl, even, odd, high, low, summed, differed, spectra, diagonal, cross, sems,
):
    pieces, late, piece, channels = record_hbm.shape
    templates, segments, length = weight_ref.shape
    bins = length // 2
    lanes = templates * BLOCK
    group = summed.shape[0]

    def load(s):
        return pltpu.make_async_copy(record_hbm.at[:, s], record.at[s], sems.at[s])

    tables_in = [
        pltpu.make_async_copy(even_hbm, even, sems.at[late]),
        pltpu.make_async_copy(odd_hbm, odd, sems.at[late + 1]),
    ]
    later_in = [
        pltpu.make_async_copy(tmpl_hbm, tmpl, sems.at[late + 2]),
        pltpu.make_async_copy(high_hbm, high, sems.at[late + 3]),
        pltpu.make_async_copy(low_hbm, low, sems.at[late + 4]),
    ]
    load(0).start()
    for copy in tables_in:
        copy.start()
    for s in range(1, late):
        load(s).start()
    for copy in later_in:
        copy.start()
    for copy in tables_in:
        copy.wait()

    @pl.loop(0, late // group)
    def _(i):
        for u in range(group):
            s = i * group + u
            load(s).wait()
            first = record[s, : pieces // 2].reshape(bins, channels)
            second = record[s, pieces // 2 :].reshape(bins, channels)
            summed[u] = first + second
            differed[u] = first - second
            store_spectra(spectra, s, even, odd, summed.at[u], differed.at[u])

    later_in[0].wait()
    rows = 2 * segments * BLOCK
    keep = (
        lax.broadcasted_iota(jnp.int32, (rows, lanes), 0) % BLOCK
        == lax.broadcasted_iota(jnp.int32, (rows, lanes), 1) % BLOCK
    )

    @pl.loop(0, bins // BLOCK // 4)
    def _(i):
        for u in range(4):
            b = i * 4 + u
            start = pl.multiple_of(b * BLOCK, BLOCK)
            left = spectra[:, :, pl.ds(start, BLOCK), :].reshape(rows, 2 * channels)
            right = tmpl[b].reshape(lanes, 2 * channels)
            product = lax.dot_general(
                left, right, (((1,), (1,)), ((), ())), preferred_element_type=F32
            )
            product = jnp.where(keep, product, 0.0).reshape(2 * segments, BLOCK, lanes)
            diagonal[b] = jnp.sum(product, axis=1)

    for g in range(bins // LANES):
        for j in range(lanes // LANES):
            blocks = [diagonal[g * 8 + i, :, j * LANES : (j + 1) * LANES] for i in range(8)]
            for i, block in enumerate(exchange_lanes(blocks)):
                cross[j * 8 + i, :, g * LANES : (g + 1) * LANES] = block

    real, imag = cross[:, :segments, :], cross[:, segments:, :]
    cosine, sine = cos_ref[...][None], sin_ref[...][None]
    total = templates * segments
    delayed = jnp.concatenate(
        [
            (real * cosine + imag * sine).reshape(total, bins),
            (imag * cosine - real * sine).reshape(total, bins),
        ],
        axis=1,
    )
    delayed_high = delayed.astype(BF16)
    delayed_low = (delayed - delayed_high.astype(F32)).astype(BF16)
    later_in[1].wait()
    later_in[2].wait()
    both = jnp.dot(
        jnp.concatenate([delayed_high, delayed_low], axis=0), high[...], preferred_element_type=F32
    )
    result = both[:total] + both[total:]
    result = result + jnp.dot(delayed_high, low[...], preferred_element_type=F32)
    scores = result.reshape(templates, segments, length) * weight_ref[...]
    stack = jnp.sum(scores, axis=1)
    for j in range(length // LANES):
        out_ref[j] = stack[:, j * LANES : (j + 1) * LANES]


def detect(record, tmpl, even, odd, high, low, cosine, sine, weights):
    pieces, late, piece, channels = record.shape
    templates, segments, length = weights.shape
    bins = length // 2
    vmem = pl.BlockSpec(memory_space=pltpu.VMEM)
    anywhere = pl.BlockSpec(memory_space=pl.ANY)
    group = 4
    return pl.pallas_call(
        detect_kernel,
        in_specs=[anywhere] * 6 + [vmem] * 3,
        out_specs=vmem,
        out_shape=jax.ShapeDtypeStruct((length // LANES, templates, LANES), F32),
        scratch_shapes=[
            pltpu.VMEM((late, pieces, piece, channels), BF16),
            pltpu.VMEM(tmpl.shape, BF16),
            pltpu.VMEM(even.shape, BF16),
            pltpu.VMEM(odd.shape, BF16),
            pltpu.VMEM(high.shape, BF16),
            pltpu.VMEM(low.shape, BF16),
            pltpu.VMEM((group, bins, channels), BF16),
            pltpu.VMEM((group, bins, channels), BF16),
            pltpu.VMEM((2, late, bins, 2 * channels), BF16),
            pltpu.VMEM((bins // BLOCK, 2 * segments, templates * BLOCK), F32),
            pltpu.VMEM((templates, 2 * segments, bins), F32),
            pltpu.SemaphoreType.DMA((late + 5,)),
        ],
        compiler_params=pltpu.CompilerParams(vmem_limit_bytes=54 << 20),
        cost_estimate=pl.CostEstimate(flops=12_000_000_000, bytes_accessed=24 << 20, transcendentals=0),
        name="detect",
    )(record, tmpl, even, odd, high, low, cosine, sine, weights)


def send(value, axis, move):
    return lax.ppermute(value, axis, [(i, move(i)) for i in range(lax.axis_size(axis))])


def body(samples, template_spectra, lag_lengths, offsets):
    segments, channels, piece = samples.shape
    chan_groups = lax.axis_size("chan")
    tmpl_groups = lax.axis_size("tmpl")
    channel_total = channels * chan_groups
    length = piece * tmpl_groups
    bins = length // 2
    templates = template_spectra.shape[1]
    me = lax.axis_index("tmpl")

    record = lax.all_gather(jnp.transpose(samples, (0, 2, 1)), "tmpl", axis=0, tiled=False)

    wide = samples.astype(F32)
    energy = jnp.sum(wide * wide, axis=1)
    tmpl, level = prepare_templates(template_spectra)
    level = jnp.sum(level, axis=1, keepdims=True) * (2.0 / length)
    sums = jnp.concatenate([energy, level], axis=1)
    for bit in (1, 2, 4):
        sums = sums + send(sums, "chan", lambda i: i ^ bit)
    energy = sums[:, :piece]
    level = sums[:, piece]
    for bit in (1, 2, 4, 8):
        other = send(energy, "tmpl", lambda i: i ^ bit)
        upper = (me & bit) != 0
        energy = jnp.concatenate(
            [jnp.where(upper, other, energy), jnp.where(upper, energy, other)], axis=1
        )
    weights = score_weights(lag_lengths, offsets, level, energy, channel_total)

    order = bin_order(bins).astype(np.int32)
    phase = offsets[:, None] * order[None, :] % length
    angle = phase.astype(F32) * (2.0 * math.pi / length)
    cosine, sine = jnp.cos(angle), jnp.sin(angle)
    even, odd, high, low = tables(length)
    partial = detect(record, tmpl, even, odd, high, low, cosine, sine, weights)
    return jnp.sum(lax.all_to_all(partial, "chan", 0, 0, tiled=False), axis=0)


def solution(mesh):
    return jax.shard_map(
        body,
        mesh=mesh,
        in_specs=(P(None, "chan", "tmpl"), P(None, "tmpl", "chan", None), P("tmpl"), P()),
        out_specs=P("tmpl", "chan"),
        check_vma=False,
    )
```

time: 127 us -> 107 us (0.84)
  Pallas kernels: 46.5 us -> 28.2 us
  local copies, waits for them, and re-layouts: 10 us -> 7.86 us
    pallas_call x1, Pallas kernels: 39.8 us -> 20.4 us  [detect(): pl.pallas_call(detect_kernel, in_specs=[anywhere] * 6 + [vmem] * 3, out_s...]
    reshape x2 -> x0, local copies, waits for them, and re-layouts: 2.04 us -> none  [the longest x1 1.04 us: body(): cosine = jnp.repeat(jnp.cos(angle), templates, axis=1)]
    ppermute x7, waiting for transfers between devices: 11.8 us -> 13.3 us  [send(): lax.ppermute(value, axis, [(i, move(i)) for i in range(lax.axis_size(axis...]
    pallas_call x1, Pallas kernels: 4.65 us -> 5.95 us  [prepare_templates(): pl.pallas_call(template_kernel, grid=(templates,), in_specs=[pl.BlockSpec...]
    unnamed x12 -> x14, local copies, waits for them, and re-layouts: 7.6 us -> 7.59 us
  transfers between devices with their start and end apart: 8 -> 8, of which waited for: 7 -> 8; matrix products, arithmetic and copies ran while one was open for 3% -> 2% of each run, Pallas kernels for 5% -> 7%
where the time goes in v2:
time: 107 us
  Pallas kernels  28.2 us (26%)
  waiting for transfers between devices  25.9 us (24%)
  starting transfers between devices  15.2 us (14%)
  blocking collectives  14.5 us (14%)
  between operations  13.5 us (13%)
  local copies, waits for them, and re-layouts  7.86 us (7%)
  other arithmetic  2.11 us (2%)
    pallas_call x1, Pallas kernels, detect(): pl.pallas_call(detect_kernel, in_specs=[anywhere] * 6 + [vmem] * 3, out_s...  20.4 us
    ppermute x7, starting transfers between devices, send(): lax.ppermute(value, axis, [(i, move(i)) for i in range(lax.axis_size(axis...  15.2 us
    all_to_all x1, blocking collectives, body(): return jnp.sum(lax.all_to_all(partial, 'chan', 0, 0, tiled=False), axis=0)  14.5 us
    ppermute x7, waiting for transfers between devices, send(): lax.ppermute(value, axis, [(i, move(i)) for i in range(lax.axis_size(axis...  13.3 us
    all_gather x1, waiting for transfers between devices, body(): lax.all_gather(jnp.transpose(samples, (0, 2, 1)), 'tmpl', axis=0, tiled=F...  11.9 us
    unnamed x14, local copies, waits for them, and re-layouts  7.59 us
    pallas_call x1, Pallas kernels, prepare_templates(): pl.pallas_call(template_kernel, grid=(templates,), in_specs=[pl.BlockSpec...  5.95 us
  transfers between devices with their start and end apart: 8, of which 8 were waited for; matrix products, arithmetic and copies ran while one was open for 2% of the time, Pallas kernels for 7%

profile of v2, /device:TPU:0, one launch (start us, length us, event | category | flops | bytes accessed | tf_op | source)
XLA Modules:
  0.0 107.3 jit_solution(8910572884633874645)
XLA Ops:
  6.6 0.7 all-gather.3.cloned.1.call-update
  7.3 3.4 %copy-done = bf16[2,16,256,512]{3,2,1,0:T(8,128)(2,1)S(1)} copy-done((bf16[2,16,256,512]{3,2,1,0:T(8,128)(2,1)S(1)}, bf16[2,16,256,512]{3,2,1,0:T(8,128)(2,1)}, u32[]{:S(2)}) %copy-start) | copy-done | bytes 8388632
  10.7 5.9 %template_flip.1 = (bf16[32,16,16,512]{3,2,1,0:T(8,128)(2,1)S(1)}, f32[16,128]{1,0:T(8,128)S(1)}) custom-call(bf16[2,16,256,512]{3,2,1,0:T(8,128)(2,1)S(1)} %copy-done), custom_call_target="tpu_custom_call" | custom-call | flops 20000000 | bytes 16777216 | tf_op jit(solution)/shard_map/template_flip/pallas_call | solution.py:60
  16.6 3.2 %copy-done.4 = bf16[32,16,16,512]{3,2,1,0:T(8,128)(2,1)} copy-done((bf16[32,16,16,512]{3,2,1,0:T(8,128)(2,1)}, bf16[32,16,16,512]{3,2,1,0:T(8,128)(2,1)S(1)}, u32[]{:S(2)}) %copy-start.4) | copy-done | bytes 8388632
  20.3 1.7 %collective-permute-start = (f32[16,65]{1,0:T(8,128)S(1)}, f32[16,65]{1,0:T(8,128)S(1)}, u32[]{:S(2)}, u32[]{:S(2)}) collective-permute-start(f32[16,65]{1,0:T(8,128)S(1)} %pad_maximum_fusion.3), channel_id=1, source_target_pairs={{0,16},{16,0},{32,48},{48,32},{64,80},{80,64},{96,112},{112,96},{1... | collective-permute-start | bytes 12488 | tf_op jit(solution)/shard_map/ppermute | solution.py:285
  22.0 2.0 %collective-permute-done = f32[16,65]{1,0:T(8,128)S(1)} collective-permute-done((f32[16,65]{1,0:T(8,128)S(1)}, f32[16,65]{1,0:T(8,128)S(1)}, u32[]{:S(2)}, u32[]{:S(2)}) %collective-permute-start) | collective-permute-done | bytes 4192 | tf_op jit(solution)/shard_map/ppermute | solution.py:285
  24.1 3.3 %collective-permute-start.1 = (f32[16,65]{1,0:T(8,128)S(1)}, f32[16,65]{1,0:T(8,128)S(1)}, u32[]{:S(2)}, u32[]{:S(2)}) collective-permute-start(f32[16,65]{1,0:T(8,128)S(1)} %fusion.5), channel_id=1, source_target_pairs={{0,32},{16,48},{32,0},{48,16},{64,96},{80,112},{96,64},{112,80},{1... | collective-permute-start | bytes 12488 | tf_op jit(solution)/shard_map/ppermute | solution.py:285
  27.4 1.9 %collective-permute-done.1 = f32[16,65]{1,0:T(8,128)S(1)} collective-permute-done((f32[16,65]{1,0:T(8,128)S(1)}, f32[16,65]{1,0:T(8,128)S(1)}, u32[]{:S(2)}, u32[]{:S(2)}) %collective-permute-start.1) | collective-permute-done | bytes 4192 | tf_op jit(solution)/shard_map/ppermute | solution.py:285
  29.3 3.1 %collective-permute-start.2 = (f32[16,65]{1,0:T(8,128)S(1)}, f32[16,65]{1,0:T(8,128)S(1)}, u32[]{:S(2)}, u32[]{:S(2)}) collective-permute-start(f32[16,65]{1,0:T(8,128)S(1)} %add.17), channel_id=1, source_target_pairs={{0,64},{16,80},{32,96},{48,112},{64,0},{80,16},{96,32},{112,48},{1... | collective-permute-start | bytes 12488 | tf_op jit(solution)/shard_map/ppermute | solution.py:285
  32.4 2.2 %collective-permute-done.2 = f32[16,65]{1,0:T(8,128)S(1)} collective-permute-done((f32[16,65]{1,0:T(8,128)S(1)}, f32[16,65]{1,0:T(8,128)S(1)}, u32[]{:S(2)}, u32[]{:S(2)}) %collective-permute-start.2) | collective-permute-done | bytes 4192 | tf_op jit(solution)/shard_map/ppermute | solution.py:285
  34.6 1.2 %collective-permute-done.3 = f32[16,64]{1,0:T(8,128)S(1)} collective-permute-done((f32[16,64]{1,0:T(8,128)S(1)}, f32[16,64]{1,0:T(8,128)S(1)}, u32[]{:S(2)}, u32[]{:S(2)}) %collective-permute-start.3) | collective-permute-done | bytes 4128 | tf_op jit(solution)/shard_map/ppermute | solution.py:285
  35.8 1.6 %collective-permute-start.4 = (f32[16,128]{1,0:T(8,128)S(1)}, f32[16,128]{1,0:T(8,128)S(1)}, u32[]{:S(2)}, u32[]{:S(2)}) collective-permute-start(f32[16,128]{1,0:T(8,128)S(1)} %pad_maximum_fusion.4), channel_id=1, source_target_pairs={{0,2},{1,3},{2,0},{3,1},{4,6},{5,7},{6,4},{7,5},{8,10},{9,11},{10,... | collective-permute-start | bytes 24584 | tf_op jit(solution)/shard_map/ppermute | solution.py:285
  37.4 2.2 %collective-permute-done.4 = f32[16,128]{1,0:T(8,128)S(1)} collective-permute-done((f32[16,128]{1,0:T(8,128)S(1)}, f32[16,128]{1,0:T(8,128)S(1)}, u32[]{:S(2)}, u32[]{:S(2)}) %collective-permute-start.4) | collective-permute-done | bytes 8224 | tf_op jit(solution)/shard_map/ppermute | solution.py:285
  39.7 1.7 %collective-permute-start.5 = (f32[16,256]{1,0:T(8,128)S(1)}, f32[16,256]{1,0:T(8,128)S(1)}, u32[]{:S(2)}, u32[]{:S(2)}) collective-permute-start(f32[16,256]{1,0:T(8,128)S(1)} %pad_maximum_fusion.2), channel_id=1, source_target_pairs={{0,4},{1,5},{2,6},{3,7},{4,0},{5,1},{6,2},{7,3},{8,12},{9,13},{10,... | collective-permute-start | bytes 49160 | tf_op jit(solution)/shard_map/ppermute | solution.py:285
  41.5 0.8 fusion.3
  42.3 1.5 %collective-permute-done.5 = f32[16,256]{1,0:T(8,128)S(1)} collective-permute-done((f32[16,256]{1,0:T(8,128)S(1)}, f32[16,256]{1,0:T(8,128)S(1)}, u32[]{:S(2)}, u32[]{:S(2)}) %collective-permute-start.5) | collective-permute-done | bytes 16416 | tf_op jit(solution)/shard_map/ppermute | solution.py:285
  43.8 3.7 %collective-permute-start.6 = (f32[16,512]{1,0:T(8,128)S(1)}, f32[16,512]{1,0:T(8,128)S(1)}, u32[]{:S(2)}, u32[]{:S(2)}) collective-permute-start(f32[16,512]{1,0:T(8,128)S(1)} %pad_maximum_fusion.1), channel_id=1, source_target_pairs={{0,8},{1,9},{2,10},{3,11},{4,12},{5,13},{6,14},{7,15},{8,0},{9,1},... | collective-permute-start | bytes 98312 | tf_op jit(solution)/shard_map/ppermute | solution.py:285
  47.8 2.4 %collective-permute-done.6 = f32[16,512]{1,0:T(8,128)S(1)} collective-permute-done((f32[16,512]{1,0:T(8,128)S(1)}, f32[16,512]{1,0:T(8,128)S(1)}, u32[]{:S(2)}, u32[]{:S(2)}) %collective-permute-start.6) | collective-permute-done | bytes 32800 | tf_op jit(solution)/shard_map/ppermute | solution.py:285
  50.2 1.8 %score_weights.1.weight_ref = f32[16,16,1024]{2,1,0:T(8,128)S(1)} custom-call(s32[16]{0:T(128)S(1)} %copy-done.3, s32[16]{0:T(128)S(1)} %copy-done.2, f32[16]{0:T(128)S(1)} %slice_reduce_fusion.refs_2_, f32[16,1024]{1,0:T(8,128)S(1)} %pad_maximum_fusion.refs_3_), custom_call_target="tpu_custom_call" | custom-call | flops 20000000 | bytes 2097152 | tf_op jit(solution)/shard_map/score_weights/pallas_call | solution.py:120
  52.0 1.0 copy-done.1
  52.9 11.9 %all-gather.3.cloned.1.call-done = bf16[256,64,256]{2,1,0:T(8,128)(2,1)} async-done(((bf16[16,64,256]{2,1,0:T(8,128)(2,1)}), bf16[256,64,256]{2,1,0:T(8,128)(2,1)}) %all-gather.3.cloned.1.call-update) | async-done | bytes 8388624 | tf_op jit(solution)/shard_map/all_gather | solution.py:298
  64.8 20.4 %detect.1 = f32[8,16,128]{2,1,0:T(8,128)} custom-call(bf16[16,16,64,256]{3,2,1,0:T(8,128)(2,1)} %bitcast.7, bf16[32,16,16,512]{3,2,1,0:T(8,128)(2,1)} %copy-done.4, bf16[512,512]{1,0:T(8,128)(2,1)} %constant.45.clone.even_hbm, bf16[512,512]{1,0:T(8,128)(2,1)} %constant.46.clone.odd_hbm, bf16[1024,1024]{1,0:T(8,128)(2,1)} %constant.47.clone.high_hbm, ...), custom_call_target="tpu_custom_call" | custom-call | flops 12000000000 | bytes 25165824 | tf_op jit(solution)/shard_map/detect/pallas_call | solution.py:259
  85.3 14.5 %all_to_all.5 = f32[8,16,128]{2,1,0:T(8,128)S(1)} all-to-all(f32[8,16,128]{2,1,0:T(8,128)} %detect.1), channel_id=1, replica_groups=mesh['chan'=8,'tmpl'=16] {'chan'}, dimensions={0} | all-to-all | bytes 131072 | tf_op jit(solution)/shard_map/all_to_all | solution.py:323
  99.8 0.6 reduce_sum.29
  (30 shorter events, 1.0 us)
Async XLA Ops:
  6.5 34.9 %copy-start.6 = (s32[512]{0:T(512)S(1)}, s32[512]{0:T(512)}, u32[]{:S(2)}) copy-start(s32[512]{0:T(512)} %constant.49) | copy-start | bytes 6148
  6.5 13.5 %copy-start.5 = (bf16[16,256,64]{1,2,0:T(8,128)(2,1)S(1)}, bf16[16,256,64]{1,2,0:T(8,128)(2,1)}, u32[]{:S(2)}) copy-start(bf16[16,256,64]{1,2,0:T(8,128)(2,1)} %param.9) | copy-start | bytes 1572868
  6.5 34.9 %copy-start.2 = (s32[16]{0:T(128)S(1)}, s32[16]{0:T(128)}, u32[]{:S(2)}) copy-start(s32[16]{0:T(128)} %refs_1_.1) | copy-start | bytes 196
  6.5 43.6 %copy-start.3 = (s32[16]{0:T(128)S(1)}, s32[16]{0:T(128)}, u32[]{:S(2)}) copy-start(s32[16]{0:T(128)} %refs_0_.1) | copy-start | bytes 196
  6.5 58.3 %all-gather.3.cloned.1.call-start = ((), (), s32[]{:S(2)}) async-start(), calls=%async_computation.1 | async-start | bytes 8912896 | tf_op jit(solution)/shard_map/all_gather | solution.py:298
  7.3 3.4 %copy-start = (bf16[2,16,256,512]{3,2,1,0:T(8,128)(2,1)S(1)}, bf16[2,16,256,512]{3,2,1,0:T(8,128)(2,1)}, u32[]{:S(2)}) copy-start(bf16[2,16,256,512]{3,2,1,0:T(8,128)(2,1)} %g_ref.1) | copy-start | bytes 25165828
  16.6 3.2 %copy-start.4 = (bf16[32,16,16,512]{3,2,1,0:T(8,128)(2,1)}, bf16[32,16,16,512]{3,2,1,0:T(8,128)(2,1)S(1)}, u32[]{:S(2)}) copy-start(bf16[32,16,16,512]{3,2,1,0:T(8,128)(2,1)S(1)} %get-tuple-element.7.tmpl_hbm) | copy-start | bytes 25165828
  20.3 3.7 %collective-permute-start = (f32[16,65]{1,0:T(8,128)S(1)}, f32[16,65]{1,0:T(8,128)S(1)}, u32[]{:S(2)}, u32[]{:S(2)}) collective-permute-start(f32[16,65]{1,0:T(8,128)S(1)} %pad_maximum_fusion.3), channel_id=1, source_target_pairs={{0,16},{16,0},{32,48},{48,32},{64,80},{80,64},{96,112},{112,96},{1... | collective-permute-start | bytes 12488 | tf_op jit(solution)/shard_map/ppermute | solution.py:285
  24.1 5.2 %collective-permute-start.1 = (f32[16,65]{1,0:T(8,128)S(1)}, f32[16,65]{1,0:T(8,128)S(1)}, u32[]{:S(2)}, u32[]{:S(2)}) collective-permute-start(f32[16,65]{1,0:T(8,128)S(1)} %fusion.5), channel_id=1, source_target_pairs={{0,32},{16,48},{32,0},{48,16},{64,96},{80,112},{96,64},{112,80},{1... | collective-permute-start | bytes 12488 | tf_op jit(solution)/shard_map/ppermute | solution.py:285
  29.3 5.3 %collective-permute-start.2 = (f32[16,65]{1,0:T(8,128)S(1)}, f32[16,65]{1,0:T(8,128)S(1)}, u32[]{:S(2)}, u32[]{:S(2)}) collective-permute-start(f32[16,65]{1,0:T(8,128)S(1)} %add.17), channel_id=1, source_target_pairs={{0,64},{16,80},{32,96},{48,112},{64,0},{80,16},{96,32},{112,48},{1... | collective-permute-start | bytes 12488 | tf_op jit(solution)/shard_map/ppermute | solution.py:285
  34.6 1.2 %collective-permute-start.3 = (f32[16,64]{1,0:T(8,128)S(1)}, f32[16,64]{1,0:T(8,128)S(1)}, u32[]{:S(2)}, u32[]{:S(2)}) collective-permute-start(f32[16,64]{1,0:T(8,128)S(1)} %bitcast.6), channel_id=1, source_target_pairs={{0,1},{1,0},{2,3},{3,2},{4,5},{5,4},{6,7},{7,6},{8,9},{9,8},{10,11... | collective-permute-start | bytes 12296 | tf_op jit(solution)/shard_map/ppermute | solution.py:285
  35.8 3.8 %collective-permute-start.4 = (f32[16,128]{1,0:T(8,128)S(1)}, f32[16,128]{1,0:T(8,128)S(1)}, u32[]{:S(2)}, u32[]{:S(2)}) collective-permute-start(f32[16,128]{1,0:T(8,128)S(1)} %pad_maximum_fusion.4), channel_id=1, source_target_pairs={{0,2},{1,3},{2,0},{3,1},{4,6},{5,7},{6,4},{7,5},{8,10},{9,11},{10,... | collective-permute-start | bytes 24584 | tf_op jit(solution)/shard_map/ppermute | solution.py:285
  39.7 4.1 %collective-permute-start.5 = (f32[16,256]{1,0:T(8,128)S(1)}, f32[16,256]{1,0:T(8,128)S(1)}, u32[]{:S(2)}, u32[]{:S(2)}) collective-permute-start(f32[16,256]{1,0:T(8,128)S(1)} %pad_maximum_fusion.2), channel_id=1, source_target_pairs={{0,4},{1,5},{2,6},{3,7},{4,0},{5,1},{6,2},{7,3},{8,12},{9,13},{10,... | collective-permute-start | bytes 49160 | tf_op jit(solution)/shard_map/ppermute | solution.py:285
  43.8 6.3 %collective-permute-start.6 = (f32[16,512]{1,0:T(8,128)S(1)}, f32[16,512]{1,0:T(8,128)S(1)}, u32[]{:S(2)}, u32[]{:S(2)}) collective-permute-start(f32[16,512]{1,0:T(8,128)S(1)} %pad_maximum_fusion.1), channel_id=1, source_target_pairs={{0,8},{1,9},{2,10},{3,11},{4,12},{5,13},{6,14},{7,15},{8,0},{9,1},... | collective-permute-start | bytes 98312 | tf_op jit(solution)/shard_map/ppermute | solution.py:285
  52.0 1.0 copy-start.1
Sparse Core Ops, SparseCore 0:
  9.1 55.7 all-gather.2

commit v3 on v2

--- a/solution.py
+++ b/solution.py
@@ -32,48 +32,59 @@
     return even.astype(BF16), odd.astype(BF16), high, low
 
 
-def template_kernel(g_ref, out_ref, energy_ref, flipped):
-    t = pl.program_id(0)
-    channels, bins = g_ref.shape[2:]
-    total = jnp.zeros((1, bins), F32)
-    for part in range(2):
-        wide = g_ref[part, 0].astype(F32)
-        total = total + jnp.sum(wide * wide, axis=0, keepdims=True)
-        turned = wide.T
-        half = bins // 2 // BLOCK
-        for j in range(channels // LANES):
-            flipped[j] = turned[:, j * LANES : (j + 1) * LANES]
-            first = part * channels + j * LANES
-            for parity in range(2):
-                rows = flipped[j, pl.ds(parity, bins // 2, stride=2), :].astype(BF16)
-                out_ref[parity * half : (parity + 1) * half, 0, :, first : first + LANES] = (
-                    rows.reshape(half, BLOCK, LANES)
-                )
-    folded = total[:, :LANES]
-    for j in range(1, bins // LANES):
-        folded = folded + total[:, j * LANES : (j + 1) * LANES]
-    energy_ref[pl.ds(t, 1), :] = folded
+def turn(bins):
+    return (np.arange(bins)[None, :] == bin_order(bins)[:, None]).astype(BF16)
+
+
+def template_kernel(turn_ref, g_ref, out_ref, energy_ref):
+    step, channels, bins = g_ref.shape[1:]
+    block = turn_ref.shape[0]
+    for t in range(step):
+        total = jnp.zeros((8, bins), F32)
+        for part in range(2):
+            wide = g_ref[part, t].astype(F32)
+            total = total + jnp.sum((wide * wide).reshape(channels // 8, 8, bins), axis=0)
+            for j in range(bins // block):
+                rows = lax.dot_general(
+                    turn_ref[...], g_ref[part, t, :, j * block : (j + 1) * block],
+                    (((1,), (1,)), ((), ())), preferred_element_type=F32,
+                ).astype(BF16)
+                half = block // 2 // BLOCK
+                for parity in range(2):
+                    first = parity * (bins // 2 // BLOCK) + j * half
+                    out_ref[first : first + half, t, :, part * channels : (part + 1) * channels] = (
+                        rows[parity * block // 2 : (parity + 1) * block // 2].reshape(half, BLOCK, channels)
+                    )
+        total = jnp.sum(total, axis=0, keepdims=True)
+        folded = total[:, :LANES]
+        for j in range(1, bins // LANES):
+            folded = folded + total[:, j * LANES : (j + 1) * LANES]
+        energy_ref[pl.ds(pl.program_id(0) * step + t, 1), :] = folded
 
 
 def prepare_templates(template_spectra):
     _, templates, channels, bins = template_spectra.shape
+    step = 4
+    matrix = turn(256)
     return pl.pallas_call(
         template_kernel,
-        grid=(templates,),
-        in_specs=[pl.BlockSpec((2, 1, channels, bins), lambda t: (0, t, 0, 0))],
+        grid=(templates // step,),
+        in_specs=[
+            pl.BlockSpec(matrix.shape, lambda t: (0, 0)),
+            pl.BlockSpec((2, step, channels, bins), lambda t: (0, t, 0, 0)),
+        ],
         out_specs=[
-            pl.BlockSpec((bins // BLOCK, 1, BLOCK, 2 * channels), lambda t: (0, t, 0, 0)),
+            pl.BlockSpec((bins // BLOCK, step, BLOCK, 2 * channels), lambda t: (0, t, 0, 0)),
             pl.BlockSpec((templates, LANES), lambda t: (0, 0)),
         ],
         out_shape=[
             jax.ShapeDtypeStruct((bins // BLOCK, templates, BLOCK, 2 * channels), BF16),
             jax.ShapeDtypeStruct((templates, LANES), F32),
         ],
-        scratch_shapes=[pltpu.VMEM((channels // LANES, bins, LANES), F32)],
-        compiler_params=pltpu.CompilerParams(vmem_limit_bytes=12 << 20),
-        cost_estimate=pl.CostEstimate(flops=20_000_000, bytes_accessed=16 << 20, transcendentals=0),
+        compiler_params=pltpu.CompilerParams(vmem_limit_bytes=56 << 20),
+        cost_estimate=pl.CostEstimate(flops=2_200_000_000, bytes_accessed=16 << 20, transcendentals=0),
         name="template_flip",
-    )(template_spectra)
+    )(matrix, template_spectra)
 
 
 def weight_kernel(channel_total, scale, lag_ref, offset_ref, level_ref, energy_ref, out_ref, prefix):
@@ -156,49 +167,61 @@
 
 
 def detect_kernel(
-    record_hbm, tmpl_hbm, even_hbm, odd_hbm, high_hbm, low_hbm, cos_ref, sin_ref, weight_ref, out_ref,
-    record, tmpl, even, odd, high, low, summed, differed, spectra, diagonal, cross, sems,
+    own, own_c, own_x, own_xc, far, far_c, far_x, far_xc, beside, beside_c, beside_x, beside_xc,
+    place_ref, tmpl_hbm, even_hbm, odd_hbm, out_ref,
+    held, tmpl, even_ref, odd_ref, summed, differed, spectra, diagonal, sems, piece_sems,
 ):
-    pieces, late, piece, channels = record_hbm.shape
-    templates, segments, length = weight_ref.shape
-    bins = length // 2
+    segments, piece, channels = own.shape
+    templates, _, bins = out_ref.shape
     lanes = templates * BLOCK
     group = summed.shape[0]
-
-    def load(s):
-        return pltpu.make_async_copy(record_hbm.at[:, s], record.at[s], sems.at[s])
+    group = held.shape[1]
+    sources = [
+        (own, 0), (own_c, 0), (own_x, 0), (own_xc, 0),
+        (beside, 0), (beside, 1), (beside_x, 0), (beside_x, 1),
+        (far, 0), (far_c, 0), (far_x, 0), (far_xc, 0),
+        (beside_c, 1), (beside_c, 0), (beside_xc, 1), (beside_xc, 0),
+    ]
+
+    def fetch(i):
+        return [
+            pltpu.make_async_copy(
+                ref.at[pl.ds(k * segments + i * group, group)], held.at[j, i], piece_sems.at[i, j]
+            )
+            for j, (ref, k) in enumerate(sources)
+        ]
 
     tables_in = [
-        pltpu.make_async_copy(even_hbm, even, sems.at[late]),
-        pltpu.make_async_copy(odd_hbm, odd, sems.at[late + 1]),
+        pltpu.make_async_copy(even_hbm, even_ref, sems.at[0]),
+        pltpu.make_async_copy(odd_hbm, odd_ref, sems.at[1]),
     ]
-    later_in = [
-        pltpu.make_async_copy(tmpl_hbm, tmpl, sems.at[late + 2]),
-        pltpu.make_async_copy(high_hbm, high, sems.at[late + 3]),
-        pltpu.make_async_copy(low_hbm, low, sems.at[late + 4]),
-    ]
-    load(0).start()
-    for copy in tables_in:
-        copy.start()
-    for s in range(1, late):
-        load(s).start()
-    for copy in later_in:
-        copy.start()
-    for copy in tables_in:
-        copy.wait()
-
-    @pl.loop(0, late // group)
+    copy = pltpu.make_async_copy(tmpl_hbm, tmpl, sems.at[2])
+    rounds = segments // group
+    for started in fetch(0) + tables_in:
+        started.start()
+    for i in range(1, rounds):
+        for started in fetch(i):
+            started.start()
+    copy.start()
+
+    pairs = len(sources) // 2
+    starts = [pl.multiple_of(place_ref[k], piece) for k in range(pairs)]
+    signs = [place_ref[pairs + k].astype(F32).astype(BF16) for k in range(pairs)]
+    for started in tables_in:
+        started.wait()
+
+    @pl.loop(0, rounds)
     def _(i):
+        for started in fetch(i):
+            started.wait()
         for u in range(group):
-            s = i * group + u
-            load(s).wait()
-            first = record[s, : pieces // 2].reshape(bins, channels)
-            second = record[s, pieces // 2 :].reshape(bins, channels)
-            summed[u] = first + second
-            differed[u] = first - second
-            store_spectra(spectra, s, even, odd, summed.at[u], differed.at[u])
-
-    later_in[0].wait()
+            for k in range(pairs):
+                first, second = held[k, i, u], held[pairs + k, i, u]
+                summed[u, pl.ds(starts[k], piece), :] = first + second
+                differed[u, pl.ds(starts[k], piece), :] = (first - second) * signs[k]
+            store_spectra(spectra, i * group + u, even_ref, odd_ref, summed.at[u], differed.at[u])
+
+    copy.wait()
     rows = 2 * segments * BLOCK
     keep = (
         lax.broadcasted_iota(jnp.int32, (rows, lanes), 0) % BLOCK
@@ -222,8 +245,12 @@
         for j in range(lanes // LANES):
             blocks = [diagonal[g * 8 + i, :, j * LANES : (j + 1) * LANES] for i in range(8)]
             for i, block in enumerate(exchange_lanes(blocks)):
-                cross[j * 8 + i, :, g * LANES : (g + 1) * LANES] = block
-
+                out_ref[j * 8 + i, :, g * LANES : (g + 1) * LANES] = block
+
+
+def score_kernel(cross, high, low, cos_ref, sin_ref, weight_ref, out_ref):
+    templates, segments, length = weight_ref.shape
+    bins = length // 2
     real, imag = cross[:, :segments, :], cross[:, segments:, :]
     cosine, sine = cos_ref[...][None], sin_ref[...][None]
     total = templates * segments
@@ -236,8 +263,6 @@
     )
     delayed_high = delayed.astype(BF16)
     delayed_low = (delayed - delayed_high.astype(F32)).astype(BF16)
-    later_in[1].wait()
-    later_in[2].wait()
     both = jnp.dot(
         jnp.concatenate([delayed_high, delayed_low], axis=0), high[...], preferred_element_type=F32
     )
@@ -249,40 +274,68 @@
         out_ref[j] = stack[:, j * LANES : (j + 1) * LANES]
 
 
-def detect(record, tmpl, even, odd, high, low, cosine, sine, weights):
-    pieces, late, piece, channels = record.shape
-    templates, segments, length = weights.shape
-    bins = length // 2
+def cross_spectra(pieces, place, tmpl, even, odd):
+    segments, piece, channels = pieces[0].shape
+    templates = tmpl.shape[1]
+    bins = even.shape[0]
     vmem = pl.BlockSpec(memory_space=pltpu.VMEM)
     anywhere = pl.BlockSpec(memory_space=pl.ANY)
     group = 4
     return pl.pallas_call(
         detect_kernel,
-        in_specs=[anywhere] * 6 + [vmem] * 3,
+        in_specs=[anywhere] * len(pieces) + [pl.BlockSpec(memory_space=pltpu.SMEM)] + [anywhere] * 3,
         out_specs=vmem,
-        out_shape=jax.ShapeDtypeStruct((length // LANES, templates, LANES), F32),
+        out_shape=jax.ShapeDtypeStruct((templates, 2 * segments, bins), F32),
         scratch_shapes=[
-            pltpu.VMEM((late, pieces, piece, channels), BF16),
+            pltpu.VMEM((16, segments // group, group, piece, channels), BF16),
             pltpu.VMEM(tmpl.shape, BF16),
             pltpu.VMEM(even.shape, BF16),
             pltpu.VMEM(odd.shape, BF16),
-            pltpu.VMEM(high.shape, BF16),
-            pltpu.VMEM(low.shape, BF16),
             pltpu.VMEM((group, bins, channels), BF16),
             pltpu.VMEM((group, bins, channels), BF16),
-            pltpu.VMEM((2, late, bins, 2 * channels), BF16),
+            pltpu.VMEM((2, segments, bins, 2 * channels), BF16),
             pltpu.VMEM((bins // BLOCK, 2 * segments, templates * BLOCK), F32),
-            pltpu.VMEM((templates, 2 * segments, bins), F32),
-            pltpu.SemaphoreType.DMA((late + 5,)),
+            pltpu.SemaphoreType.DMA((3,)),
+            pltpu.SemaphoreType.DMA((segments // group, 16)),
         ],
-        compiler_params=pltpu.CompilerParams(vmem_limit_bytes=54 << 20),
+        compiler_params=pltpu.CompilerParams(vmem_limit_bytes=58 << 20),
         cost_estimate=pl.CostEstimate(flops=12_000_000_000, bytes_accessed=24 << 20, transcendentals=0),
-        name="detect",
-    )(record, tmpl, even, odd, high, low, cosine, sine, weights)
+        name="cross_spectra",
+    )(*pieces, place, tmpl, even, odd)
+
+
+def score(cross, high, low, cosine, sine, weights):
+    templates, _, length = weights.shape
+    vmem = pl.BlockSpec(memory_space=pltpu.VMEM)
+    return pl.pallas_call(
+        score_kernel,
+        in_specs=[vmem] * 6,
+        out_specs=vmem,
+        out_shape=jax.ShapeDtypeStruct((length // LANES, templates, LANES), F32),
+        compiler_params=pltpu.CompilerParams(vmem_limit_bytes=24 << 20),
+        cost_estimate=pl.CostEstimate(flops=2_000_000_000, bytes_accessed=6 << 20, transcendentals=0),
+        name="score",
+    )(cross, high, low, cosine, sine, weights)
 
 
 def send(value, axis, move):
     return lax.ppermute(value, axis, [(i, move(i)) for i in range(lax.axis_size(axis))])
+
+
+def apart(i):
+    return (i + (-4 if i % 2 else 4)) % 16
+
+
+def across(i):
+    return i ^ 2
+
+
+def sibling(i):
+    return i ^ 1
+
+
+def after(value, *earlier):
+    return lax.optimization_barrier((value, *earlier))[0]
 
 
 def body(samples, template_spectra, lag_lengths, offsets):
@@ -295,31 +348,60 @@
     templates = template_spectra.shape[1]
     me = lax.axis_index("tmpl")
 
-    record = lax.all_gather(jnp.transpose(samples, (0, 2, 1)), "tmpl", axis=0, tiled=False)
-
     wide = samples.astype(F32)
     energy = jnp.sum(wide * wide, axis=1)
-    tmpl, level = prepare_templates(template_spectra)
-    level = jnp.sum(level, axis=1, keepdims=True) * (2.0 / length)
-    sums = jnp.concatenate([energy, level], axis=1)
-    for bit in (1, 2, 4):
-        sums = sums + send(sums, "chan", lambda i: i ^ bit)
-    energy = sums[:, :piece]
-    level = sums[:, piece]
-    for bit in (1, 2, 4, 8):
+
+    def double(energy, bit):
         other = send(energy, "tmpl", lambda i: i ^ bit)
         upper = (me & bit) != 0
-        energy = jnp.concatenate(
+        return jnp.concatenate(
             [jnp.where(upper, other, energy), jnp.where(upper, energy, other)], axis=1
         )
+
+    fence = lax.optimization_barrier
+    own = jnp.transpose(samples, (0, 2, 1))
+    own_c = send(own, "tmpl", sibling)
+    beside = send(jnp.concatenate([own, own_c], axis=0), "tmpl", apart)
+    energy = double(double(energy, 1), 2)
+    own_x = send(after(own, energy), "tmpl", across)
+    tmpl, level = prepare_templates(after(template_spectra, energy))
+    level = jnp.sum(level, axis=1, keepdims=True) * (2.0 / length)
+    energy = double(energy, 4)
+    beside, tmpl, level, energy = fence((beside, tmpl, level, energy))
+
+    far = send(beside[:segments], "tmpl", apart)
+    beside_c = send(beside, "tmpl", sibling)
+    energy = double(energy, 8)
+    sums = jnp.concatenate([energy, jnp.broadcast_to(level, (templates, LANES))], axis=1)
+    sums = sums + send(sums, "chan", lambda i: i ^ 4)
+    own_xc = send(after(own_x, beside), "tmpl", sibling)
+    beside_x = send(after(jnp.concatenate([own_x, own_xc], axis=0), energy), "tmpl", apart)
+    far, sums = fence((far, sums))
+    far_x = send(far, "tmpl", across)
+    far_c = send(far, "tmpl", sibling)
+    sums = sums + send(sums, "chan", lambda i: i ^ 1)
+    sums = sums + send(sums, "chan", lambda i: i ^ 2)
+    energy, level = sums[:, :length], sums[:, length]
     weights = score_weights(lag_lengths, offsets, level, energy, channel_total)
+    beside_x, far_x, far_c, weights = fence((beside_x, far_x, far_c, weights))
+    beside_xc = send(beside_x, "tmpl", sibling)
+    far_xc = send(far_x, "tmpl", sibling)
 
     order = bin_order(bins).astype(np.int32)
     phase = offsets[:, None] * order[None, :] % length
     angle = phase.astype(F32) * (2.0 * math.pi / length)
     cosine, sine = jnp.cos(angle), jnp.sin(angle)
     even, odd, high, low = tables(length)
-    partial = detect(record, tmpl, even, odd, high, low, cosine, sine, weights)
+
+    k = lax.iota(jnp.int32, 8)
+    z = (me // 4 + jnp.where(k < 4, 0, 2 * (me % 2) - 1)) % 4
+    start = (z % 2 * 4 + ((me ^ k) & 3)) * piece
+    place = jnp.concatenate([start, jnp.where(z < 2, 1, -1)]).astype(jnp.int32)
+    pieces = (
+        own, own_c, own_x, own_xc, far, far_c, far_x, far_xc, beside, beside_c, beside_x, beside_xc,
+    )
+    cross = cross_spectra(pieces, place, tmpl, even, odd)
+    partial = score(cross, high, low, cosine, sine, weights)
     return jnp.sum(lax.all_to_all(partial, "chan", 0, 0, tiled=False), axis=0)
 
 

time: 107 us -> 92.6 us (0.87)
  between operations: 13.5 us -> 0.21 us
  waiting for transfers between devices: 25.9 us -> 19.2 us
  local copies, waits for them, and re-layouts: 7.86 us -> 3.2 us
  starting transfers between devices: 15.2 us -> 18.7 us
  Pallas kernels: 28.2 us -> 31.4 us
  other arithmetic: 2.11 us -> 5.17 us
    all_gather x1 -> x0, waiting for transfers between devices: 11.9 us -> none  [body(): lax.all_gather(jnp.transpose(samples, (0, 2, 1)), 'tmpl', axis=0, tiled=F...]
    ppermute x7 -> x18, waiting for transfers between devices: 13.3 us -> 19.2 us  [send(): lax.ppermute(value, axis, [(i, move(i)) for i in range(lax.axis_size(axis...]
    unnamed x14 -> x22, local copies, waits for them, and re-layouts: 7.59 us -> 1.93 us
    ppermute x7 -> x18, starting transfers between devices: 15.2 us -> 18.7 us  [send(): lax.ppermute(value, axis, [(i, move(i)) for i in range(lax.axis_size(axis...]
    pallas_call x2 -> x3, Pallas kernels: 26.4 us -> 29.7 us  [the longest x1 19.5 us: cross_spectra(): pl.pallas_call(detect_kernel, in_specs=[anywhere] * len(pieces) + [pl.Blo...]
    concatenate x5 -> x7, other arithmetic: 0.17 us -> 2.1 us  [the longest x1 1.32 us: body(): beside = send(jnp.concatenate([own, own_c], axis=0), 'tmpl', apart)]
    reduce_sum x1, other arithmetic: 0.21 us -> 1.29 us  [body(): energy = jnp.sum(wide * wide, axis=1)]
  transfers between devices with their start and end apart: 8 -> 18, of which waited for: 8 -> 10; matrix products, arithmetic and copies ran while one was open for 2% -> 6% of each run, Pallas kernels for 7% -> 11%
where the time goes in v3:
time: 92.6 us; the launch traced here: 92.2 us
  Pallas kernels  31.4 us (34%)
  waiting for transfers between devices  19.2 us (21%)
  starting transfers between devices  18.7 us (20%)
  blocking collectives  14.3 us (15%)
  other arithmetic  5.17 us (6%)
  local copies, waits for them, and re-layouts  3.2 us (3%)
    pallas_call x1, Pallas kernels, cross_spectra(): pl.pallas_call(detect_kernel, in_specs=[anywhere] * len(pieces) + [pl.Blo...  19.5 us
    ppermute x18, waiting for transfers between devices, send(): lax.ppermute(value, axis, [(i, move(i)) for i in range(lax.axis_size(axis...  19.2 us
    ppermute x18, starting transfers between devices, send(): lax.ppermute(value, axis, [(i, move(i)) for i in range(lax.axis_size(axis...  18.7 us
    all_to_all x1, blocking collectives, body(): return jnp.sum(lax.all_to_all(partial, 'chan', 0, 0, tiled=False), axis=0)  14.3 us
    pallas_call x1, Pallas kernels, prepare_templates(): pl.pallas_call(template_kernel, grid=(templates // step,), in_specs=[pl.B...  8.3 us
    unnamed x22, local copies, waits for them, and re-layouts  1.93 us
  transfers between devices with their start and end apart: 18, of which 10 were waited for; matrix products, arithmetic and copies ran while one was open for 6% of the time, Pallas kernels for 11%

profile of v3, /device:TPU:0, one launch (start us, length us, event | category | flops | bytes accessed | tf_op | source)
XLA Modules:
  0.0 92.2 jit_solution(4969394250402716762)
XLA Ops:
  0.0 1.3 %multiply_reduce_fusion = f32[16,64]{1,0:T(8,128)S(1)} fusion(bf16[16,256,64]{1,2,0:T(8,128)(2,1)} %param.10), kind=kLoop, calls=%fused_computation.2 | loop fusion | flops 785408 | bytes 528384 | tf_op jit(solution)/shard_map/reduce_sum | solution.py:352
  2.8 1.7 %collective-permute-start.2 = (f32[16,128]{1,0:T(8,128)S(1)}, f32[16,128]{1,0:T(8,128)S(1)}, u32[]{:S(2)}, u32[]{:S(2)}) collective-permute-start(f32[16,128]{1,0:T(8,128)S(1)} %pad_maximum_fusion.5), channel_id=1, source_target_pairs={{0,2},{1,3},{2,0},{3,1},{4,6},{5,7},{6,4},{7,5},{8,10},{9,11},{10,... | collective-permute-start | bytes 24584 | tf_op jit(solution)/shard_map/ppermute | solution.py:322
  4.4 1.3 %pad_maximum_fusion = bf16[32,64,256]{2,1,0:T(8,128)(2,1)S(1)} fusion(bf16[16,64,256]{2,1,0:T(8,128)(2,1)S(1)} %collective-permute-done.own_c, bf16[16,64,256]{2,1,0:T(8,128)(2,1)} %bitcast.5), kind=kLoop, calls=%fused_computation | loop fusion | flops 524288 | bytes 2097152 | tf_op jit(solution)/shard_map/concatenate | solution.py:364
  5.8 2.0 %collective-permute-start.4 = (bf16[32,64,256]{2,1,0:T(8,128)(2,1)S(1)}, bf16[32,64,256]{2,1,0:T(8,128)(2,1)}, u32[]{:S(2)}, u32[]{:S(2)}) collective-permute-start(bf16[32,64,256]{2,1,0:T(8,128)(2,1)S(1)} %pad_maximum_fusion), channel_id=1, source_target_pairs={{0,4},{1,13},{2,6},{3,15},{4,8},{5,1},{6,10},{7,3},{8,12},{9,5},{1... | collective-permute-start | bytes 3145736 | tf_op jit(solution)/shard_map/ppermute | solution.py:322
  7.8 1.9 %collective-permute-start.5 = (f32[16,256]{1,0:T(8,128)S(1)}, f32[16,256]{1,0:T(8,128)S(1)}, u32[]{:S(2)}, u32[]{:S(2)}) collective-permute-start(f32[16,256]{1,0:T(8,128)S(1)} %pad_maximum_fusion.4), channel_id=1, source_target_pairs={{0,4},{1,5},{2,6},{3,7},{4,0},{5,1},{6,2},{7,3},{8,12},{9,13},{10,... | collective-permute-start | bytes 49160 | tf_op jit(solution)/shard_map/ppermute | solution.py:322
  10.3 8.3 %template_flip.1 = (bf16[32,16,16,512]{3,2,1,0:T(8,128)(2,1)}, f32[16,128]{1,0:T(8,128)}) custom-call(bf16[256,256]{1,0:T(8,128)(2,1)} %constant.90.clone.turn_ref, bf16[2,16,256,512]{3,2,1,0:T(8,128)(2,1)} %g_ref), custom_call_target="tpu_custom_call" | custom-call | flops 2200000000 | bytes 16777216 | tf_op jit(solution)/shard_map/template_flip/pallas_call | solution.py:69
  20.4 2.3 %collective-permute-done.4.beside = bf16[32,64,256]{2,1,0:T(8,128)(2,1)} collective-permute-done((bf16[32,64,256]{2,1,0:T(8,128)(2,1)S(1)}, bf16[32,64,256]{2,1,0:T(8,128)(2,1)}, u32[]{:S(2)}, u32[]{:S(2)}) %collective-permute-start.4) | collective-permute-done | bytes 1048608 | tf_op jit(solution)/shard_map/ppermute | solution.py:322
  22.8 1.1 %collective-permute-done.3.own_x = bf16[16,64,256]{2,1,0:T(8,128)(2,1)S(1)} collective-permute-done((bf16[16,64,256]{2,1,0:T(8,128)(2,1)}, bf16[16,64,256]{2,1,0:T(8,128)(2,1)S(1)}, u32[]{:S(2)}, u32[]{:S(2)}) %collective-permute-start.3) | collective-permute-done | bytes 524320 | tf_op jit(solution)/shard_map/ppermute | solution.py:322
  23.9 1.5 %collective-permute-start.8 = (f32[16,512]{1,0:T(8,128)S(1)}, f32[16,512]{1,0:T(8,128)S(1)}, u32[]{:S(2)}, u32[]{:S(2)}) collective-permute-start(f32[16,512]{1,0:T(8,128)S(1)} %pad_maximum_fusion.3), channel_id=1, source_target_pairs={{0,8},{1,9},{2,10},{3,11},{4,12},{5,13},{6,14},{7,15},{8,0},{9,1},... | collective-permute-start | bytes 98312 | tf_op jit(solution)/shard_map/ppermute | solution.py:322
  27.1 2.2 %collective-permute-done.8 = f32[16,512]{1,0:T(8,128)S(1)} collective-permute-done((f32[16,512]{1,0:T(8,128)S(1)}, f32[16,512]{1,0:T(8,128)S(1)}, u32[]{:S(2)}, u32[]{:S(2)}) %collective-permute-start.8) | collective-permute-done | bytes 32800 | tf_op jit(solution)/shard_map/ppermute | solution.py:322
  29.4 2.8 %collective-permute-start.9 = (f32[16,1152]{1,0:T(8,128)S(1)}, f32[16,1152]{1,0:T(8,128)S(1)}, u32[]{:S(2)}, u32[]{:S(2)}) collective-permute-start(f32[16,1152]{1,0:T(8,128)S(1)} %pad_maximum_fusion.2), channel_id=1, source_target_pairs={{0,64},{16,80},{32,96},{48,112},{64,0},{80,16},{96,32},{112,48},{1... | collective-permute-start | bytes 221192 | tf_op jit(solution)/shard_map/ppermute | solution.py:322
  33.2 2.1 %collective-permute-done.9 = f32[16,1152]{1,0:T(8,128)S(1)} collective-permute-done((f32[16,1152]{1,0:T(8,128)S(1)}, f32[16,1152]{1,0:T(8,128)S(1)}, u32[]{:S(2)}, u32[]{:S(2)}) %collective-permute-start.9) | collective-permute-done | bytes 73760 | tf_op jit(solution)/shard_map/ppermute | solution.py:322
  35.3 1.6 %collective-permute-done.7.far = bf16[16,64,256]{2,1,0:T(8,128)(2,1)S(1)} collective-permute-done((bf16[16,64,256]{2,1,0:T(8,128)(2,1)S(1)}, bf16[16,64,256]{2,1,0:T(8,128)(2,1)S(1)}, u32[]{:S(2)}, u32[]{:S(2)}) %collective-permute-start.7) | collective-permute-done | bytes 524320 | tf_op jit(solution)/shard_map/ppermute | solution.py:322
  36.9 1.3 %collective-permute-start.11 = (bf16[16,64,256]{2,1,0:T(8,128)(2,1)S(1)}, bf16[16,64,256]{2,1,0:T(8,128)(2,1)}, u32[]{:S(2)}, u32[]{:S(2)}) collective-permute-start(bf16[16,64,256]{2,1,0:T(8,128)(2,1)S(1)} %collective-permute-done.7.far), channel_id=1, source_target_pairs={{0,2},{1,3},{2,0},{3,1},{4,6},{5,7},{6,4},{7,5},{8,10},{9,11},{10,... | collective-permute-start | bytes 1572872 | tf_op jit(solution)/shard_map/ppermute | solution.py:322
  38.2 1.6 %collective-permute-start.13 = (f32[16,1152]{1,0:T(8,128)S(1)}, f32[16,1152]{1,0:T(8,128)S(1)}, u32[]{:S(2)}, u32[]{:S(2)}) collective-permute-start(f32[16,1152]{1,0:T(8,128)S(1)} %fusion.11), channel_id=1, source_target_pairs={{0,16},{16,0},{32,48},{48,32},{64,80},{80,64},{96,112},{112,96},{1... | collective-permute-start | bytes 221192 | tf_op jit(solution)/shard_map/ppermute | solution.py:322
  39.8 3.1 %collective-permute-done.13 = f32[16,1152]{1,0:T(8,128)S(1)} collective-permute-done((f32[16,1152]{1,0:T(8,128)S(1)}, f32[16,1152]{1,0:T(8,128)S(1)}, u32[]{:S(2)}, u32[]{:S(2)}) %collective-permute-start.13) | collective-permute-done | bytes 73760 | tf_op jit(solution)/shard_map/ppermute | solution.py:322
  42.9 3.3 %collective-permute-start.14 = (f32[16,1152]{1,0:T(8,128)S(1)}, f32[16,1152]{1,0:T(8,128)S(1)}, u32[]{:S(2)}, u32[]{:S(2)}) collective-permute-start(f32[16,1152]{1,0:T(8,128)S(1)} %add.41), channel_id=1, source_target_pairs={{0,32},{16,48},{32,0},{48,16},{64,96},{80,112},{96,64},{112,80},{1... | collective-permute-start | bytes 221192 | tf_op jit(solution)/shard_map/ppermute | solution.py:322
  46.2 2.7 %collective-permute-done.14 = f32[16,1152]{1,0:T(8,128)S(1)} collective-permute-done((f32[16,1152]{1,0:T(8,128)S(1)}, f32[16,1152]{1,0:T(8,128)S(1)}, u32[]{:S(2)}, u32[]{:S(2)}) %collective-permute-start.14) | collective-permute-done | bytes 73760 | tf_op jit(solution)/shard_map/ppermute | solution.py:322
  49.0 1.8 %score_weights.1.weight_ref = f32[16,16,1024]{2,1,0:T(8,128)S(1)} custom-call(s32[16]{0:T(128)S(1)} %copy-done.1, s32[16]{0:T(128)S(1)} %copy-done, f32[16]{0:T(128)S(1)} %slice_reduce_fusion.refs_2_, f32[16,1024]{1,0:T(8,128)S(1)} %slice.13.refs_3_), custom_call_target="tpu_custom_call" | custom-call | flops 20000000 | bytes 2097152 | tf_op jit(solution)/shard_map/score_weights/pallas_call | solution.py:131
  52.5 2.2 %collective-permute-done.15.far_xc = bf16[16,64,256]{2,1,0:T(8,128)(2,1)} collective-permute-done((bf16[16,64,256]{2,1,0:T(8,128)(2,1)}, bf16[16,64,256]{2,1,0:T(8,128)(2,1)}, u32[]{:S(2)}, u32[]{:S(2)}) %collective-permute-start.15) | collective-permute-done | bytes 524320 | tf_op jit(solution)/shard_map/ppermute | solution.py:322
  54.7 19.5 %cross_spectra.1.cross = f32[16,32,512]{2,1,0:T(8,128)} custom-call(bf16[16,64,256]{2,1,0:T(8,128)(2,1)} %bitcast.7, bf16[16,64,256]{2,1,0:T(8,128)(2,1)} %copy-done.5, bf16[16,64,256]{2,1,0:T(8,128)(2,1)} %copy-done.6, bf16[16,64,256]{2,1,0:T(8,128)(2,1)} %copy-done.7, bf16[16,64,256]{2,1,0:T(8,128)(2,1)} %copy-done.9, bf16[16,64,256]{2,1,0:T(8,128)(2,1)} %copy-done.10, ...), custom_call_target="tpu_custom_call" | custom-call | flops 12000000000 | bytes 25165824 | tf_op jit(solution)/shard_map/cross_spectra/pallas_call | solution.py:284
  74.2 1.2 %copy-done.4 = f32[16,32,512]{2,1,0:T(8,128)S(1)} copy-done((f32[16,32,512]{2,1,0:T(8,128)S(1)}, f32[16,32,512]{2,1,0:T(8,128)}, u32[]{:S(2)}) %copy-start.4) | copy-done | bytes 1048600
  75.5 1.8 %score.1 = f32[8,16,128]{2,1,0:T(8,128)S(1)} custom-call(f32[16,32,512]{2,1,0:T(8,128)S(1)} %copy-done.4, bf16[1024,1024]{1,0:T(8,128)(2,1)S(1)} %copy-done.2, bf16[1024,1024]{1,0:T(8,128)(2,1)S(1)} %copy-done.3, f32[16,512]{1,0:T(8,128)S(1)} %get-tuple-element.44.cos_ref, f32[16,512]{1,0:T(8,128)S(1)} %get-tuple-element.43.sin_ref, ...), custom_call_target="tpu_custom_call" | custom-call | flops 2000000000 | bytes 6291456 | tf_op jit(solution)/shard_map/score/pallas_call | solution.py:310
  77.3 14.3 %all_to_all.5 = f32[8,16,128]{2,1,0:T(8,128)S(1)} all-to-all(f32[8,16,128]{2,1,0:T(8,128)S(1)} %score.1), channel_id=1, replica_groups=mesh['chan'=8,'tmpl'=16] {'chan'}, dimensions={0} | all-to-all | bytes 131072 | tf_op jit(solution)/shard_map/all_to_all | solution.py:405
  (63 shorter events, 9.1 us)
Async XLA Ops:
  0.0 49.0 %copy-start.1 = (s32[16]{0:T(128)S(1)}, s32[16]{0:T(128)}, u32[]{:S(2)}) copy-start(s32[16]{0:T(128)} %refs_0_.1) | copy-start | bytes 196
  0.0 49.0 %copy-start = (s32[16]{0:T(128)S(1)}, s32[16]{0:T(128)}, u32[]{:S(2)}) copy-start(s32[16]{0:T(128)} %refs_1_.1) | copy-start | bytes 196
  0.0 52.2 %copy-start.8 = (s32[512]{0:T(512)S(1)}, s32[512]{0:T(512)}, u32[]{:S(2)}) copy-start(s32[512]{0:T(512)} %constant.96) | copy-start | bytes 6148
  0.0 4.4 %collective-permute-start = (bf16[16,64,256]{2,1,0:T(8,128)(2,1)}, bf16[16,64,256]{2,1,0:T(8,128)(2,1)S(1)}, u32[]{:S(2)}, u32[]{:S(2)}) collective-permute-start(bf16[16,64,256]{2,1,0:T(8,128)(2,1)} %bitcast.4), channel_id=1, source_target_pairs={{0,1},{1,0},{2,3},{3,2},{4,5},{5,4},{6,7},{7,6},{8,9},{9,8},{10,11... | collective-permute-start | bytes 1572872 | tf_op jit(solution)/shard_map/ppermute | solution.py:322
  1.3 1.4 %collective-permute-start.1 = (f32[16,64]{1,0:T(8,128)S(1)}, f32[16,64]{1,0:T(8,128)S(1)}, u32[]{:S(2)}, u32[]{:S(2)}) collective-permute-start(f32[16,64]{1,0:T(8,128)S(1)} %multiply_reduce_fusion), channel_id=1, source_target_pairs={{0,1},{1,0},{2,3},{3,2},{4,5},{5,4},{6,7},{7,6},{8,9},{9,8},{10,11... | collective-permute-start | bytes 12296 | tf_op jit(solution)/shard_map/ppermute | solution.py:322
  2.8 5.0 %collective-permute-start.2 = (f32[16,128]{1,0:T(8,128)S(1)}, f32[16,128]{1,0:T(8,128)S(1)}, u32[]{:S(2)}, u32[]{:S(2)}) collective-permute-start(f32[16,128]{1,0:T(8,128)S(1)} %pad_maximum_fusion.5), channel_id=1, source_target_pairs={{0,2},{1,3},{2,0},{3,1},{4,6},{5,7},{6,4},{7,5},{8,10},{9,11},{10,... | collective-permute-start | bytes 24584 | tf_op jit(solution)/shard_map/ppermute | solution.py:322
  4.4 47.8 %copy-start.5 = (bf16[16,64,256]{2,1,0:T(8,128)(2,1)}, bf16[16,64,256]{2,1,0:T(8,128)(2,1)S(1)}, u32[]{:S(2)}) copy-start(bf16[16,64,256]{2,1,0:T(8,128)(2,1)S(1)} %collective-permute-done.own_c) | copy-start | bytes 1572868
  5.8 17.0 %collective-permute-start.4 = (bf16[32,64,256]{2,1,0:T(8,128)(2,1)S(1)}, bf16[32,64,256]{2,1,0:T(8,128)(2,1)}, u32[]{:S(2)}, u32[]{:S(2)}) collective-permute-start(bf16[32,64,256]{2,1,0:T(8,128)(2,1)S(1)} %pad_maximum_fusion), channel_id=1, source_target_pairs={{0,4},{1,13},{2,6},{3,15},{4,8},{5,1},{6,10},{7,3},{8,12},{9,5},{1... | collective-permute-start | bytes 3145736 | tf_op jit(solution)/shard_map/ppermute | solution.py:322
  7.8 12.6 %collective-permute-start.5 = (f32[16,256]{1,0:T(8,128)S(1)}, f32[16,256]{1,0:T(8,128)S(1)}, u32[]{:S(2)}, u32[]{:S(2)}) collective-permute-start(f32[16,256]{1,0:T(8,128)S(1)} %pad_maximum_fusion.4), channel_id=1, source_target_pairs={{0,4},{1,5},{2,6},{3,7},{4,0},{5,1},{6,2},{7,3},{8,12},{9,13},{10,... | collective-permute-start | bytes 49160 | tf_op jit(solution)/shard_map/ppermute | solution.py:322
  9.8 14.1 %collective-permute-start.3 = (bf16[16,64,256]{2,1,0:T(8,128)(2,1)}, bf16[16,64,256]{2,1,0:T(8,128)(2,1)S(1)}, u32[]{:S(2)}, u32[]{:S(2)}) collective-permute-start(bf16[16,64,256]{2,1,0:T(8,128)(2,1)} %bitcast.6), channel_id=1, source_target_pairs={{0,2},{1,3},{2,0},{3,1},{4,6},{5,7},{6,4},{7,5},{8,10},{9,11},{10,... | collective-permute-start | bytes 1572872 | tf_op jit(solution)/shard_map/ppermute | solution.py:322
  23.9 28.3 %copy-start.6 = (bf16[16,64,256]{2,1,0:T(8,128)(2,1)}, bf16[16,64,256]{2,1,0:T(8,128)(2,1)S(1)}, u32[]{:S(2)}) copy-start(bf16[16,64,256]{2,1,0:T(8,128)(2,1)S(1)} %collective-permute-done.3.own_x) | copy-start | bytes 1572868
  23.9 8.3 %collective-permute-start.6 = (bf16[16,64,256]{2,1,0:T(8,128)(2,1)S(1)}, bf16[16,64,256]{2,1,0:T(8,128)(2,1)S(1)}, u32[]{:S(2)}, u32[]{:S(2)}) collective-permute-start(bf16[16,64,256]{2,1,0:T(8,128)(2,1)S(1)} %collective-permute-done.3.own_x), channel_id=1, source_target_pairs={{0,1},{1,0},{2,3},{3,2},{4,5},{5,4},{6,7},{7,6},{8,9},{9,8},{10,11... | collective-permute-start | bytes 1572872 | tf_op jit(solution)/shard_map/ppermute | solution.py:322
  23.9 5.4 %collective-permute-start.8 = (f32[16,512]{1,0:T(8,128)S(1)}, f32[16,512]{1,0:T(8,128)S(1)}, u32[]{:S(2)}, u32[]{:S(2)}) collective-permute-start(f32[16,512]{1,0:T(8,128)S(1)} %pad_maximum_fusion.3), channel_id=1, source_target_pairs={{0,8},{1,9},{2,10},{3,11},{4,12},{5,13},{6,14},{7,15},{8,0},{9,1},... | collective-permute-start | bytes 98312 | tf_op jit(solution)/shard_map/ppermute | solution.py:322
  26.5 10.5 %collective-permute-start.7 = (bf16[16,64,256]{2,1,0:T(8,128)(2,1)S(1)}, bf16[16,64,256]{2,1,0:T(8,128)(2,1)S(1)}, u32[]{:S(2)}, u32[]{:S(2)}) collective-permute-start(bf16[16,64,256]{2,1,0:T(8,128)(2,1)S(1)} %slice.9), channel_id=1, source_target_pairs={{0,4},{1,13},{2,6},{3,15},{4,8},{5,1},{6,10},{7,3},{8,12},{9,5},{1... | collective-permute-start | bytes 1572872 | tf_op jit(solution)/shard_map/ppermute | solution.py:322
  29.4 5.9 %collective-permute-start.9 = (f32[16,1152]{1,0:T(8,128)S(1)}, f32[16,1152]{1,0:T(8,128)S(1)}, u32[]{:S(2)}, u32[]{:S(2)}) collective-permute-start(f32[16,1152]{1,0:T(8,128)S(1)} %pad_maximum_fusion.2), channel_id=1, source_target_pairs={{0,64},{16,80},{32,96},{48,112},{64,0},{80,16},{96,32},{112,48},{1... | collective-permute-start | bytes 221192 | tf_op jit(solution)/shard_map/ppermute | solution.py:322
  32.3 18.5 %collective-permute-start.10 = (bf16[32,64,256]{2,1,0:T(8,128)(2,1)S(1)}, bf16[32,64,256]{2,1,0:T(8,128)(2,1)}, u32[]{:S(2)}, u32[]{:S(2)}) collective-permute-start(bf16[32,64,256]{2,1,0:T(8,128)(2,1)S(1)} %pad_maximum_fusion.1), channel_id=1, source_target_pairs={{0,4},{1,13},{2,6},{3,15},{4,8},{5,1},{6,10},{7,3},{8,12},{9,5},{1... | collective-permute-start | bytes 3145736 | tf_op jit(solution)/shard_map/ppermute | solution.py:322
  36.9 13.8 %collective-permute-start.11 = (bf16[16,64,256]{2,1,0:T(8,128)(2,1)S(1)}, bf16[16,64,256]{2,1,0:T(8,128)(2,1)}, u32[]{:S(2)}, u32[]{:S(2)}) collective-permute-start(bf16[16,64,256]{2,1,0:T(8,128)(2,1)S(1)} %collective-permute-done.7.far), channel_id=1, source_target_pairs={{0,2},{1,3},{2,0},{3,1},{4,6},{5,7},{6,4},{7,5},{8,10},{9,11},{10,... | collective-permute-start | bytes 1572872 | tf_op jit(solution)/shard_map/ppermute | solution.py:322
  38.2 12.6 %collective-permute-start.12 = (bf16[16,64,256]{2,1,0:T(8,128)(2,1)S(1)}, bf16[16,64,256]{2,1,0:T(8,128)(2,1)S(1)}, u32[]{:S(2)}, u32[]{:S(2)}) collective-permute-start(bf16[16,64,256]{2,1,0:T(8,128)(2,1)S(1)} %collective-permute-done.7.far), channel_id=1, source_target_pairs={{0,1},{1,0},{2,3},{3,2},{4,5},{5,4},{6,7},{7,6},{8,9},{9,8},{10,11... | collective-permute-start | bytes 1572872 | tf_op jit(solution)/shard_map/ppermute | solution.py:322
  38.2 4.7 %collective-permute-start.13 = (f32[16,1152]{1,0:T(8,128)S(1)}, f32[16,1152]{1,0:T(8,128)S(1)}, u32[]{:S(2)}, u32[]{:S(2)}) collective-permute-start(f32[16,1152]{1,0:T(8,128)S(1)} %fusion.11), channel_id=1, source_target_pairs={{0,16},{16,0},{32,48},{48,32},{64,80},{80,64},{96,112},{112,96},{1... | collective-permute-start | bytes 221192 | tf_op jit(solution)/shard_map/ppermute | solution.py:322
  42.9 5.9 %collective-permute-start.14 = (f32[16,1152]{1,0:T(8,128)S(1)}, f32[16,1152]{1,0:T(8,128)S(1)}, u32[]{:S(2)}, u32[]{:S(2)}) collective-permute-start(f32[16,1152]{1,0:T(8,128)S(1)} %add.41), channel_id=1, source_target_pairs={{0,32},{16,48},{32,0},{48,16},{64,96},{80,112},{96,64},{112,80},{1... | collective-permute-start | bytes 221192 | tf_op jit(solution)/shard_map/ppermute | solution.py:322
  46.2 6.3 %collective-permute-start.16 = (bf16[32,64,256]{2,1,0:T(8,128)(2,1)}, bf16[32,64,256]{2,1,0:T(8,128)(2,1)}, u32[]{:S(2)}, u32[]{:S(2)}) collective-permute-start(bf16[32,64,256]{2,1,0:T(8,128)(2,1)} %collective-permute-done.4.beside), channel_id=1, source_target_pairs={{0,1},{1,0},{2,3},{3,2},{4,5},{5,4},{6,7},{7,6},{8,9},{9,8},{10,11... | collective-permute-start | bytes 3145736 | tf_op jit(solution)/shard_map/ppermute | solution.py:322
  50.8 3.8 %collective-permute-start.17 = (bf16[32,64,256]{2,1,0:T(8,128)(2,1)}, bf16[32,64,256]{2,1,0:T(8,128)(2,1)}, u32[]{:S(2)}, u32[]{:S(2)}) collective-permute-start(bf16[32,64,256]{2,1,0:T(8,128)(2,1)} %collective-permute-done.10.beside_x), channel_id=1, source_target_pairs={{0,1},{1,0},{2,3},{3,2},{4,5},{5,4},{6,7},{7,6},{8,9},{9,8},{10,11... | collective-permute-start | bytes 3145736 | tf_op jit(solution)/shard_map/ppermute | solution.py:322
  51.6 3.1 %collective-permute-start.15 = (bf16[16,64,256]{2,1,0:T(8,128)(2,1)}, bf16[16,64,256]{2,1,0:T(8,128)(2,1)}, u32[]{:S(2)}, u32[]{:S(2)}) collective-permute-start(bf16[16,64,256]{2,1,0:T(8,128)(2,1)} %collective-permute-done.11.far_x), channel_id=1, source_target_pairs={{0,1},{1,0},{2,3},{3,2},{4,5},{5,4},{6,7},{7,6},{8,9},{9,8},{10,11... | collective-permute-start | bytes 1572872 | tf_op jit(solution)/shard_map/ppermute | solution.py:322
  52.4 21.8 %copy-start.2 = (bf16[1024,1024]{1,0:T(8,128)(2,1)S(1)}, bf16[1024,1024]{1,0:T(8,128)(2,1)}, u32[]{:S(2)}) copy-start(bf16[1024,1024]{1,0:T(8,128)(2,1)} %constant.94.clone.high) | copy-start | bytes 6291460
  (5 other events, 54.3 us)

commit v4 on v3

v4 whole, which is shorter than its diff:
```python
import math

import jax
import jax.numpy as jnp
import numpy as np
from jax import lax
from jax.experimental import pallas as pl
from jax.experimental.pallas import tpu as pltpu
from jax.sharding import PartitionSpec as P

epsilon = 1e-06
LANES = 128
BLOCK = 16
F32 = jnp.float32
BF16 = jnp.bfloat16


def bin_order(bins):
    return np.concatenate([np.arange(0, bins, 2), np.arange(1, bins, 2)])


def tables(length):
    bins = length // 2
    angle = 2.0 * np.pi * (np.outer(bin_order(bins), np.arange(length)) % length) / length
    cosine, sine = np.cos(angle), -np.sin(angle)
    near = bins // 2
    even = np.concatenate([cosine[:near, :bins], sine[:near, :bins]], axis=0)
    odd = np.concatenate([cosine[near:, :bins], sine[near:, :bins]], axis=0)
    backward = np.concatenate([cosine, sine], axis=0) * (2.0 / length)
    return np.stack([even, odd]).astype(BF16), backward.astype(BF16)


def turn(bins):
    return (np.arange(bins)[None, :] == bin_order(bins)[:, None]).astype(BF16)


def template_kernel(turn_ref, g_ref, out_ref, energy_ref):
    step, channels, bins = g_ref.shape[1:]
    block = turn_ref.shape[0]
    for t in range(step):
        total = jnp.zeros((8, bins), F32)
        for part in range(2):
            wide = g_ref[part, t].astype(F32)
            total = total + jnp.sum((wide * wide).reshape(channels // 8, 8, bins), axis=0)
            for j in range(bins // block):
                rows = lax.dot_general(
                    turn_ref[...], g_ref[part, t, :, j * block : (j + 1) * block],
                    (((1,), (1,)), ((), ())), preferred_element_type=F32,
                ).astype(BF16)
                half = block // 2 // BLOCK
                for parity in range(2):
                    first = parity * (bins // 2 // BLOCK) + j * half
                    out_ref[first : first + half, t, :, part * channels : (part + 1) * channels] = (
                        rows[parity * block // 2 : (parity + 1) * block // 2].reshape(half, BLOCK, channels)
                    )
        level = jnp.sum(jnp.sum(total, axis=0, keepdims=True), axis=1, keepdims=True) * (1.0 / bins)
        energy_ref[pl.ds(pl.program_id(0) * step + t, 1), :] = jnp.broadcast_to(level, (1, LANES))


def prepare_templates(template_spectra):
    _, templates, channels, bins = template_spectra.shape
    step = 4
    matrix = turn(256)
    return pl.pallas_call(
        template_kernel,
        grid=(templates // step,),
        in_specs=[
            pl.BlockSpec(matrix.shape, lambda t: (0, 0)),
            pl.BlockSpec((2, step, channels, bins), lambda t: (0, t, 0, 0)),
        ],
        out_specs=[
            pl.BlockSpec((bins // BLOCK, step, BLOCK, 2 * channels), lambda t: (0, t, 0, 0)),
            pl.BlockSpec((templates, LANES), lambda t: (0, 0)),
        ],
        out_shape=[
            jax.ShapeDtypeStruct((bins // BLOCK, templates, BLOCK, 2 * channels), BF16),
            jax.ShapeDtypeStruct((templates, LANES), F32),
        ],
        compiler_params=pltpu.CompilerParams(vmem_limit_bytes=56 << 20),
        cost_estimate=pl.CostEstimate(flops=2_200_000_000, bytes_accessed=16 << 20, transcendentals=0),
        name="template_flip",
    )(matrix, template_spectra)


def weight_kernel(channel_total, scale, lag_ref, offset_ref, level_ref, energy_ref, out_ref, prefix):
    segments, length = energy_ref.shape
    templates = out_ref.shape[0]
    row = lax.broadcasted_iota(jnp.int32, (segments, length), 0)
    energy = energy_ref[...]
    delayed = jnp.zeros((segments, length), F32)
    for s in range(segments):
        delayed = jnp.where(row == s, pltpu.roll(energy, offset_ref[s], axis=1), delayed)
    before = lax.broadcasted_iota(jnp.int32, (LANES, LANES), 0) < lax.broadcasted_iota(
        jnp.int32, (LANES, LANES), 1
    )
    before = before.astype(F32)
    carry = jnp.zeros((segments, 1), F32)
    blocks = length // LANES
    for j in range(blocks):
        piece = delayed[:, j * LANES : (j + 1) * LANES]
        prefix[:, j * LANES : (j + 1) * LANES] = carry + jnp.dot(
            piece, before, precision=lax.Precision.HIGHEST, preferred_element_type=F32
        )
        carry = carry + jnp.sum(piece, axis=1, keepdims=True)
    first = prefix[:, :length]
    prefix[:, length : 2 * length] = first + carry
    prefix[:, 2 * length :] = first[:, :LANES] + 2.0 * carry
    span = length + LANES
    for t in range(templates):
        lag = lag_ref[t]
        start = pl.multiple_of((lag // LANES) * LANES, LANES)
        ahead = pltpu.roll(prefix[:, pl.ds(start, span)], span - lag % LANES, axis=1)[:, :length]
        power = (ahead - first) / (channel_total * lag.astype(F32))
        out_ref[t] = scale * lax.rsqrt(level_ref[t] * power + epsilon)


def store_spectra(spectra, s, forward, summed, differed):
    near, channels = forward.shape[1] // 2, summed.shape[-1]
    for parity, record in enumerate((summed, differed)):
        first = parity * near
        result = jnp.dot(forward[parity], record[...], preferred_element_type=F32).astype(BF16)
        real, imag = result[:near], result[near:]
        spectra[0, s, first : first + near, :channels] = real
        spectra[0, s, first : first + near, channels:] = imag
        spectra[1, s, first : first + near, :channels] = imag
        spectra[1, s, first : first + near, channels:] = -real


def exchange_lanes(blocks):
    blocks = list(blocks)
    index = lax.broadcasted_iota(jnp.int32, blocks[0].shape, 1) // BLOCK
    for bit in (1, 2, 4):
        upper = (index & bit) != 0
        for i in range(8):
            if i & bit:
                continue
            first, second = blocks[i], blocks[i + bit]
            shift = BLOCK * bit
            blocks[i] = jnp.where(upper, pltpu.roll(second, shift, axis=1), first)
            blocks[i + bit] = jnp.where(upper, second, pltpu.roll(first, LANES - shift, axis=1))
    return blocks


def detect_kernel(channel_total, *refs):
    sources, refs = refs[:16], refs[16:]
    lag_ref, offset_ref, level_ref, place_ref, energy_ref = refs[:5]
    forward_hbm, tmpl_hbm, back_hbm, cos_ref, sin_ref, out_ref = refs[5:11]
    forward, tmpl, back, weights, prefix, summed, differed, spectra, diagonal, cross, sems = refs[11:]
    segments, piece, channels = sources[0].shape
    templates, _, length = weights.shape
    bins = length // 2
    lanes = templates * BLOCK
    group = summed.shape[0]
    tables_in = [
        pltpu.make_async_copy(source, target, sems.at[j])
        for j, (source, target) in enumerate(
            ((forward_hbm, forward), (back_hbm, back))
        )
    ]
    copy_tmpl = pltpu.make_async_copy(tmpl_hbm, tmpl, sems.at[2])
    for copy in (tables_in[0], copy_tmpl, tables_in[1]):
        copy.start()
    weight_kernel(channel_total, 1.0 / math.sqrt(segments), lag_ref, offset_ref, level_ref, energy_ref, weights, prefix)

    pairs = len(sources) // 2
    starts = [pl.multiple_of(place_ref[k], piece) for k in range(pairs)]
    signs = [place_ref[pairs + k].astype(F32).astype(BF16) for k in range(pairs)]
    tables_in[0].wait()

    @pl.loop(0, segments // group)
    def _(i):
        for u in range(group):
            s = i * group + u
            for k in range(pairs):
                first, second = sources[k][s], sources[pairs + k][s]
                summed[u, pl.ds(starts[k], piece), :] = first + second
                differed[u, pl.ds(starts[k], piece), :] = (first - second) * signs[k]
            store_spectra(spectra, s, forward, summed.at[u], differed.at[u])

    copy_tmpl.wait()
    rows = 2 * segments * BLOCK
    keep = (
        lax.broadcasted_iota(jnp.int32, (rows, lanes), 0) % BLOCK
        == lax.broadcasted_iota(jnp.int32, (rows, lanes), 1) % BLOCK
    )

    @pl.loop(0, bins // BLOCK // 4)
    def _(i):
        for u in range(4):
            b = i * 4 + u
            start = pl.multiple_of(b * BLOCK, BLOCK)
            left = spectra[:, :, pl.ds(start, BLOCK), :].reshape(rows, 2 * channels)
            right = tmpl[b].reshape(lanes, 2 * channels)
            product = lax.dot_general(
                left, right, (((1,), (1,)), ((), ())), preferred_element_type=F32
            )
            product = jnp.where(keep, product, 0.0).reshape(2 * segments, BLOCK, lanes)
            diagonal[b] = jnp.sum(product, axis=1)

    for g in range(bins // LANES):
        for j in range(lanes // LANES):
            blocks = [diagonal[g * 8 + i, :, j * LANES : (j + 1) * LANES] for i in range(8)]
            for i, block in enumerate(exchange_lanes(blocks)):
                cross[j * 8 + i, :, g * LANES : (g + 1) * LANES] = block

    real, imag = cross[:, :segments, :], cross[:, segments:, :]
    cosine, sine = cos_ref[...][None], sin_ref[...][None]
    total = templates * segments
    delayed = jnp.concatenate(
        [
            (real * cosine + imag * sine).reshape(total, bins),
            (imag * cosine - real * sine).reshape(total, bins),
        ],
        axis=1,
    )
    delayed_high = delayed.astype(BF16)
    delayed_low = (delayed - delayed_high.astype(F32)).astype(BF16)
    tables_in[1].wait()
    both = jnp.dot(
        jnp.concatenate([delayed_high, delayed_low], axis=0), back[...], preferred_element_type=F32
    )
    result = both[:total] + both[total:]
    scores = result.reshape(templates, segments, length) * weights[...]
    stack = jnp.sum(scores, axis=1)
    for j in range(length // LANES):
        out_ref[j] = stack[:, j * LANES : (j + 1) * LANES]


def detect(pieces, lag_lengths, offsets, level, place, energy, forward, tmpl, back, cosine, sine, channel_total):
    segments, piece, channels = pieces[0].shape
    templates, length = lag_lengths.shape[0], energy.shape[1]
    bins = length // 2
    vmem = pl.BlockSpec(memory_space=pltpu.VMEM)
    smem = pl.BlockSpec(memory_space=pltpu.SMEM)
    anywhere = pl.BlockSpec(memory_space=pl.ANY)
    group = 4

    def kernel(*refs):
        detect_kernel(channel_total, *refs)

    return pl.pallas_call(
        kernel,
        in_specs=[vmem] * len(pieces) + [smem] * 4 + [vmem] + [anywhere] * 3 + [vmem] * 2,
        out_specs=vmem,
        out_shape=jax.ShapeDtypeStruct((length // LANES, templates, LANES), F32),
        scratch_shapes=[
            pltpu.VMEM(forward.shape, BF16),
            pltpu.VMEM(tmpl.shape, BF16),
            pltpu.VMEM(back.shape, BF16),
            pltpu.VMEM((templates, segments, length), F32),
            pltpu.VMEM((segments, 2 * length + LANES), F32),
            pltpu.VMEM((group, bins, channels), BF16),
            pltpu.VMEM((group, bins, channels), BF16),
            pltpu.VMEM((2, segments, bins, 2 * channels), BF16),
            pltpu.VMEM((bins // BLOCK, 2 * segments, templates * BLOCK), F32),
            pltpu.VMEM((templates, 2 * segments, bins), F32),
            pltpu.SemaphoreType.DMA((3,)),
        ],
        compiler_params=pltpu.CompilerParams(vmem_limit_bytes=44 << 20),
        cost_estimate=pl.CostEstimate(flops=12_000_000_000, bytes_accessed=24 << 20, transcendentals=0),
        name="detect",
    )(*pieces, lag_lengths, offsets, level, place, energy, forward, tmpl, back, cosine, sine)


def send(value, axis, move):
    return lax.ppermute(value, axis, [(i, move(i)) for i in range(lax.axis_size(axis))])


def apart(i):
    return (i + (-4 if i % 2 else 4)) % 16


def across(i):
    return i ^ 2


def sibling(i):
    return i ^ 1


def after(value, *earlier):
    return lax.optimization_barrier((value, *earlier))[0]


def body(samples, template_spectra, lag_lengths, offsets):
    segments, channels, piece = samples.shape
    chan_groups = lax.axis_size("chan")
    tmpl_groups = lax.axis_size("tmpl")
    channel_total = channels * chan_groups
    length = piece * tmpl_groups
    bins = length // 2
    templates = template_spectra.shape[1]
    me = lax.axis_index("tmpl")

    wide = samples.astype(F32)
    energy = jnp.sum(wide * wide, axis=1)

    def double(energy, bit, flip=0):
        other = send(energy, "tmpl", lambda i: i ^ bit ^ flip)
        upper = (me & bit) != 0
        return jnp.concatenate(
            [jnp.where(upper, other, energy), jnp.where(upper, energy, other)], axis=1
        )

    fence = lax.optimization_barrier
    own = jnp.transpose(samples, (0, 2, 1))
    beside_0 = send(own, "tmpl", apart)
    own_c = send(own, "tmpl", sibling)
    beside_1 = send(own_c, "tmpl", apart)
    energy = double(after(double(energy, 1), own_c), 2)
    own_x = send(own, "tmpl", across)
    energy_early = energy
    energy = double(energy, 4)
    far = send(beside_0, "tmpl", apart)
    tmpl, level = prepare_templates(after(template_spectra, energy_early))
    far, own_x, beside_1, level, energy = fence((far, own_x, beside_1, level, energy))

    far_x = send(far, "tmpl", across)
    energy = double(energy, 8, 4)
    own_xc = send(own_x, "tmpl", sibling)
    beside_0c, beside_1c = send(beside_0, "tmpl", sibling), send(beside_1, "tmpl", sibling)
    far_c = send(far, "tmpl", sibling)
    own_x, own_xc, energy = fence((own_x, own_xc, energy))
    beside_x0, beside_x1 = send(own_x, "tmpl", apart), send(own_xc, "tmpl", apart)
    sums = jnp.concatenate([energy, level], axis=1)
    sums = sums + send(sums, "chan", lambda i: i ^ 1)
    sums = sums + send(sums, "chan", lambda i: i ^ 3)
    sums = sums + send(sums, "chan", lambda i: i ^ 4)
    energy, level = sums[:, :length], sums[:, length]
    beside_x0c, beside_x1c = send(beside_x0, "tmpl", sibling), send(beside_x1, "tmpl", sibling)
    far_xc = send(far_x, "tmpl", sibling)

    order = bin_order(bins).astype(np.int32)
    phase = offsets[:, None] * order[None, :] % length
    angle = phase.astype(F32) * (2.0 * math.pi / length)
    cosine, sine = jnp.cos(angle), jnp.sin(angle)
    forward, back = tables(length)

    k = lax.iota(jnp.int32, 8)
    z = (me // 4 + jnp.where(k < 4, 0, 2 * (me % 2) - 1)) % 4
    start = (z % 2 * 4 + ((me ^ k) & 3)) * piece
    place = jnp.concatenate([start, jnp.where(z < 2, 1, -1)]).astype(jnp.int32)
    pieces = (
        own, own_c, own_x, own_xc, beside_0, beside_1, beside_x0, beside_x1,
        far, far_c, far_x, far_xc, beside_1c, beside_0c, beside_x1c, beside_x0c,
    )
    partial = detect(
        pieces, lag_lengths, offsets, level, place, energy, forward, tmpl, back, cosine, sine, channel_total
    )
    return jnp.sum(lax.all_to_all(partial, "chan", 0, 0, tiled=False), axis=0)


def solution(mesh):
    return jax.shard_map(
        body,
        mesh=mesh,
        in_specs=(P(None, "chan", "tmpl"), P(None, "tmpl", "chan", None), P("tmpl"), P()),
        out_specs=P("tmpl", "chan"),
        check_vma=False,
    )
```

time: 92.6 us -> 85.4 us (0.922)
  Pallas kernels: 31.4 us -> 26.1 us
  other arithmetic: 5.17 us -> 2.35 us
  starting transfers between devices: 18.7 us -> 20 us
  local copies, waits for them, and re-layouts: 3.2 us -> 2.07 us
    pallas_call x3 -> x1, Pallas kernels: 23.1 us -> 17.8 us  [detect(): pl.pallas_call(kernel, in_specs=[vmem] * len(pieces) + [smem] * 4 + [vmem...]
    concatenate x3 -> x0, other arithmetic: 1.43 us -> none  [the longest x1 1.32 us: body(): beside = send(jnp.concatenate([own, own_c], axis=0), 'tmpl', apart)]
    ppermute x18 -> x22, starting transfers between devices: 18.7 us -> 20 us  [send(): lax.ppermute(value, axis, [(i, move(i)) for i in range(lax.axis_size(axis...]
    slice x1 -> x0, local copies, waits for them, and re-layouts: 1.08 us -> none  [body(): far = send(beside[:segments], 'tmpl', apart)]
    unnamed x22 -> x11, local copies, waits for them, and re-layouts: 1.93 us -> 1.25 us
    ppermute x18 -> x22, waiting for transfers between devices: 19.2 us -> 19.4 us  [send(): lax.ppermute(value, axis, [(i, move(i)) for i in range(lax.axis_size(axis...]
  transfers between devices with their start and end apart: 18 -> 22, of which waited for: 10 -> 11; matrix products, arithmetic and copies ran while one was open for 6% -> 3% of each run, Pallas kernels for 11% -> 10%
where the time goes in v4:
time: 85.4 us; the launch traced here: 84.5 us
  Pallas kernels  26.1 us (31%)
  starting transfers between devices  20 us (23%)
  waiting for transfers between devices  19.4 us (23%)
  blocking collectives  14.4 us (17%)
  other arithmetic  2.35 us (3%)
  local copies, waits for them, and re-layouts  2.07 us (2%)
    ppermute x22, starting transfers between devices, send(): lax.ppermute(value, axis, [(i, move(i)) for i in range(lax.axis_size(axis...  20 us
    ppermute x22, waiting for transfers between devices, send(): lax.ppermute(value, axis, [(i, move(i)) for i in range(lax.axis_size(axis...  19.4 us
    pallas_call x1, Pallas kernels, detect(): pl.pallas_call(kernel, in_specs=[vmem] * len(pieces) + [smem] * 4 + [vmem...  17.8 us
    all_to_all x1, blocking collectives, body(): return jnp.sum(lax.all_to_all(partial, 'chan', 0, 0, tiled=False), axis=0)  14.4 us
    pallas_call x1, Pallas kernels, prepare_templates(): pl.pallas_call(template_kernel, grid=(templates // step,), in_specs=[pl.B...  8.3 us
  transfers between devices with their start and end apart: 22, of which 11 were waited for; matrix products, arithmetic and copies ran while one was open for 3% of the time, Pallas kernels for 10%

profile of v4, /device:TPU:0, one launch (start us, length us, event | category | flops | bytes accessed | tf_op | source)
XLA Modules:
  0.0 84.5 jit_solution(13224944142723910633)
XLA Ops:
  0.1 2.1 %collective-permute-start.1 = (bf16[16,64,256]{2,1,0:T(8,128)(2,1)}, bf16[16,64,256]{2,1,0:T(8,128)(2,1)S(1)}, u32[]{:S(2)}, u32[]{:S(2)}) collective-permute-start(bf16[16,64,256]{2,1,0:T(8,128)(2,1)} %bitcast.2), channel_id=1, source_target_pairs={{0,4},{1,13},{2,6},{3,15},{4,8},{5,1},{6,10},{7,3},{8,12},{9,5},{1... | collective-permute-start | bytes 1572872 | tf_op jit(solution)/shard_map/ppermute | solution.py:266
  2.2 1.3 %multiply_reduce_fusion = f32[16,64]{1,0:T(8,128)S(1)} fusion(bf16[16,256,64]{1,2,0:T(8,128)(2,1)} %param.8), kind=kLoop, calls=%fused_computation | loop fusion | flops 785408 | bytes 528384 | tf_op jit(solution)/shard_map/reduce_sum | solution.py:296
  3.5 2.3 %collective-permute-start.5 = (f32[16,64]{1,0:T(8,128)S(1)}, f32[16,64]{1,0:T(8,128)S(1)}, u32[]{:S(2)}, u32[]{:S(2)}) collective-permute-start(f32[16,64]{1,0:T(8,128)S(1)} %multiply_reduce_fusion), channel_id=1, source_target_pairs={{0,1},{1,0},{2,3},{3,2},{4,5},{5,4},{6,7},{7,6},{8,9},{9,8},{10,11... | collective-permute-start | bytes 12296 | tf_op jit(solution)/shard_map/ppermute | solution.py:266
  5.8 0.8 collective-permute-done.5
  6.7 1.5 %collective-permute-start.6 = (f32[16,128]{1,0:T(8,128)S(1)}, f32[16,128]{1,0:T(8,128)S(1)}, u32[]{:S(2)}, u32[]{:S(2)}) collective-permute-start(f32[16,128]{1,0:T(8,128)S(1)} %pad_maximum_fusion.3), channel_id=1, source_target_pairs={{0,2},{1,3},{2,0},{3,1},{4,6},{5,7},{6,4},{7,5},{8,10},{9,11},{10,... | collective-permute-start | bytes 24584 | tf_op jit(solution)/shard_map/ppermute | solution.py:266
  8.8 2.9 %collective-permute-done.1.refs_4_ = bf16[16,64,256]{2,1,0:T(8,128)(2,1)S(1)} collective-permute-done((bf16[16,64,256]{2,1,0:T(8,128)(2,1)}, bf16[16,64,256]{2,1,0:T(8,128)(2,1)S(1)}, u32[]{:S(2)}, u32[]{:S(2)}) %collective-permute-start.1) | collective-permute-done | bytes 524320 | tf_op jit(solution)/shard_map/ppermute | solution.py:266
  11.7 1.9 %collective-permute-start.7 = (f32[16,256]{1,0:T(8,128)S(1)}, f32[16,256]{1,0:T(8,128)S(1)}, u32[]{:S(2)}, u32[]{:S(2)}) collective-permute-start(f32[16,256]{1,0:T(8,128)S(1)} %pad_maximum_fusion.2), channel_id=1, source_target_pairs={{0,4},{1,5},{2,6},{3,7},{4,0},{5,1},{6,2},{7,3},{8,12},{9,13},{10,... | collective-permute-start | bytes 49160 | tf_op jit(solution)/shard_map/ppermute | solution.py:266
  13.6 8.3 %template_flip.1 = (bf16[32,16,16,512]{3,2,1,0:T(8,128)(2,1)}, f32[16,128]{1,0:T(8,128)}) custom-call(bf16[256,256]{1,0:T(8,128)(2,1)} %constant.84.clone.turn_ref, bf16[2,16,256,512]{3,2,1,0:T(8,128)(2,1)} %g_ref), custom_call_target="tpu_custom_call" | custom-call | flops 2200000000 | bytes 16777216 | tf_op jit(solution)/shard_map/template_flip/pallas_call | solution.py:64
  22.3 2.4 %collective-permute-done.2.refs_8_ = bf16[16,64,256]{2,1,0:T(8,128)(2,1)S(1)} collective-permute-done((bf16[16,64,256]{2,1,0:T(8,128)(2,1)S(1)}, bf16[16,64,256]{2,1,0:T(8,128)(2,1)S(1)}, u32[]{:S(2)}, u32[]{:S(2)}) %collective-permute-start.2) | collective-permute-done | bytes 524320 | tf_op jit(solution)/shard_map/ppermute | solution.py:266
  24.8 0.7 collective-permute-start.9
  25.7 1.5 %collective-permute-start.13 = (bf16[16,64,256]{2,1,0:T(8,128)(2,1)S(1)}, bf16[16,64,256]{2,1,0:T(8,128)(2,1)}, u32[]{:S(2)}, u32[]{:S(2)}) collective-permute-start(bf16[16,64,256]{2,1,0:T(8,128)(2,1)S(1)} %collective-permute-done.2.refs_8_), channel_id=1, source_target_pairs={{0,2},{1,3},{2,0},{3,1},{4,6},{5,7},{6,4},{7,5},{8,10},{9,11},{10,... | collective-permute-start | bytes 1572872 | tf_op jit(solution)/shard_map/ppermute | solution.py:266
  27.2 2.8 %collective-permute-done.9 = f32[16,512]{1,0:T(8,128)S(1)} collective-permute-done((f32[16,512]{1,0:T(8,128)S(1)}, f32[16,512]{1,0:T(8,128)S(1)}, u32[]{:S(2)}, u32[]{:S(2)}) %collective-permute-start.9) | collective-permute-done | bytes 32800 | tf_op jit(solution)/shard_map/ppermute | solution.py:266
  30.8 1.6 %collective-permute-start.19 = (f32[16,1152]{1,0:T(8,128)S(1)}, f32[16,1152]{1,0:T(8,128)S(1)}, u32[]{:S(2)}, u32[]{:S(2)}) collective-permute-start(f32[16,1152]{1,0:T(8,128)S(1)} %constant_dynamic-update-slice_fusion), channel_id=1, source_target_pairs={{0,16},{16,0},{32,48},{48,32},{64,80},{80,64},{96,112},{112,96},{1... | collective-permute-start | bytes 221192 | tf_op jit(solution)/shard_map/ppermute | solution.py:266
  32.4 2.8 %collective-permute-done.19 = f32[16,1152]{1,0:T(8,128)S(1)} collective-permute-done((f32[16,1152]{1,0:T(8,128)S(1)}, f32[16,1152]{1,0:T(8,128)S(1)}, u32[]{:S(2)}, u32[]{:S(2)}) %collective-permute-start.19) | collective-permute-done | bytes 73760 | tf_op jit(solution)/shard_map/ppermute | solution.py:266
  35.2 3.1 %collective-permute-start.20 = (f32[16,1152]{1,0:T(8,128)S(1)}, f32[16,1152]{1,0:T(8,128)S(1)}, u32[]{:S(2)}, u32[]{:S(2)}) collective-permute-start(f32[16,1152]{1,0:T(8,128)S(1)} %add.40), channel_id=1, source_target_pairs={{0,48},{16,32},{32,16},{48,0},{64,112},{80,96},{96,80},{112,64},{1... | collective-permute-start | bytes 221192 | tf_op jit(solution)/shard_map/ppermute | solution.py:266
  38.3 2.5 %collective-permute-done.20 = f32[16,1152]{1,0:T(8,128)S(1)} collective-permute-done((f32[16,1152]{1,0:T(8,128)S(1)}, f32[16,1152]{1,0:T(8,128)S(1)}, u32[]{:S(2)}, u32[]{:S(2)}) %collective-permute-start.20) | collective-permute-done | bytes 73760 | tf_op jit(solution)/shard_map/ppermute | solution.py:266
  40.9 3.1 %collective-permute-start.21 = (f32[16,1152]{1,0:T(8,128)S(1)}, f32[16,1152]{1,0:T(8,128)S(1)}, u32[]{:S(2)}, u32[]{:S(2)}) collective-permute-start(f32[16,1152]{1,0:T(8,128)S(1)} %add.41), channel_id=1, source_target_pairs={{0,64},{16,80},{32,96},{48,112},{64,0},{80,16},{96,32},{112,48},{1... | collective-permute-start | bytes 221192 | tf_op jit(solution)/shard_map/ppermute | solution.py:266
  44.5 2.3 %collective-permute-done.21 = f32[16,1152]{1,0:T(8,128)S(1)} collective-permute-done((f32[16,1152]{1,0:T(8,128)S(1)}, f32[16,1152]{1,0:T(8,128)S(1)}, u32[]{:S(2)}, u32[]{:S(2)}) %collective-permute-start.21) | collective-permute-done | bytes 73760 | tf_op jit(solution)/shard_map/ppermute | solution.py:266
  48.1 0.9 %collective-permute-done.14.refs_11_ = bf16[16,64,256]{2,1,0:T(8,128)(2,1)S(1)} collective-permute-done((bf16[16,64,256]{2,1,0:T(8,128)(2,1)}, bf16[16,64,256]{2,1,0:T(8,128)(2,1)S(1)}, u32[]{:S(2)}, u32[]{:S(2)}) %collective-permute-start.14) | collective-permute-done | bytes 524320 | tf_op jit(solution)/shard_map/ppermute | solution.py:266
  48.9 0.7 collective-permute-done.18.refs_15_
  49.7 0.7 collective-permute-done.17.refs_14_
  50.4 1.2 %copy-done.3 = bf16[2,512,512]{2,1,0:T(8,128)(2,1)S(1)} copy-done((bf16[2,512,512]{2,1,0:T(8,128)(2,1)S(1)}, bf16[2,512,512]{2,1,0:T(8,128)(2,1)}, u32[]{:S(2)}) %copy-start.3) | copy-done | bytes 1048600
  51.7 17.8 %detect.1 = f32[8,16,128]{2,1,0:T(8,128)S(1)} custom-call(bf16[16,64,256]{2,1,0:T(8,128)(2,1)S(1)} %bitcast.4, bf16[16,64,256]{2,1,0:T(8,128)(2,1)S(1)} %collective-permute-done.refs_1_, bf16[16,64,256]{2,1,0:T(8,128)(2,1)S(1)} %collective-permute-done.3.refs_2_, bf16[16,64,256]{2,1,0:T(8,128)(2,1)} %collective-permute-done.8.refs_3_, ...), custom_call_target="tpu_custom_call" | custom-call | flops 12000000000 | bytes 25165824 | tf_op jit(solution)/shard_map/detect/pallas_call | solution.py:241
  69.5 14.4 %all_to_all.5 = f32[8,16,128]{2,1,0:T(8,128)S(1)} all-to-all(f32[8,16,128]{2,1,0:T(8,128)S(1)} %detect.1), channel_id=1, replica_groups=mesh['chan'=8,'tmpl'=16] {'chan'}, dimensions={0} | all-to-all | bytes 131072 | tf_op jit(solution)/shard_map/all_to_all | solution.py:350
  (53 shorter events, 4.6 us)
Async XLA Ops:
  0.0 50.4 %copy-start = (bf16[16,256,64]{1,2,0:T(8,128)(2,1)S(1)}, bf16[16,256,64]{1,2,0:T(8,128)(2,1)}, u32[]{:S(2)}) copy-start(bf16[16,256,64]{1,2,0:T(8,128)(2,1)} %param.8) | copy-start | bytes 1572868
  0.0 50.4 %copy-start.2 = (s32[16]{0:T(128)S(1)}, s32[16]{0:T(128)}, u32[]{:S(2)}) copy-start(s32[16]{0:T(128)} %refs_16_.1) | copy-start | bytes 196
  0.0 6.7 %collective-permute-start = (bf16[16,64,256]{2,1,0:T(8,128)(2,1)}, bf16[16,64,256]{2,1,0:T(8,128)(2,1)S(1)}, u32[]{:S(2)}, u32[]{:S(2)}) collective-permute-start(bf16[16,64,256]{2,1,0:T(8,128)(2,1)} %bitcast.1), channel_id=1, source_target_pairs={{0,1},{1,0},{2,3},{3,2},{4,5},{5,4},{6,7},{7,6},{8,9},{9,8},{10,11... | collective-permute-start | bytes 1572872 | tf_op jit(solution)/shard_map/ppermute | solution.py:266
  0.1 11.6 %collective-permute-start.1 = (bf16[16,64,256]{2,1,0:T(8,128)(2,1)}, bf16[16,64,256]{2,1,0:T(8,128)(2,1)S(1)}, u32[]{:S(2)}, u32[]{:S(2)}) collective-permute-start(bf16[16,64,256]{2,1,0:T(8,128)(2,1)} %bitcast.2), channel_id=1, source_target_pairs={{0,4},{1,13},{2,6},{3,15},{4,8},{5,1},{6,10},{7,3},{8,12},{9,5},{1... | collective-permute-start | bytes 1572872 | tf_op jit(solution)/shard_map/ppermute | solution.py:266
  3.5 3.2 %collective-permute-start.5 = (f32[16,64]{1,0:T(8,128)S(1)}, f32[16,64]{1,0:T(8,128)S(1)}, u32[]{:S(2)}, u32[]{:S(2)}) collective-permute-start(f32[16,64]{1,0:T(8,128)S(1)} %multiply_reduce_fusion), channel_id=1, source_target_pairs={{0,1},{1,0},{2,3},{3,2},{4,5},{5,4},{6,7},{7,6},{8,9},{9,8},{10,11... | collective-permute-start | bytes 12296 | tf_op jit(solution)/shard_map/ppermute | solution.py:266
  6.7 5.0 %collective-permute-start.6 = (f32[16,128]{1,0:T(8,128)S(1)}, f32[16,128]{1,0:T(8,128)S(1)}, u32[]{:S(2)}, u32[]{:S(2)}) collective-permute-start(f32[16,128]{1,0:T(8,128)S(1)} %pad_maximum_fusion.3), channel_id=1, source_target_pairs={{0,2},{1,3},{2,0},{3,1},{4,6},{5,7},{6,4},{7,5},{8,10},{9,11},{10,... | collective-permute-start | bytes 24584 | tf_op jit(solution)/shard_map/ppermute | solution.py:266
  8.2 14.1 %collective-permute-start.3 = (bf16[16,64,256]{2,1,0:T(8,128)(2,1)}, bf16[16,64,256]{2,1,0:T(8,128)(2,1)S(1)}, u32[]{:S(2)}, u32[]{:S(2)}) collective-permute-start(bf16[16,64,256]{2,1,0:T(8,128)(2,1)} %bitcast.3), channel_id=1, source_target_pairs={{0,2},{1,3},{2,0},{3,1},{4,6},{5,7},{6,4},{7,5},{8,10},{9,11},{10,... | collective-permute-start | bytes 1572872 | tf_op jit(solution)/shard_map/ppermute | solution.py:266
  8.8 16.0 %collective-permute-start.4 = (bf16[16,64,256]{2,1,0:T(8,128)(2,1)S(1)}, bf16[16,64,256]{2,1,0:T(8,128)(2,1)S(1)}, u32[]{:S(2)}, u32[]{:S(2)}) collective-permute-start(bf16[16,64,256]{2,1,0:T(8,128)(2,1)S(1)} %collective-permute-done.refs_1_), channel_id=1, source_target_pairs={{0,4},{1,13},{2,6},{3,15},{4,8},{5,1},{6,10},{7,3},{8,12},{9,5},{1... | collective-permute-start | bytes 1572872 | tf_op jit(solution)/shard_map/ppermute | solution.py:266
  11.7 13.1 %collective-permute-start.2 = (bf16[16,64,256]{2,1,0:T(8,128)(2,1)S(1)}, bf16[16,64,256]{2,1,0:T(8,128)(2,1)S(1)}, u32[]{:S(2)}, u32[]{:S(2)}) collective-permute-start(bf16[16,64,256]{2,1,0:T(8,128)(2,1)S(1)} %collective-permute-done.1.refs_4_), channel_id=1, source_target_pairs={{0,4},{1,13},{2,6},{3,15},{4,8},{5,1},{6,10},{7,3},{8,12},{9,5},{1... | collective-permute-start | bytes 1572872 | tf_op jit(solution)/shard_map/ppermute | solution.py:266
  11.7 10.2 %collective-permute-start.7 = (f32[16,256]{1,0:T(8,128)S(1)}, f32[16,256]{1,0:T(8,128)S(1)}, u32[]{:S(2)}, u32[]{:S(2)}) collective-permute-start(f32[16,256]{1,0:T(8,128)S(1)} %pad_maximum_fusion.2), channel_id=1, source_target_pairs={{0,4},{1,5},{2,6},{3,7},{4,0},{5,1},{6,2},{7,3},{8,12},{9,13},{10,... | collective-permute-start | bytes 49160 | tf_op jit(solution)/shard_map/ppermute | solution.py:266
  24.8 5.2 %collective-permute-start.8 = (bf16[16,64,256]{2,1,0:T(8,128)(2,1)S(1)}, bf16[16,64,256]{2,1,0:T(8,128)(2,1)}, u32[]{:S(2)}, u32[]{:S(2)}) collective-permute-start(bf16[16,64,256]{2,1,0:T(8,128)(2,1)S(1)} %collective-permute-done.3.refs_2_), channel_id=1, source_target_pairs={{0,1},{1,0},{2,3},{3,2},{4,5},{5,4},{6,7},{7,6},{8,9},{9,8},{10,11... | collective-permute-start | bytes 1572872 | tf_op jit(solution)/shard_map/ppermute | solution.py:266
  24.8 5.1 %collective-permute-start.9 = (f32[16,512]{1,0:T(8,128)S(1)}, f32[16,512]{1,0:T(8,128)S(1)}, u32[]{:S(2)}, u32[]{:S(2)}) collective-permute-start(f32[16,512]{1,0:T(8,128)S(1)} %pad_maximum_fusion.1), channel_id=1, source_target_pairs={{0,12},{1,13},{2,14},{3,15},{4,8},{5,9},{6,10},{7,11},{8,4},{9,5},... | collective-permute-start | bytes 98312 | tf_op jit(solution)/shard_map/ppermute | solution.py:266
  25.5 18.5 %collective-permute-start.16 = (bf16[16,64,256]{2,1,0:T(8,128)(2,1)S(1)}, bf16[16,64,256]{2,1,0:T(8,128)(2,1)}, u32[]{:S(2)}, u32[]{:S(2)}) collective-permute-start(bf16[16,64,256]{2,1,0:T(8,128)(2,1)S(1)} %collective-permute-done.1.refs_4_), channel_id=1, source_target_pairs={{0,1},{1,0},{2,3},{3,2},{4,5},{5,4},{6,7},{7,6},{8,9},{9,8},{10,11... | collective-permute-start | bytes 1572872 | tf_op jit(solution)/shard_map/ppermute | solution.py:266
  25.7 18.3 %collective-permute-start.13 = (bf16[16,64,256]{2,1,0:T(8,128)(2,1)S(1)}, bf16[16,64,256]{2,1,0:T(8,128)(2,1)}, u32[]{:S(2)}, u32[]{:S(2)}) collective-permute-start(bf16[16,64,256]{2,1,0:T(8,128)(2,1)S(1)} %collective-permute-done.2.refs_8_), channel_id=1, source_target_pairs={{0,2},{1,3},{2,0},{3,1},{4,6},{5,7},{6,4},{7,5},{8,10},{9,11},{10,... | collective-permute-start | bytes 1572872 | tf_op jit(solution)/shard_map/ppermute | solution.py:266
  30.0 16.9 %collective-permute-start.10 = (bf16[16,64,256]{2,1,0:T(8,128)(2,1)S(1)}, bf16[16,64,256]{2,1,0:T(8,128)(2,1)}, u32[]{:S(2)}, u32[]{:S(2)}) collective-permute-start(bf16[16,64,256]{2,1,0:T(8,128)(2,1)S(1)} %collective-permute-done.3.refs_2_), channel_id=1, source_target_pairs={{0,4},{1,13},{2,6},{3,15},{4,8},{5,1},{6,10},{7,3},{8,12},{9,5},{1... | collective-permute-start | bytes 1572872 | tf_op jit(solution)/shard_map/ppermute | solution.py:266
  30.0 17.3 %collective-permute-start.11 = (bf16[16,64,256]{2,1,0:T(8,128)(2,1)}, bf16[16,64,256]{2,1,0:T(8,128)(2,1)}, u32[]{:S(2)}, u32[]{:S(2)}) collective-permute-start(bf16[16,64,256]{2,1,0:T(8,128)(2,1)} %collective-permute-done.8.refs_3_), channel_id=1, source_target_pairs={{0,4},{1,13},{2,6},{3,15},{4,8},{5,1},{6,10},{7,3},{8,12},{9,5},{1... | collective-permute-start | bytes 1572872 | tf_op jit(solution)/shard_map/ppermute | solution.py:266
  30.8 4.4 %collective-permute-start.19 = (f32[16,1152]{1,0:T(8,128)S(1)}, f32[16,1152]{1,0:T(8,128)S(1)}, u32[]{:S(2)}, u32[]{:S(2)}) collective-permute-start(f32[16,1152]{1,0:T(8,128)S(1)} %constant_dynamic-update-slice_fusion), channel_id=1, source_target_pairs={{0,16},{16,0},{32,48},{48,32},{64,80},{80,64},{96,112},{112,96},{1... | collective-permute-start | bytes 221192 | tf_op jit(solution)/shard_map/ppermute | solution.py:266
  35.2 5.6 %collective-permute-start.20 = (f32[16,1152]{1,0:T(8,128)S(1)}, f32[16,1152]{1,0:T(8,128)S(1)}, u32[]{:S(2)}, u32[]{:S(2)}) collective-permute-start(f32[16,1152]{1,0:T(8,128)S(1)} %add.40), channel_id=1, source_target_pairs={{0,48},{16,32},{32,16},{48,0},{64,112},{80,96},{96,80},{112,64},{1... | collective-permute-start | bytes 221192 | tf_op jit(solution)/shard_map/ppermute | solution.py:266
  40.9 5.9 %collective-permute-start.21 = (f32[16,1152]{1,0:T(8,128)S(1)}, f32[16,1152]{1,0:T(8,128)S(1)}, u32[]{:S(2)}, u32[]{:S(2)}) collective-permute-start(f32[16,1152]{1,0:T(8,128)S(1)} %add.41), channel_id=1, source_target_pairs={{0,64},{16,80},{32,96},{48,112},{64,0},{80,16},{96,32},{112,48},{1... | collective-permute-start | bytes 221192 | tf_op jit(solution)/shard_map/ppermute | solution.py:266
  44.0 4.1 %collective-permute-start.12 = (bf16[16,64,256]{2,1,0:T(8,128)(2,1)S(1)}, bf16[16,64,256]{2,1,0:T(8,128)(2,1)S(1)}, u32[]{:S(2)}, u32[]{:S(2)}) collective-permute-start(bf16[16,64,256]{2,1,0:T(8,128)(2,1)S(1)} %collective-permute-done.2.refs_8_), channel_id=1, source_target_pairs={{0,1},{1,0},{2,3},{3,2},{4,5},{5,4},{6,7},{7,6},{8,9},{9,8},{10,11... | collective-permute-start | bytes 1572872 | tf_op jit(solution)/shard_map/ppermute | solution.py:266
  44.0 4.1 %collective-permute-start.15 = (bf16[16,64,256]{2,1,0:T(8,128)(2,1)S(1)}, bf16[16,64,256]{2,1,0:T(8,128)(2,1)S(1)}, u32[]{:S(2)}, u32[]{:S(2)}) collective-permute-start(bf16[16,64,256]{2,1,0:T(8,128)(2,1)S(1)} %collective-permute-done.4.refs_5_), channel_id=1, source_target_pairs={{0,1},{1,0},{2,3},{3,2},{4,5},{5,4},{6,7},{7,6},{8,9},{9,8},{10,11... | collective-permute-start | bytes 1572872 | tf_op jit(solution)/shard_map/ppermute | solution.py:266
  46.8 2.1 %collective-permute-start.14 = (bf16[16,64,256]{2,1,0:T(8,128)(2,1)}, bf16[16,64,256]{2,1,0:T(8,128)(2,1)S(1)}, u32[]{:S(2)}, u32[]{:S(2)}) collective-permute-start(bf16[16,64,256]{2,1,0:T(8,128)(2,1)} %collective-permute-done.13.refs_10_), channel_id=1, source_target_pairs={{0,1},{1,0},{2,3},{3,2},{4,5},{5,4},{6,7},{7,6},{8,9},{9,8},{10,11... | collective-permute-start | bytes 1572872 | tf_op jit(solution)/shard_map/ppermute | solution.py:266
  46.8 2.9 %collective-permute-start.18 = (bf16[16,64,256]{2,1,0:T(8,128)(2,1)}, bf16[16,64,256]{2,1,0:T(8,128)(2,1)S(1)}, u32[]{:S(2)}, u32[]{:S(2)}) collective-permute-start(bf16[16,64,256]{2,1,0:T(8,128)(2,1)} %collective-permute-done.10.refs_6_), channel_id=1, source_target_pairs={{0,1},{1,0},{2,3},{3,2},{4,5},{5,4},{6,7},{7,6},{8,9},{9,8},{10,11... | collective-permute-start | bytes 1572872 | tf_op jit(solution)/shard_map/ppermute | solution.py:266
  47.3 3.1 %collective-permute-start.17 = (bf16[16,64,256]{2,1,0:T(8,128)(2,1)}, bf16[16,64,256]{2,1,0:T(8,128)(2,1)S(1)}, u32[]{:S(2)}, u32[]{:S(2)}) collective-permute-start(bf16[16,64,256]{2,1,0:T(8,128)(2,1)} %collective-permute-done.11.refs_7_), channel_id=1, source_target_pairs={{0,1},{1,0},{2,3},{3,2},{4,5},{5,4},{6,7},{7,6},{8,9},{9,8},{10,11... | collective-permute-start | bytes 1572872 | tf_op jit(solution)/shard_map/ppermute | solution.py:266
  (3 other events, 96.6 us)

commit v5 on v4

--- a/solution.py
+++ b/solution.py
@@ -184,10 +184,10 @@
         == lax.broadcasted_iota(jnp.int32, (rows, lanes), 1) % BLOCK
     )
 
-    @pl.loop(0, bins // BLOCK // 4)
+    @pl.loop(0, bins // BLOCK // 16)
     def _(i):
-        for u in range(4):
-            b = i * 4 + u
+        for u in range(16):
+            b = i * 16 + u
             start = pl.multiple_of(b * BLOCK, BLOCK)
             left = spectra[:, :, pl.ds(start, BLOCK), :].reshape(rows, 2 * channels)
             right = tmpl[b].reshape(lanes, 2 * channels)
@@ -233,7 +233,7 @@
     vmem = pl.BlockSpec(memory_space=pltpu.VMEM)
     smem = pl.BlockSpec(memory_space=pltpu.SMEM)
     anywhere = pl.BlockSpec(memory_space=pl.ANY)
-    group = 4
+    group = 8
 
     def kernel(*refs):
         detect_kernel(channel_total, *refs)
@@ -313,7 +313,7 @@
     energy = double(energy, 4)
     far = send(beside_0, "tmpl", apart)
     tmpl, level = prepare_templates(after(template_spectra, energy_early))
-    far, own_x, beside_1, level, energy = fence((far, own_x, beside_1, level, energy))
+    own_x, beside_1, level, energy = fence((own_x, beside_1, level, energy))
 
     far_x = send(far, "tmpl", across)
     energy = double(energy, 8, 4)

time: 85.4 us -> 83.1 us (0.973)
  waiting for transfers between devices: 19.4 us -> 15.8 us
  starting transfers between devices: 20 us -> 23.1 us
  Pallas kernels: 26.1 us -> 24.4 us
    ppermute x22, waiting for transfers between devices: 19.4 us -> 15.8 us  [send(): lax.ppermute(value, axis, [(i, move(i)) for i in range(lax.axis_size(axis...]
    ppermute x22, starting transfers between devices: 20 us -> 23.1 us  [send(): lax.ppermute(value, axis, [(i, move(i)) for i in range(lax.axis_size(axis...]
    pallas_call x1, Pallas kernels: 17.8 us -> 16.1 us  [detect(): pl.pallas_call(kernel, in_specs=[vmem] * len(pieces) + [smem] * 4 + [vmem...]
  transfers between devices with their start and end apart: 22 -> 22, of which waited for: 11 -> 10; matrix products, arithmetic and copies ran while one was open for 3% -> 3% of each run, Pallas kernels for 10% -> 10%
where the time goes in v5:
time: 83.1 us; the launch traced here: 82.2 us
  Pallas kernels  24.4 us (29%)
  starting transfers between devices  23.1 us (28%)
  waiting for transfers between devices  15.8 us (19%)
  blocking collectives  14.4 us (17%)
  other arithmetic  2.35 us (3%)
  local copies, waits for them, and re-layouts  2.06 us (2%)
    ppermute x22, starting transfers between devices, send(): lax.ppermute(value, axis, [(i, move(i)) for i in range(lax.axis_size(axis...  23.1 us
    pallas_call x1, Pallas kernels, detect(): pl.pallas_call(kernel, in_specs=[vmem] * len(pieces) + [smem] * 4 + [vmem...  16.1 us
    ppermute x22, waiting for transfers between devices, send(): lax.ppermute(value, axis, [(i, move(i)) for i in range(lax.axis_size(axis...  15.8 us
    all_to_all x1, blocking collectives, body(): return jnp.sum(lax.all_to_all(partial, 'chan', 0, 0, tiled=False), axis=0)  14.4 us
    pallas_call x1, Pallas kernels, prepare_templates(): pl.pallas_call(template_kernel, grid=(templates // step,), in_specs=[pl.B...  8.3 us
  transfers between devices with their start and end apart: 22, of which 10 were waited for; matrix products, arithmetic and copies ran while one was open for 3% of the time, Pallas kernels for 10%

profile of v5, /device:TPU:0, one launch (start us, length us, event | category | flops | bytes accessed | tf_op | source)
XLA Modules:
  0.0 82.2 jit_solution(9662799205720046834)
XLA Ops:
  0.1 2.1 %collective-permute-start.8 = (bf16[16,64,256]{2,1,0:T(8,128)(2,1)}, bf16[16,64,256]{2,1,0:T(8,128)(2,1)S(1)}, u32[]{:S(2)}, u32[]{:S(2)}) collective-permute-start(bf16[16,64,256]{2,1,0:T(8,128)(2,1)} %bitcast.2), channel_id=1, source_target_pairs={{0,4},{1,13},{2,6},{3,15},{4,8},{5,1},{6,10},{7,3},{8,12},{9,5},{1... | collective-permute-start | bytes 1572872 | tf_op jit(solution)/shard_map/ppermute | solution.py:266
  2.2 1.3 %multiply_reduce_fusion = f32[16,64]{1,0:T(8,128)S(1)} fusion(bf16[16,256,64]{1,2,0:T(8,128)(2,1)} %param.8), kind=kLoop, calls=%fused_computation | loop fusion | flops 785408 | bytes 528384 | tf_op jit(solution)/shard_map/reduce_sum | solution.py:296
  3.5 2.3 %collective-permute-start.3 = (f32[16,64]{1,0:T(8,128)S(1)}, f32[16,64]{1,0:T(8,128)S(1)}, u32[]{:S(2)}, u32[]{:S(2)}) collective-permute-start(f32[16,64]{1,0:T(8,128)S(1)} %multiply_reduce_fusion), channel_id=1, source_target_pairs={{0,1},{1,0},{2,3},{3,2},{4,5},{5,4},{6,7},{7,6},{8,9},{9,8},{10,11... | collective-permute-start | bytes 12296 | tf_op jit(solution)/shard_map/ppermute | solution.py:266
  5.8 0.8 %collective-permute-done.3 = f32[16,64]{1,0:T(8,128)S(1)} collective-permute-done((f32[16,64]{1,0:T(8,128)S(1)}, f32[16,64]{1,0:T(8,128)S(1)}, u32[]{:S(2)}, u32[]{:S(2)}) %collective-permute-start.3) | collective-permute-done | bytes 4128 | tf_op jit(solution)/shard_map/ppermute | solution.py:266
  6.7 1.5 %collective-permute-start.4 = (f32[16,128]{1,0:T(8,128)S(1)}, f32[16,128]{1,0:T(8,128)S(1)}, u32[]{:S(2)}, u32[]{:S(2)}) collective-permute-start(f32[16,128]{1,0:T(8,128)S(1)} %pad_maximum_fusion.3), channel_id=1, source_target_pairs={{0,2},{1,3},{2,0},{3,1},{4,6},{5,7},{6,4},{7,5},{8,10},{9,11},{10,... | collective-permute-start | bytes 24584 | tf_op jit(solution)/shard_map/ppermute | solution.py:266
  8.8 2.9 %collective-permute-done.8.refs_4_ = bf16[16,64,256]{2,1,0:T(8,128)(2,1)S(1)} collective-permute-done((bf16[16,64,256]{2,1,0:T(8,128)(2,1)}, bf16[16,64,256]{2,1,0:T(8,128)(2,1)S(1)}, u32[]{:S(2)}, u32[]{:S(2)}) %collective-permute-start.8) | collective-permute-done | bytes 524320 | tf_op jit(solution)/shard_map/ppermute | solution.py:266
  11.7 1.9 %collective-permute-start.5 = (f32[16,256]{1,0:T(8,128)S(1)}, f32[16,256]{1,0:T(8,128)S(1)}, u32[]{:S(2)}, u32[]{:S(2)}) collective-permute-start(f32[16,256]{1,0:T(8,128)S(1)} %pad_maximum_fusion.2), channel_id=1, source_target_pairs={{0,4},{1,5},{2,6},{3,7},{4,0},{5,1},{6,2},{7,3},{8,12},{9,13},{10,... | collective-permute-start | bytes 49160 | tf_op jit(solution)/shard_map/ppermute | solution.py:266
  13.6 8.3 %template_flip.1 = (bf16[32,16,16,512]{3,2,1,0:T(8,128)(2,1)}, f32[16,128]{1,0:T(8,128)}) custom-call(bf16[256,256]{1,0:T(8,128)(2,1)} %constant.84.clone.turn_ref, bf16[2,16,256,512]{3,2,1,0:T(8,128)(2,1)} %g_ref), custom_call_target="tpu_custom_call" | custom-call | flops 2200000000 | bytes 16777216 | tf_op jit(solution)/shard_map/template_flip/pallas_call | solution.py:64
  23.0 2.5 %collective-permute-start.7 = (f32[16,512]{1,0:T(8,128)S(1)}, f32[16,512]{1,0:T(8,128)S(1)}, u32[]{:S(2)}, u32[]{:S(2)}) collective-permute-start(f32[16,512]{1,0:T(8,128)S(1)} %pad_maximum_fusion.1), channel_id=1, source_target_pairs={{0,12},{1,13},{2,14},{3,15},{4,8},{5,9},{6,10},{7,11},{8,4},{9,5},... | collective-permute-start | bytes 98312 | tf_op jit(solution)/shard_map/ppermute | solution.py:266
  25.6 1.5 %collective-permute-start.13 = (bf16[16,64,256]{2,1,0:T(8,128)(2,1)S(1)}, bf16[16,64,256]{2,1,0:T(8,128)(2,1)}, u32[]{:S(2)}, u32[]{:S(2)}) collective-permute-start(bf16[16,64,256]{2,1,0:T(8,128)(2,1)S(1)} %collective-permute-done.11.refs_8_), channel_id=1, source_target_pairs={{0,2},{1,3},{2,0},{3,1},{4,6},{5,7},{6,4},{7,5},{8,10},{9,11},{10,... | collective-permute-start | bytes 1572872 | tf_op jit(solution)/shard_map/ppermute | solution.py:266
  27.2 0.9 %collective-permute-done.7 = f32[16,512]{1,0:T(8,128)S(1)} collective-permute-done((f32[16,512]{1,0:T(8,128)S(1)}, f32[16,512]{1,0:T(8,128)S(1)}, u32[]{:S(2)}, u32[]{:S(2)}) %collective-permute-start.7) | collective-permute-done | bytes 32800 | tf_op jit(solution)/shard_map/ppermute | solution.py:266
  28.2 0.7 collective-permute-start.10
  29.7 1.6 %collective-permute-start.19 = (f32[16,1152]{1,0:T(8,128)S(1)}, f32[16,1152]{1,0:T(8,128)S(1)}, u32[]{:S(2)}, u32[]{:S(2)}) collective-permute-start(f32[16,1152]{1,0:T(8,128)S(1)} %constant_dynamic-update-slice_fusion), channel_id=1, source_target_pairs={{0,16},{16,0},{32,48},{48,32},{64,80},{80,64},{96,112},{112,96},{1... | collective-permute-start | bytes 221192 | tf_op jit(solution)/shard_map/ppermute | solution.py:266
  31.2 3.4 %collective-permute-done.19 = f32[16,1152]{1,0:T(8,128)S(1)} collective-permute-done((f32[16,1152]{1,0:T(8,128)S(1)}, f32[16,1152]{1,0:T(8,128)S(1)}, u32[]{:S(2)}, u32[]{:S(2)}) %collective-permute-start.19) | collective-permute-done | bytes 73760 | tf_op jit(solution)/shard_map/ppermute | solution.py:266
  34.7 3.1 %collective-permute-start.20 = (f32[16,1152]{1,0:T(8,128)S(1)}, f32[16,1152]{1,0:T(8,128)S(1)}, u32[]{:S(2)}, u32[]{:S(2)}) collective-permute-start(f32[16,1152]{1,0:T(8,128)S(1)} %add.40), channel_id=1, source_target_pairs={{0,48},{16,32},{32,16},{48,0},{64,112},{80,96},{96,80},{112,64},{1... | collective-permute-start | bytes 221192 | tf_op jit(solution)/shard_map/ppermute | solution.py:266
  37.8 2.5 %collective-permute-done.20 = f32[16,1152]{1,0:T(8,128)S(1)} collective-permute-done((f32[16,1152]{1,0:T(8,128)S(1)}, f32[16,1152]{1,0:T(8,128)S(1)}, u32[]{:S(2)}, u32[]{:S(2)}) %collective-permute-start.20) | collective-permute-done | bytes 73760 | tf_op jit(solution)/shard_map/ppermute | solution.py:266
  40.4 3.1 %collective-permute-start.21 = (f32[16,1152]{1,0:T(8,128)S(1)}, f32[16,1152]{1,0:T(8,128)S(1)}, u32[]{:S(2)}, u32[]{:S(2)}) collective-permute-start(f32[16,1152]{1,0:T(8,128)S(1)} %add.41), channel_id=1, source_target_pairs={{0,64},{16,80},{32,96},{48,112},{64,0},{80,16},{96,32},{112,48},{1... | collective-permute-start | bytes 221192 | tf_op jit(solution)/shard_map/ppermute | solution.py:266
  44.0 2.3 %collective-permute-done.21 = f32[16,1152]{1,0:T(8,128)S(1)} collective-permute-done((f32[16,1152]{1,0:T(8,128)S(1)}, f32[16,1152]{1,0:T(8,128)S(1)}, u32[]{:S(2)}, u32[]{:S(2)}) %collective-permute-start.21) | collective-permute-done | bytes 73760 | tf_op jit(solution)/shard_map/ppermute | solution.py:266
  47.6 0.9 %collective-permute-done.14.refs_11_ = bf16[16,64,256]{2,1,0:T(8,128)(2,1)S(1)} collective-permute-done((bf16[16,64,256]{2,1,0:T(8,128)(2,1)}, bf16[16,64,256]{2,1,0:T(8,128)(2,1)S(1)}, u32[]{:S(2)}, u32[]{:S(2)}) %collective-permute-start.14) | collective-permute-done | bytes 524320 | tf_op jit(solution)/shard_map/ppermute | solution.py:266
  48.4 0.7 collective-permute-done.18.refs_15_
  49.2 0.7 collective-permute-done.17.refs_14_
  49.9 1.2 %copy-done.3 = bf16[2,512,512]{2,1,0:T(8,128)(2,1)S(1)} copy-done((bf16[2,512,512]{2,1,0:T(8,128)(2,1)S(1)}, bf16[2,512,512]{2,1,0:T(8,128)(2,1)}, u32[]{:S(2)}) %copy-start.3) | copy-done | bytes 1048600
  51.1 16.1 %detect.1 = f32[8,16,128]{2,1,0:T(8,128)S(1)} custom-call(bf16[16,64,256]{2,1,0:T(8,128)(2,1)S(1)} %bitcast.4, bf16[16,64,256]{2,1,0:T(8,128)(2,1)S(1)} %collective-permute-done.refs_1_, bf16[16,64,256]{2,1,0:T(8,128)(2,1)S(1)} %collective-permute-done.1.refs_2_, bf16[16,64,256]{2,1,0:T(8,128)(2,1)} %collective-permute-done.6.refs_3_, ...), custom_call_target="tpu_custom_call" | custom-call | flops 12000000000 | bytes 25165824 | tf_op jit(solution)/shard_map/detect/pallas_call | solution.py:241
  67.2 14.4 %all_to_all.5 = f32[8,16,128]{2,1,0:T(8,128)S(1)} all-to-all(f32[8,16,128]{2,1,0:T(8,128)S(1)} %detect.1), channel_id=1, replica_groups=mesh['chan'=8,'tmpl'=16] {'chan'}, dimensions={0} | all-to-all | bytes 131072 | tf_op jit(solution)/shard_map/all_to_all | solution.py:350
  (53 shorter events, 5.1 us)
Async XLA Ops:
  0.0 49.9 %copy-start = (bf16[16,256,64]{1,2,0:T(8,128)(2,1)S(1)}, bf16[16,256,64]{1,2,0:T(8,128)(2,1)}, u32[]{:S(2)}) copy-start(bf16[16,256,64]{1,2,0:T(8,128)(2,1)} %param.8) | copy-start | bytes 1572868
  0.0 49.9 %copy-start.2 = (s32[16]{0:T(128)S(1)}, s32[16]{0:T(128)}, u32[]{:S(2)}) copy-start(s32[16]{0:T(128)} %refs_16_.1) | copy-start | bytes 196
  0.0 6.7 %collective-permute-start = (bf16[16,64,256]{2,1,0:T(8,128)(2,1)}, bf16[16,64,256]{2,1,0:T(8,128)(2,1)S(1)}, u32[]{:S(2)}, u32[]{:S(2)}) collective-permute-start(bf16[16,64,256]{2,1,0:T(8,128)(2,1)} %bitcast.1), channel_id=1, source_target_pairs={{0,1},{1,0},{2,3},{3,2},{4,5},{5,4},{6,7},{7,6},{8,9},{9,8},{10,11... | collective-permute-start | bytes 1572872 | tf_op jit(solution)/shard_map/ppermute | solution.py:266
  0.1 11.6 %collective-permute-start.8 = (bf16[16,64,256]{2,1,0:T(8,128)(2,1)}, bf16[16,64,256]{2,1,0:T(8,128)(2,1)S(1)}, u32[]{:S(2)}, u32[]{:S(2)}) collective-permute-start(bf16[16,64,256]{2,1,0:T(8,128)(2,1)} %bitcast.2), channel_id=1, source_target_pairs={{0,4},{1,13},{2,6},{3,15},{4,8},{5,1},{6,10},{7,3},{8,12},{9,5},{1... | collective-permute-start | bytes 1572872 | tf_op jit(solution)/shard_map/ppermute | solution.py:266
  3.5 3.2 %collective-permute-start.3 = (f32[16,64]{1,0:T(8,128)S(1)}, f32[16,64]{1,0:T(8,128)S(1)}, u32[]{:S(2)}, u32[]{:S(2)}) collective-permute-start(f32[16,64]{1,0:T(8,128)S(1)} %multiply_reduce_fusion), channel_id=1, source_target_pairs={{0,1},{1,0},{2,3},{3,2},{4,5},{5,4},{6,7},{7,6},{8,9},{9,8},{10,11... | collective-permute-start | bytes 12296 | tf_op jit(solution)/shard_map/ppermute | solution.py:266
  6.7 5.0 %collective-permute-start.4 = (f32[16,128]{1,0:T(8,128)S(1)}, f32[16,128]{1,0:T(8,128)S(1)}, u32[]{:S(2)}, u32[]{:S(2)}) collective-permute-start(f32[16,128]{1,0:T(8,128)S(1)} %pad_maximum_fusion.3), channel_id=1, source_target_pairs={{0,2},{1,3},{2,0},{3,1},{4,6},{5,7},{6,4},{7,5},{8,10},{9,11},{10,... | collective-permute-start | bytes 24584 | tf_op jit(solution)/shard_map/ppermute | solution.py:266
  8.2 14.1 %collective-permute-start.1 = (bf16[16,64,256]{2,1,0:T(8,128)(2,1)}, bf16[16,64,256]{2,1,0:T(8,128)(2,1)S(1)}, u32[]{:S(2)}, u32[]{:S(2)}) collective-permute-start(bf16[16,64,256]{2,1,0:T(8,128)(2,1)} %bitcast.3), channel_id=1, source_target_pairs={{0,2},{1,3},{2,0},{3,1},{4,6},{5,7},{6,4},{7,5},{8,10},{9,11},{10,... | collective-permute-start | bytes 1572872 | tf_op jit(solution)/shard_map/ppermute | solution.py:266
  8.8 13.6 %collective-permute-start.2 = (bf16[16,64,256]{2,1,0:T(8,128)(2,1)S(1)}, bf16[16,64,256]{2,1,0:T(8,128)(2,1)S(1)}, u32[]{:S(2)}, u32[]{:S(2)}) collective-permute-start(bf16[16,64,256]{2,1,0:T(8,128)(2,1)S(1)} %collective-permute-done.refs_1_), channel_id=1, source_target_pairs={{0,4},{1,13},{2,6},{3,15},{4,8},{5,1},{6,10},{7,3},{8,12},{9,5},{1... | collective-permute-start | bytes 1572872 | tf_op jit(solution)/shard_map/ppermute | solution.py:266
  11.7 14.0 %collective-permute-start.11 = (bf16[16,64,256]{2,1,0:T(8,128)(2,1)S(1)}, bf16[16,64,256]{2,1,0:T(8,128)(2,1)S(1)}, u32[]{:S(2)}, u32[]{:S(2)}) collective-permute-start(bf16[16,64,256]{2,1,0:T(8,128)(2,1)S(1)} %collective-permute-done.8.refs_4_), channel_id=1, source_target_pairs={{0,4},{1,13},{2,6},{3,15},{4,8},{5,1},{6,10},{7,3},{8,12},{9,5},{1... | collective-permute-start | bytes 1572872 | tf_op jit(solution)/shard_map/ppermute | solution.py:266
  11.7 10.2 %collective-permute-start.5 = (f32[16,256]{1,0:T(8,128)S(1)}, f32[16,256]{1,0:T(8,128)S(1)}, u32[]{:S(2)}, u32[]{:S(2)}) collective-permute-start(f32[16,256]{1,0:T(8,128)S(1)} %pad_maximum_fusion.2), channel_id=1, source_target_pairs={{0,4},{1,5},{2,6},{3,7},{4,0},{5,1},{6,2},{7,3},{8,12},{9,13},{10,... | collective-permute-start | bytes 49160 | tf_op jit(solution)/shard_map/ppermute | solution.py:266
  22.4 5.8 %collective-permute-start.6 = (bf16[16,64,256]{2,1,0:T(8,128)(2,1)S(1)}, bf16[16,64,256]{2,1,0:T(8,128)(2,1)}, u32[]{:S(2)}, u32[]{:S(2)}) collective-permute-start(bf16[16,64,256]{2,1,0:T(8,128)(2,1)S(1)} %collective-permute-done.1.refs_2_), channel_id=1, source_target_pairs={{0,1},{1,0},{2,3},{3,2},{4,5},{5,4},{6,7},{7,6},{8,9},{9,8},{10,11... | collective-permute-start | bytes 1572872 | tf_op jit(solution)/shard_map/ppermute | solution.py:266
  23.0 5.1 %collective-permute-start.7 = (f32[16,512]{1,0:T(8,128)S(1)}, f32[16,512]{1,0:T(8,128)S(1)}, u32[]{:S(2)}, u32[]{:S(2)}) collective-permute-start(f32[16,512]{1,0:T(8,128)S(1)} %pad_maximum_fusion.1), channel_id=1, source_target_pairs={{0,12},{1,13},{2,14},{3,15},{4,8},{5,9},{6,10},{7,11},{8,4},{9,5},... | collective-permute-start | bytes 98312 | tf_op jit(solution)/shard_map/ppermute | solution.py:266
  25.5 18.0 %collective-permute-start.16 = (bf16[16,64,256]{2,1,0:T(8,128)(2,1)S(1)}, bf16[16,64,256]{2,1,0:T(8,128)(2,1)}, u32[]{:S(2)}, u32[]{:S(2)}) collective-permute-start(bf16[16,64,256]{2,1,0:T(8,128)(2,1)S(1)} %collective-permute-done.8.refs_4_), channel_id=1, source_target_pairs={{0,1},{1,0},{2,3},{3,2},{4,5},{5,4},{6,7},{7,6},{8,9},{9,8},{10,11... | collective-permute-start | bytes 1572872 | tf_op jit(solution)/shard_map/ppermute | solution.py:266
  25.6 17.8 %collective-permute-start.13 = (bf16[16,64,256]{2,1,0:T(8,128)(2,1)S(1)}, bf16[16,64,256]{2,1,0:T(8,128)(2,1)}, u32[]{:S(2)}, u32[]{:S(2)}) collective-permute-start(bf16[16,64,256]{2,1,0:T(8,128)(2,1)S(1)} %collective-permute-done.11.refs_8_), channel_id=1, source_target_pairs={{0,2},{1,3},{2,0},{3,1},{4,6},{5,7},{6,4},{7,5},{8,10},{9,11},{10,... | collective-permute-start | bytes 1572872 | tf_op jit(solution)/shard_map/ppermute | solution.py:266
  28.1 18.2 %collective-permute-start.9 = (bf16[16,64,256]{2,1,0:T(8,128)(2,1)S(1)}, bf16[16,64,256]{2,1,0:T(8,128)(2,1)}, u32[]{:S(2)}, u32[]{:S(2)}) collective-permute-start(bf16[16,64,256]{2,1,0:T(8,128)(2,1)S(1)} %collective-permute-done.1.refs_2_), channel_id=1, source_target_pairs={{0,4},{1,13},{2,6},{3,15},{4,8},{5,1},{6,10},{7,3},{8,12},{9,5},{1... | collective-permute-start | bytes 1572872 | tf_op jit(solution)/shard_map/ppermute | solution.py:266
  28.2 18.6 %collective-permute-start.10 = (bf16[16,64,256]{2,1,0:T(8,128)(2,1)}, bf16[16,64,256]{2,1,0:T(8,128)(2,1)}, u32[]{:S(2)}, u32[]{:S(2)}) collective-permute-start(bf16[16,64,256]{2,1,0:T(8,128)(2,1)} %collective-permute-done.6.refs_3_), channel_id=1, source_target_pairs={{0,4},{1,13},{2,6},{3,15},{4,8},{5,1},{6,10},{7,3},{8,12},{9,5},{1... | collective-permute-start | bytes 1572872 | tf_op jit(solution)/shard_map/ppermute | solution.py:266
  29.7 5.0 %collective-permute-start.19 = (f32[16,1152]{1,0:T(8,128)S(1)}, f32[16,1152]{1,0:T(8,128)S(1)}, u32[]{:S(2)}, u32[]{:S(2)}) collective-permute-start(f32[16,1152]{1,0:T(8,128)S(1)} %constant_dynamic-update-slice_fusion), channel_id=1, source_target_pairs={{0,16},{16,0},{32,48},{48,32},{64,80},{80,64},{96,112},{112,96},{1... | collective-permute-start | bytes 221192 | tf_op jit(solution)/shard_map/ppermute | solution.py:266
  34.7 5.6 %collective-permute-start.20 = (f32[16,1152]{1,0:T(8,128)S(1)}, f32[16,1152]{1,0:T(8,128)S(1)}, u32[]{:S(2)}, u32[]{:S(2)}) collective-permute-start(f32[16,1152]{1,0:T(8,128)S(1)} %add.40), channel_id=1, source_target_pairs={{0,48},{16,32},{32,16},{48,0},{64,112},{80,96},{96,80},{112,64},{1... | collective-permute-start | bytes 221192 | tf_op jit(solution)/shard_map/ppermute | solution.py:266
  40.4 5.9 %collective-permute-start.21 = (f32[16,1152]{1,0:T(8,128)S(1)}, f32[16,1152]{1,0:T(8,128)S(1)}, u32[]{:S(2)}, u32[]{:S(2)}) collective-permute-start(f32[16,1152]{1,0:T(8,128)S(1)} %add.41), channel_id=1, source_target_pairs={{0,64},{16,80},{32,96},{48,112},{64,0},{80,16},{96,32},{112,48},{1... | collective-permute-start | bytes 221192 | tf_op jit(solution)/shard_map/ppermute | solution.py:266
  43.5 4.1 %collective-permute-start.15 = (bf16[16,64,256]{2,1,0:T(8,128)(2,1)S(1)}, bf16[16,64,256]{2,1,0:T(8,128)(2,1)S(1)}, u32[]{:S(2)}, u32[]{:S(2)}) collective-permute-start(bf16[16,64,256]{2,1,0:T(8,128)(2,1)S(1)} %collective-permute-done.2.refs_5_), channel_id=1, source_target_pairs={{0,1},{1,0},{2,3},{3,2},{4,5},{5,4},{6,7},{7,6},{8,9},{9,8},{10,11... | collective-permute-start | bytes 1572872 | tf_op jit(solution)/shard_map/ppermute | solution.py:266
  43.5 4.1 %collective-permute-start.12 = (bf16[16,64,256]{2,1,0:T(8,128)(2,1)S(1)}, bf16[16,64,256]{2,1,0:T(8,128)(2,1)S(1)}, u32[]{:S(2)}, u32[]{:S(2)}) collective-permute-start(bf16[16,64,256]{2,1,0:T(8,128)(2,1)S(1)} %collective-permute-done.11.refs_8_), channel_id=1, source_target_pairs={{0,1},{1,0},{2,3},{3,2},{4,5},{5,4},{6,7},{7,6},{8,9},{9,8},{10,11... | collective-permute-start | bytes 1572872 | tf_op jit(solution)/shard_map/ppermute | solution.py:266
  46.3 2.1 %collective-permute-start.14 = (bf16[16,64,256]{2,1,0:T(8,128)(2,1)}, bf16[16,64,256]{2,1,0:T(8,128)(2,1)S(1)}, u32[]{:S(2)}, u32[]{:S(2)}) collective-permute-start(bf16[16,64,256]{2,1,0:T(8,128)(2,1)} %collective-permute-done.13.refs_10_), channel_id=1, source_target_pairs={{0,1},{1,0},{2,3},{3,2},{4,5},{5,4},{6,7},{7,6},{8,9},{9,8},{10,11... | collective-permute-start | bytes 1572872 | tf_op jit(solution)/shard_map/ppermute | solution.py:266
  46.3 2.9 %collective-permute-start.18 = (bf16[16,64,256]{2,1,0:T(8,128)(2,1)}, bf16[16,64,256]{2,1,0:T(8,128)(2,1)S(1)}, u32[]{:S(2)}, u32[]{:S(2)}) collective-permute-start(bf16[16,64,256]{2,1,0:T(8,128)(2,1)} %collective-permute-done.9.refs_6_), channel_id=1, source_target_pairs={{0,1},{1,0},{2,3},{3,2},{4,5},{5,4},{6,7},{7,6},{8,9},{9,8},{10,11... | collective-permute-start | bytes 1572872 | tf_op jit(solution)/shard_map/ppermute | solution.py:266
  46.8 3.1 %collective-permute-start.17 = (bf16[16,64,256]{2,1,0:T(8,128)(2,1)}, bf16[16,64,256]{2,1,0:T(8,128)(2,1)S(1)}, u32[]{:S(2)}, u32[]{:S(2)}) collective-permute-start(bf16[16,64,256]{2,1,0:T(8,128)(2,1)} %collective-permute-done.10.refs_7_), channel_id=1, source_target_pairs={{0,1},{1,0},{2,3},{3,2},{4,5},{5,4},{6,7},{7,6},{8,9},{9,8},{10,11... | collective-permute-start | bytes 1572872 | tf_op jit(solution)/shard_map/ppermute | solution.py:266
  (3 other events, 95.6 us)

commit v6 on v5

--- a/solution.py
+++ b/solution.py
@@ -184,10 +184,10 @@
         == lax.broadcasted_iota(jnp.int32, (rows, lanes), 1) % BLOCK
     )
 
-    @pl.loop(0, bins // BLOCK // 16)
+    @pl.loop(0, bins // BLOCK // 32)
     def _(i):
-        for u in range(16):
-            b = i * 16 + u
+        for u in range(32):
+            b = i * 32 + u
             start = pl.multiple_of(b * BLOCK, BLOCK)
             left = spectra[:, :, pl.ds(start, BLOCK), :].reshape(rows, 2 * channels)
             right = tmpl[b].reshape(lanes, 2 * channels)

time: 83.1 us -> 81.6 us (0.982)
  Pallas kernels: 24.4 us -> 22.9 us
    pallas_call x1, Pallas kernels: 16.1 us -> 14.6 us  [detect(): pl.pallas_call(kernel, in_specs=[vmem] * len(pieces) + [smem] * 4 + [vmem...]
where the time goes in v6:
time: 81.6 us; the launch traced here: 80.8 us
  starting transfers between devices  23.1 us (28%)
  Pallas kernels  22.9 us (28%)
  waiting for transfers between devices  15.8 us (19%)
  blocking collectives  14.4 us (18%)
  other arithmetic  2.35 us (3%)
  local copies, waits for them, and re-layouts  2.06 us (3%)
    ppermute x22, starting transfers between devices, send(): lax.ppermute(value, axis, [(i, move(i)) for i in range(lax.axis_size(axis...  23.1 us
    ppermute x22, waiting for transfers between devices, send(): lax.ppermute(value, axis, [(i, move(i)) for i in range(lax.axis_size(axis...  15.8 us
    pallas_call x1, Pallas kernels, detect(): pl.pallas_call(kernel, in_specs=[vmem] * len(pieces) + [smem] * 4 + [vmem...  14.6 us
    all_to_all x1, blocking collectives, body(): return jnp.sum(lax.all_to_all(partial, 'chan', 0, 0, tiled=False), axis=0)  14.4 us
    pallas_call x1, Pallas kernels, prepare_templates(): pl.pallas_call(template_kernel, grid=(templates // step,), in_specs=[pl.B...  8.3 us
  transfers between devices with their start and end apart: 22, of which 10 were waited for; matrix products, arithmetic and copies ran while one was open for 3% of the time, Pallas kernels for 10%

profile of v6, /device:TPU:0, one launch (start us, length us, event | category | flops | bytes accessed | tf_op | source)
XLA Modules:
  0.0 80.8 jit_solution(12472249080579302313)
XLA Ops:
  0.1 2.1 %collective-permute-start.8 = (bf16[16,64,256]{2,1,0:T(8,128)(2,1)}, bf16[16,64,256]{2,1,0:T(8,128)(2,1)S(1)}, u32[]{:S(2)}, u32[]{:S(2)}) collective-permute-start(bf16[16,64,256]{2,1,0:T(8,128)(2,1)} %bitcast.2), channel_id=1, source_target_pairs={{0,4},{1,13},{2,6},{3,15},{4,8},{5,1},{6,10},{7,3},{8,12},{9,5},{1... | collective-permute-start | bytes 1572872 | tf_op jit(solution)/shard_map/ppermute | solution.py:266
  2.2 1.3 %multiply_reduce_fusion = f32[16,64]{1,0:T(8,128)S(1)} fusion(bf16[16,256,64]{1,2,0:T(8,128)(2,1)} %param.8), kind=kLoop, calls=%fused_computation | loop fusion | flops 785408 | bytes 528384 | tf_op jit(solution)/shard_map/reduce_sum | solution.py:296
  3.5 2.3 %collective-permute-start.3 = (f32[16,64]{1,0:T(8,128)S(1)}, f32[16,64]{1,0:T(8,128)S(1)}, u32[]{:S(2)}, u32[]{:S(2)}) collective-permute-start(f32[16,64]{1,0:T(8,128)S(1)} %multiply_reduce_fusion), channel_id=1, source_target_pairs={{0,1},{1,0},{2,3},{3,2},{4,5},{5,4},{6,7},{7,6},{8,9},{9,8},{10,11... | collective-permute-start | bytes 12296 | tf_op jit(solution)/shard_map/ppermute | solution.py:266
  5.8 0.8 %collective-permute-done.3 = f32[16,64]{1,0:T(8,128)S(1)} collective-permute-done((f32[16,64]{1,0:T(8,128)S(1)}, f32[16,64]{1,0:T(8,128)S(1)}, u32[]{:S(2)}, u32[]{:S(2)}) %collective-permute-start.3) | collective-permute-done | bytes 4128 | tf_op jit(solution)/shard_map/ppermute | solution.py:266
  6.7 1.5 %collective-permute-start.4 = (f32[16,128]{1,0:T(8,128)S(1)}, f32[16,128]{1,0:T(8,128)S(1)}, u32[]{:S(2)}, u32[]{:S(2)}) collective-permute-start(f32[16,128]{1,0:T(8,128)S(1)} %pad_maximum_fusion.3), channel_id=1, source_target_pairs={{0,2},{1,3},{2,0},{3,1},{4,6},{5,7},{6,4},{7,5},{8,10},{9,11},{10,... | collective-permute-start | bytes 24584 | tf_op jit(solution)/shard_map/ppermute | solution.py:266
  8.8 2.9 %collective-permute-done.8.refs_4_ = bf16[16,64,256]{2,1,0:T(8,128)(2,1)S(1)} collective-permute-done((bf16[16,64,256]{2,1,0:T(8,128)(2,1)}, bf16[16,64,256]{2,1,0:T(8,128)(2,1)S(1)}, u32[]{:S(2)}, u32[]{:S(2)}) %collective-permute-start.8) | collective-permute-done | bytes 524320 | tf_op jit(solution)/shard_map/ppermute | solution.py:266
  11.7 1.9 %collective-permute-start.5 = (f32[16,256]{1,0:T(8,128)S(1)}, f32[16,256]{1,0:T(8,128)S(1)}, u32[]{:S(2)}, u32[]{:S(2)}) collective-permute-start(f32[16,256]{1,0:T(8,128)S(1)} %pad_maximum_fusion.2), channel_id=1, source_target_pairs={{0,4},{1,5},{2,6},{3,7},{4,0},{5,1},{6,2},{7,3},{8,12},{9,13},{10,... | collective-permute-start | bytes 49160 | tf_op jit(solution)/shard_map/ppermute | solution.py:266
  13.6 8.3 %template_flip.1 = (bf16[32,16,16,512]{3,2,1,0:T(8,128)(2,1)}, f32[16,128]{1,0:T(8,128)}) custom-call(bf16[256,256]{1,0:T(8,128)(2,1)} %constant.84.clone.turn_ref, bf16[2,16,256,512]{3,2,1,0:T(8,128)(2,1)} %g_ref), custom_call_target="tpu_custom_call" | custom-call | flops 2200000000 | bytes 16777216 | tf_op jit(solution)/shard_map/template_flip/pallas_call | solution.py:64
  23.0 2.5 %collective-permute-start.7 = (f32[16,512]{1,0:T(8,128)S(1)}, f32[16,512]{1,0:T(8,128)S(1)}, u32[]{:S(2)}, u32[]{:S(2)}) collective-permute-start(f32[16,512]{1,0:T(8,128)S(1)} %pad_maximum_fusion.1), channel_id=1, source_target_pairs={{0,12},{1,13},{2,14},{3,15},{4,8},{5,9},{6,10},{7,11},{8,4},{9,5},... | collective-permute-start | bytes 98312 | tf_op jit(solution)/shard_map/ppermute | solution.py:266
  25.6 1.5 %collective-permute-start.13 = (bf16[16,64,256]{2,1,0:T(8,128)(2,1)S(1)}, bf16[16,64,256]{2,1,0:T(8,128)(2,1)}, u32[]{:S(2)}, u32[]{:S(2)}) collective-permute-start(bf16[16,64,256]{2,1,0:T(8,128)(2,1)S(1)} %collective-permute-done.11.refs_8_), channel_id=1, source_target_pairs={{0,2},{1,3},{2,0},{3,1},{4,6},{5,7},{6,4},{7,5},{8,10},{9,11},{10,... | collective-permute-start | bytes 1572872 | tf_op jit(solution)/shard_map/ppermute | solution.py:266
  27.2 0.9 %collective-permute-done.7 = f32[16,512]{1,0:T(8,128)S(1)} collective-permute-done((f32[16,512]{1,0:T(8,128)S(1)}, f32[16,512]{1,0:T(8,128)S(1)}, u32[]{:S(2)}, u32[]{:S(2)}) %collective-permute-start.7) | collective-permute-done | bytes 32800 | tf_op jit(solution)/shard_map/ppermute | solution.py:266
  28.2 0.7 collective-permute-start.10
  29.7 1.6 %collective-permute-start.19 = (f32[16,1152]{1,0:T(8,128)S(1)}, f32[16,1152]{1,0:T(8,128)S(1)}, u32[]{:S(2)}, u32[]{:S(2)}) collective-permute-start(f32[16,1152]{1,0:T(8,128)S(1)} %constant_dynamic-update-slice_fusion), channel_id=1, source_target_pairs={{0,16},{16,0},{32,48},{48,32},{64,80},{80,64},{96,112},{112,96},{1... | collective-permute-start | bytes 221192 | tf_op jit(solution)/shard_map/ppermute | solution.py:266
  31.2 3.4 %collective-permute-done.19 = f32[16,1152]{1,0:T(8,128)S(1)} collective-permute-done((f32[16,1152]{1,0:T(8,128)S(1)}, f32[16,1152]{1,0:T(8,128)S(1)}, u32[]{:S(2)}, u32[]{:S(2)}) %collective-permute-start.19) | collective-permute-done | bytes 73760 | tf_op jit(solution)/shard_map/ppermute | solution.py:266
  34.7 3.1 %collective-permute-start.20 = (f32[16,1152]{1,0:T(8,128)S(1)}, f32[16,1152]{1,0:T(8,128)S(1)}, u32[]{:S(2)}, u32[]{:S(2)}) collective-permute-start(f32[16,1152]{1,0:T(8,128)S(1)} %add.40), channel_id=1, source_target_pairs={{0,48},{16,32},{32,16},{48,0},{64,112},{80,96},{96,80},{112,64},{1... | collective-permute-start | bytes 221192 | tf_op jit(solution)/shard_map/ppermute | solution.py:266
  37.8 2.5 %collective-permute-done.20 = f32[16,1152]{1,0:T(8,128)S(1)} collective-permute-done((f32[16,1152]{1,0:T(8,128)S(1)}, f32[16,1152]{1,0:T(8,128)S(1)}, u32[]{:S(2)}, u32[]{:S(2)}) %collective-permute-start.20) | collective-permute-done | bytes 73760 | tf_op jit(solution)/shard_map/ppermute | solution.py:266
  40.4 3.1 %collective-permute-start.21 = (f32[16,1152]{1,0:T(8,128)S(1)}, f32[16,1152]{1,0:T(8,128)S(1)}, u32[]{:S(2)}, u32[]{:S(2)}) collective-permute-start(f32[16,1152]{1,0:T(8,128)S(1)} %add.41), channel_id=1, source_target_pairs={{0,64},{16,80},{32,96},{48,112},{64,0},{80,16},{96,32},{112,48},{1... | collective-permute-start | bytes 221192 | tf_op jit(solution)/shard_map/ppermute | solution.py:266
  44.0 2.3 %collective-permute-done.21 = f32[16,1152]{1,0:T(8,128)S(1)} collective-permute-done((f32[16,1152]{1,0:T(8,128)S(1)}, f32[16,1152]{1,0:T(8,128)S(1)}, u32[]{:S(2)}, u32[]{:S(2)}) %collective-permute-start.21) | collective-permute-done | bytes 73760 | tf_op jit(solution)/shard_map/ppermute | solution.py:266
  47.6 0.9 %collective-permute-done.14.refs_11_ = bf16[16,64,256]{2,1,0:T(8,128)(2,1)S(1)} collective-permute-done((bf16[16,64,256]{2,1,0:T(8,128)(2,1)}, bf16[16,64,256]{2,1,0:T(8,128)(2,1)S(1)}, u32[]{:S(2)}, u32[]{:S(2)}) %collective-permute-start.14) | collective-permute-done | bytes 524320 | tf_op jit(solution)/shard_map/ppermute | solution.py:266
  48.4 0.7 collective-permute-done.18.refs_15_
  49.2 0.7 collective-permute-done.17.refs_14_
  49.9 1.2 %copy-done.3 = bf16[2,512,512]{2,1,0:T(8,128)(2,1)S(1)} copy-done((bf16[2,512,512]{2,1,0:T(8,128)(2,1)S(1)}, bf16[2,512,512]{2,1,0:T(8,128)(2,1)}, u32[]{:S(2)}) %copy-start.3) | copy-done | bytes 1048600
  51.1 14.6 %detect.1 = f32[8,16,128]{2,1,0:T(8,128)S(1)} custom-call(bf16[16,64,256]{2,1,0:T(8,128)(2,1)S(1)} %bitcast.4, bf16[16,64,256]{2,1,0:T(8,128)(2,1)S(1)} %collective-permute-done.refs_1_, bf16[16,64,256]{2,1,0:T(8,128)(2,1)S(1)} %collective-permute-done.1.refs_2_, bf16[16,64,256]{2,1,0:T(8,128)(2,1)} %collective-permute-done.6.refs_3_, ...), custom_call_target="tpu_custom_call" | custom-call | flops 12000000000 | bytes 25165824 | tf_op jit(solution)/shard_map/detect/pallas_call | solution.py:241
  65.8 14.4 %all_to_all.5 = f32[8,16,128]{2,1,0:T(8,128)S(1)} all-to-all(f32[8,16,128]{2,1,0:T(8,128)S(1)} %detect.1), channel_id=1, replica_groups=mesh['chan'=8,'tmpl'=16] {'chan'}, dimensions={0} | all-to-all | bytes 131072 | tf_op jit(solution)/shard_map/all_to_all | solution.py:350
  (53 shorter events, 5.1 us)
Async XLA Ops:
  0.0 49.9 %copy-start = (bf16[16,256,64]{1,2,0:T(8,128)(2,1)S(1)}, bf16[16,256,64]{1,2,0:T(8,128)(2,1)}, u32[]{:S(2)}) copy-start(bf16[16,256,64]{1,2,0:T(8,128)(2,1)} %param.8) | copy-start | bytes 1572868
  0.0 49.9 %copy-start.2 = (s32[16]{0:T(128)S(1)}, s32[16]{0:T(128)}, u32[]{:S(2)}) copy-start(s32[16]{0:T(128)} %refs_16_.1) | copy-start | bytes 196
  0.0 6.7 %collective-permute-start = (bf16[16,64,256]{2,1,0:T(8,128)(2,1)}, bf16[16,64,256]{2,1,0:T(8,128)(2,1)S(1)}, u32[]{:S(2)}, u32[]{:S(2)}) collective-permute-start(bf16[16,64,256]{2,1,0:T(8,128)(2,1)} %bitcast.1), channel_id=1, source_target_pairs={{0,1},{1,0},{2,3},{3,2},{4,5},{5,4},{6,7},{7,6},{8,9},{9,8},{10,11... | collective-permute-start | bytes 1572872 | tf_op jit(solution)/shard_map/ppermute | solution.py:266
  0.1 11.6 %collective-permute-start.8 = (bf16[16,64,256]{2,1,0:T(8,128)(2,1)}, bf16[16,64,256]{2,1,0:T(8,128)(2,1)S(1)}, u32[]{:S(2)}, u32[]{:S(2)}) collective-permute-start(bf16[16,64,256]{2,1,0:T(8,128)(2,1)} %bitcast.2), channel_id=1, source_target_pairs={{0,4},{1,13},{2,6},{3,15},{4,8},{5,1},{6,10},{7,3},{8,12},{9,5},{1... | collective-permute-start | bytes 1572872 | tf_op jit(solution)/shard_map/ppermute | solution.py:266
  3.5 3.2 %collective-permute-start.3 = (f32[16,64]{1,0:T(8,128)S(1)}, f32[16,64]{1,0:T(8,128)S(1)}, u32[]{:S(2)}, u32[]{:S(2)}) collective-permute-start(f32[16,64]{1,0:T(8,128)S(1)} %multiply_reduce_fusion), channel_id=1, source_target_pairs={{0,1},{1,0},{2,3},{3,2},{4,5},{5,4},{6,7},{7,6},{8,9},{9,8},{10,11... | collective-permute-start | bytes 12296 | tf_op jit(solution)/shard_map/ppermute | solution.py:266
  6.7 5.0 %collective-permute-start.4 = (f32[16,128]{1,0:T(8,128)S(1)}, f32[16,128]{1,0:T(8,128)S(1)}, u32[]{:S(2)}, u32[]{:S(2)}) collective-permute-start(f32[16,128]{1,0:T(8,128)S(1)} %pad_maximum_fusion.3), channel_id=1, source_target_pairs={{0,2},{1,3},{2,0},{3,1},{4,6},{5,7},{6,4},{7,5},{8,10},{9,11},{10,... | collective-permute-start | bytes 24584 | tf_op jit(solution)/shard_map/ppermute | solution.py:266
  8.2 14.1 %collective-permute-start.1 = (bf16[16,64,256]{2,1,0:T(8,128)(2,1)}, bf16[16,64,256]{2,1,0:T(8,128)(2,1)S(1)}, u32[]{:S(2)}, u32[]{:S(2)}) collective-permute-start(bf16[16,64,256]{2,1,0:T(8,128)(2,1)} %bitcast.3), channel_id=1, source_target_pairs={{0,2},{1,3},{2,0},{3,1},{4,6},{5,7},{6,4},{7,5},{8,10},{9,11},{10,... | collective-permute-start | bytes 1572872 | tf_op jit(solution)/shard_map/ppermute | solution.py:266
  8.8 13.6 %collective-permute-start.2 = (bf16[16,64,256]{2,1,0:T(8,128)(2,1)S(1)}, bf16[16,64,256]{2,1,0:T(8,128)(2,1)S(1)}, u32[]{:S(2)}, u32[]{:S(2)}) collective-permute-start(bf16[16,64,256]{2,1,0:T(8,128)(2,1)S(1)} %collective-permute-done.refs_1_), channel_id=1, source_target_pairs={{0,4},{1,13},{2,6},{3,15},{4,8},{5,1},{6,10},{7,3},{8,12},{9,5},{1... | collective-permute-start | bytes 1572872 | tf_op jit(solution)/shard_map/ppermute | solution.py:266
  11.7 14.0 %collective-permute-start.11 = (bf16[16,64,256]{2,1,0:T(8,128)(2,1)S(1)}, bf16[16,64,256]{2,1,0:T(8,128)(2,1)S(1)}, u32[]{:S(2)}, u32[]{:S(2)}) collective-permute-start(bf16[16,64,256]{2,1,0:T(8,128)(2,1)S(1)} %collective-permute-done.8.refs_4_), channel_id=1, source_target_pairs={{0,4},{1,13},{2,6},{3,15},{4,8},{5,1},{6,10},{7,3},{8,12},{9,5},{1... | collective-permute-start | bytes 1572872 | tf_op jit(solution)/shard_map/ppermute | solution.py:266
  11.7 10.2 %collective-permute-start.5 = (f32[16,256]{1,0:T(8,128)S(1)}, f32[16,256]{1,0:T(8,128)S(1)}, u32[]{:S(2)}, u32[]{:S(2)}) collective-permute-start(f32[16,256]{1,0:T(8,128)S(1)} %pad_maximum_fusion.2), channel_id=1, source_target_pairs={{0,4},{1,5},{2,6},{3,7},{4,0},{5,1},{6,2},{7,3},{8,12},{9,13},{10,... | collective-permute-start | bytes 49160 | tf_op jit(solution)/shard_map/ppermute | solution.py:266
  22.4 5.8 %collective-permute-start.6 = (bf16[16,64,256]{2,1,0:T(8,128)(2,1)S(1)}, bf16[16,64,256]{2,1,0:T(8,128)(2,1)}, u32[]{:S(2)}, u32[]{:S(2)}) collective-permute-start(bf16[16,64,256]{2,1,0:T(8,128)(2,1)S(1)} %collective-permute-done.1.refs_2_), channel_id=1, source_target_pairs={{0,1},{1,0},{2,3},{3,2},{4,5},{5,4},{6,7},{7,6},{8,9},{9,8},{10,11... | collective-permute-start | bytes 1572872 | tf_op jit(solution)/shard_map/ppermute | solution.py:266
  23.0 5.1 %collective-permute-start.7 = (f32[16,512]{1,0:T(8,128)S(1)}, f32[16,512]{1,0:T(8,128)S(1)}, u32[]{:S(2)}, u32[]{:S(2)}) collective-permute-start(f32[16,512]{1,0:T(8,128)S(1)} %pad_maximum_fusion.1), channel_id=1, source_target_pairs={{0,12},{1,13},{2,14},{3,15},{4,8},{5,9},{6,10},{7,11},{8,4},{9,5},... | collective-permute-start | bytes 98312 | tf_op jit(solution)/shard_map/ppermute | solution.py:266
  25.5 18.0 %collective-permute-start.16 = (bf16[16,64,256]{2,1,0:T(8,128)(2,1)S(1)}, bf16[16,64,256]{2,1,0:T(8,128)(2,1)}, u32[]{:S(2)}, u32[]{:S(2)}) collective-permute-start(bf16[16,64,256]{2,1,0:T(8,128)(2,1)S(1)} %collective-permute-done.8.refs_4_), channel_id=1, source_target_pairs={{0,1},{1,0},{2,3},{3,2},{4,5},{5,4},{6,7},{7,6},{8,9},{9,8},{10,11... | collective-permute-start | bytes 1572872 | tf_op jit(solution)/shard_map/ppermute | solution.py:266
  25.6 17.8 %collective-permute-start.13 = (bf16[16,64,256]{2,1,0:T(8,128)(2,1)S(1)}, bf16[16,64,256]{2,1,0:T(8,128)(2,1)}, u32[]{:S(2)}, u32[]{:S(2)}) collective-permute-start(bf16[16,64,256]{2,1,0:T(8,128)(2,1)S(1)} %collective-permute-done.11.refs_8_), channel_id=1, source_target_pairs={{0,2},{1,3},{2,0},{3,1},{4,6},{5,7},{6,4},{7,5},{8,10},{9,11},{10,... | collective-permute-start | bytes 1572872 | tf_op jit(solution)/shard_map/ppermute | solution.py:266
  28.1 18.2 %collective-permute-start.9 = (bf16[16,64,256]{2,1,0:T(8,128)(2,1)S(1)}, bf16[16,64,256]{2,1,0:T(8,128)(2,1)}, u32[]{:S(2)}, u32[]{:S(2)}) collective-permute-start(bf16[16,64,256]{2,1,0:T(8,128)(2,1)S(1)} %collective-permute-done.1.refs_2_), channel_id=1, source_target_pairs={{0,4},{1,13},{2,6},{3,15},{4,8},{5,1},{6,10},{7,3},{8,12},{9,5},{1... | collective-permute-start | bytes 1572872 | tf_op jit(solution)/shard_map/ppermute | solution.py:266
  28.2 18.6 %collective-permute-start.10 = (bf16[16,64,256]{2,1,0:T(8,128)(2,1)}, bf16[16,64,256]{2,1,0:T(8,128)(2,1)}, u32[]{:S(2)}, u32[]{:S(2)}) collective-permute-start(bf16[16,64,256]{2,1,0:T(8,128)(2,1)} %collective-permute-done.6.refs_3_), channel_id=1, source_target_pairs={{0,4},{1,13},{2,6},{3,15},{4,8},{5,1},{6,10},{7,3},{8,12},{9,5},{1... | collective-permute-start | bytes 1572872 | tf_op jit(solution)/shard_map/ppermute | solution.py:266
  29.7 5.0 %collective-permute-start.19 = (f32[16,1152]{1,0:T(8,128)S(1)}, f32[16,1152]{1,0:T(8,128)S(1)}, u32[]{:S(2)}, u32[]{:S(2)}) collective-permute-start(f32[16,1152]{1,0:T(8,128)S(1)} %constant_dynamic-update-slice_fusion), channel_id=1, source_target_pairs={{0,16},{16,0},{32,48},{48,32},{64,80},{80,64},{96,112},{112,96},{1... | collective-permute-start | bytes 221192 | tf_op jit(solution)/shard_map/ppermute | solution.py:266
  34.7 5.6 %collective-permute-start.20 = (f32[16,1152]{1,0:T(8,128)S(1)}, f32[16,1152]{1,0:T(8,128)S(1)}, u32[]{:S(2)}, u32[]{:S(2)}) collective-permute-start(f32[16,1152]{1,0:T(8,128)S(1)} %add.40), channel_id=1, source_target_pairs={{0,48},{16,32},{32,16},{48,0},{64,112},{80,96},{96,80},{112,64},{1... | collective-permute-start | bytes 221192 | tf_op jit(solution)/shard_map/ppermute | solution.py:266
  40.4 5.9 %collective-permute-start.21 = (f32[16,1152]{1,0:T(8,128)S(1)}, f32[16,1152]{1,0:T(8,128)S(1)}, u32[]{:S(2)}, u32[]{:S(2)}) collective-permute-start(f32[16,1152]{1,0:T(8,128)S(1)} %add.41), channel_id=1, source_target_pairs={{0,64},{16,80},{32,96},{48,112},{64,0},{80,16},{96,32},{112,48},{1... | collective-permute-start | bytes 221192 | tf_op jit(solution)/shard_map/ppermute | solution.py:266
  43.5 4.1 %collective-permute-start.15 = (bf16[16,64,256]{2,1,0:T(8,128)(2,1)S(1)}, bf16[16,64,256]{2,1,0:T(8,128)(2,1)S(1)}, u32[]{:S(2)}, u32[]{:S(2)}) collective-permute-start(bf16[16,64,256]{2,1,0:T(8,128)(2,1)S(1)} %collective-permute-done.2.refs_5_), channel_id=1, source_target_pairs={{0,1},{1,0},{2,3},{3,2},{4,5},{5,4},{6,7},{7,6},{8,9},{9,8},{10,11... | collective-permute-start | bytes 1572872 | tf_op jit(solution)/shard_map/ppermute | solution.py:266
  43.5 4.1 %collective-permute-start.12 = (bf16[16,64,256]{2,1,0:T(8,128)(2,1)S(1)}, bf16[16,64,256]{2,1,0:T(8,128)(2,1)S(1)}, u32[]{:S(2)}, u32[]{:S(2)}) collective-permute-start(bf16[16,64,256]{2,1,0:T(8,128)(2,1)S(1)} %collective-permute-done.11.refs_8_), channel_id=1, source_target_pairs={{0,1},{1,0},{2,3},{3,2},{4,5},{5,4},{6,7},{7,6},{8,9},{9,8},{10,11... | collective-permute-start | bytes 1572872 | tf_op jit(solution)/shard_map/ppermute | solution.py:266
  46.3 2.1 %collective-permute-start.14 = (bf16[16,64,256]{2,1,0:T(8,128)(2,1)}, bf16[16,64,256]{2,1,0:T(8,128)(2,1)S(1)}, u32[]{:S(2)}, u32[]{:S(2)}) collective-permute-start(bf16[16,64,256]{2,1,0:T(8,128)(2,1)} %collective-permute-done.13.refs_10_), channel_id=1, source_target_pairs={{0,1},{1,0},{2,3},{3,2},{4,5},{5,4},{6,7},{7,6},{8,9},{9,8},{10,11... | collective-permute-start | bytes 1572872 | tf_op jit(solution)/shard_map/ppermute | solution.py:266
  46.3 2.9 %collective-permute-start.18 = (bf16[16,64,256]{2,1,0:T(8,128)(2,1)}, bf16[16,64,256]{2,1,0:T(8,128)(2,1)S(1)}, u32[]{:S(2)}, u32[]{:S(2)}) collective-permute-start(bf16[16,64,256]{2,1,0:T(8,128)(2,1)} %collective-permute-done.9.refs_6_), channel_id=1, source_target_pairs={{0,1},{1,0},{2,3},{3,2},{4,5},{5,4},{6,7},{7,6},{8,9},{9,8},{10,11... | collective-permute-start | bytes 1572872 | tf_op jit(solution)/shard_map/ppermute | solution.py:266
  46.8 3.1 %collective-permute-start.17 = (bf16[16,64,256]{2,1,0:T(8,128)(2,1)}, bf16[16,64,256]{2,1,0:T(8,128)(2,1)S(1)}, u32[]{:S(2)}, u32[]{:S(2)}) collective-permute-start(bf16[16,64,256]{2,1,0:T(8,128)(2,1)} %collective-permute-done.10.refs_7_), channel_id=1, source_target_pairs={{0,1},{1,0},{2,3},{3,2},{4,5},{5,4},{6,7},{7,6},{8,9},{9,8},{10,11... | collective-permute-start | bytes 1572872 | tf_op jit(solution)/shard_map/ppermute | solution.py:266
  (3 other events, 95.6 us)
